TPU v7x, 32 devices: a whole 2x2x4 slice. The times are simulated.
32 devices in a mesh: memory: 4 (over z), group: 8 (over y, x, core).
Axes of the slice: x: 2, y: 2, z: 4, core: 2. Of those that a mesh axis runs over, the one named last changes fastest.
Arguments:
- queries: bfloat16 [8, 32, 32, 128], P('group', 'memory')
- positives: bfloat16 [8, 32, 128, 128], P('group', 'memory'), may hold values from -6 to 6
- memory: bfloat16 [8, 512, 128, 128], P('group', 'memory'), may hold values from -6 to 6
- candidates: int32 [8, 32, 64], P('group', 'memory'), may hold values from 0 to 511, as said below
- counts: int32 [8, 32], P('group', 'memory'), may hold values from 16 to 32
Outputs:
- batch_scores: float32 [8, 32, 64], P('group', 'memory')
- memory_scores: float32 [8, 32, 64], P('group', 'memory')
- loss: float32 [8, 32], P('group', 'memory')
Inputs may be any that keep to these rules, and one draw needn't show every extreme that they name: `candidates`: passage id r of a column lies on memory index r // 128. Among the valid slots of the queries of one device (queries[g, m * 8 to (m + 1) * 8 - 1]), at most 96 name passages of any one memory index, and some memory index is named by exactly 96 of them. Ids may repeat.
All inputs are finite; a program needn't handle non-finite values.
Results may differ from a plain program's by a relative error of at most 0.0003.
Values may be sent and summed in bfloat16 or wider, within the bound.
No kernel may reach another device: no remote copies, remote signals or barrier semaphores. Data moves between devices by JAX's collectives and lax.ppermute only.
A program may use at most 128 MiB of HBM per device.

v0:
```python
import functools

import jax
import jax.numpy as jnp
from jax import lax
from jax.experimental import pallas as pl
from jax.experimental.pallas import tpu as pltpu
from jax.sharding import PartitionSpec as P

LANES = 128
MIB = 1024 * 1024
SLOTS = 8
CHUNK = 32
LIST_ROWS = 16


def in_hbm(array):
    return pltpu.with_memory_space_constraint(array, pltpu.HBM)


def token_max(passages, tokens):
    count, width, depth = passages.shape
    product = lax.dot_general(
        passages.reshape(count * width, depth),
        tokens,
        (((1,), (1,)), ((), ())),
        preferred_element_type=jnp.float32,
    )
    return jnp.max(product.reshape(count, width, tokens.shape[0]), axis=1)


def token_sum(best, queries):
    tokens = best.shape[1]
    per_query = tokens // queries
    row = lax.broadcasted_iota(jnp.int32, (queries, tokens), 0)
    col = lax.broadcasted_iota(jnp.int32, (queries, tokens), 1)
    own = (col // per_query == row).astype(jnp.float32)
    return lax.dot_general(
        own,
        best,
        (((1,), (1,)), ((), ())),
        precision=lax.Precision.HIGHEST,
        preferred_element_type=jnp.float32,
    )


def column_of(row):
    size = row.shape[1]
    square = (size, size)
    diagonal = lax.broadcasted_iota(jnp.int32, square, 0) == lax.broadcasted_iota(
        jnp.int32, square, 1
    )
    return jnp.sum(jnp.where(diagonal, jnp.broadcast_to(row, square), 0), axis=1, keepdims=True)


def row_of(column):
    size = column.shape[0]
    square = (size, size)
    diagonal = lax.broadcasted_iota(jnp.int32, square, 0) == lax.broadcasted_iota(
        jnp.int32, square, 1
    )
    return jnp.sum(jnp.where(diagonal, jnp.broadcast_to(column, square), 0), axis=0, keepdims=True)


def split_ids(p_count, candidate_ref, count_ref):
    ids = candidate_ref[0]
    row = lax.broadcasted_iota(jnp.int32, ids.shape, 0)
    valid_count = jnp.zeros(ids.shape, jnp.int32)
    for index in range(ids.shape[0]):
        valid_count = jnp.where(row == index, count_ref[0, index], valid_count)
    valid = lax.broadcasted_iota(jnp.int32, ids.shape, 1) < valid_count
    holder = jnp.where(valid, ids // p_count, -1)
    return (ids % p_count).astype(jnp.float32), holder.astype(jnp.float32)


def pack_kernel(p_count, query_ref, candidate_ref, count_ref, out_ref):
    _, q_count, slots = candidate_ref.shape
    _, _, q_tokens, depth = query_ref.shape
    tokens = q_count * q_tokens
    out_ref[:tokens] = query_ref[0].reshape(tokens, depth)
    planes = jnp.concatenate(split_ids(p_count, candidate_ref, count_ref), axis=0)
    empty = jnp.zeros((2 * q_count, depth - slots), jnp.float32)
    out_ref[tokens:] = jnp.concatenate([planes, empty], axis=1).astype(out_ref.dtype)


def pack(queries, candidates, counts, p_count):
    _, q_count, q_tokens, depth = queries.shape
    vmem = pl.BlockSpec(memory_space=pltpu.VMEM)
    return pl.pallas_call(
        functools.partial(pack_kernel, p_count),
        in_specs=[vmem, vmem, pl.BlockSpec(memory_space=pltpu.SMEM)],
        out_shape=jax.ShapeDtypeStruct((q_count * (q_tokens + 2), depth), queries.dtype),
        compiler_params=pltpu.CompilerParams(vmem_limit_bytes=4 * MIB),
        name="pack",
    )(in_hbm(queries), in_hbm(candidates), in_hbm(counts))


def memory_kernel(shards, slots, *refs):
    packed_refs, memory_ref = refs[:shards], refs[shards]
    out_refs = refs[shards + 1 : 2 * shards + 1]
    passage_ref, query_ref, rank_ref, best_ref, list_ref, scalar_ref, copy_sems, list_sem = refs[
        2 * shards + 1 :
    ]
    q_count = out_refs[0].shape[0]
    p_count = passage_ref.shape[0]
    total, q_tokens, depth = query_ref.shape
    chunks = p_count // CHUNK

    def fetch(chunk):
        rows = pl.ds(pl.multiple_of(chunk * CHUNK, CHUNK), CHUNK)
        return pltpu.make_async_copy(
            memory_ref.at[0, rows], passage_ref.at[rows], copy_sems.at[chunk]
        )

    for chunk in range(chunks):
        fetch(chunk).start()

    me = lax.axis_index("memory").astype(jnp.float32)
    keys = []
    for index, packed_ref in enumerate(packed_refs):
        tokens = packed_ref[: q_count * q_tokens].reshape(q_count, q_tokens, depth)
        query_ref[index * q_count : (index + 1) * q_count] = tokens
        planes = packed_ref[q_count * q_tokens :].astype(jnp.float32)
        local, holder = planes[:q_count], planes[q_count:]
        keys.append(jnp.where(holder == me, local, -1.0))
    keys = jnp.concatenate(keys, axis=0)
    passage = lax.broadcasted_iota(jnp.int32, (total, p_count), 1).astype(jnp.float32)
    named = jnp.zeros((total, p_count), jnp.float32)
    for slot in range(slots):
        named = jnp.where(keys[:, slot : slot + 1] == passage, 1.0, named)

    square = (total, total)
    earlier = lax.broadcasted_iota(jnp.int32, square, 1) < lax.broadcasted_iota(
        jnp.int32, square, 0
    )
    before = jnp.dot(earlier.astype(jnp.float32), named, preferred_element_type=jnp.float32)
    rank_ref[...] = jnp.where(named > 0.0, before, -1.0)
    counts = jnp.sum(named, axis=0, keepdims=True)
    most = jnp.broadcast_to(jnp.max(counts, axis=1, keepdims=True), counts.shape)

    def left_over(first):
        left = jnp.where(rank_ref[...] == first, 1.0, 0.0)
        left = jnp.sum(left, axis=0, keepdims=True)
        square = (p_count, p_count)
        row = lax.broadcasted_iota(jnp.int32, square, 0).astype(jnp.float32)
        column = lax.broadcasted_iota(jnp.int32, square, 1).astype(jnp.float32)
        place = jnp.dot(left, (row < column).astype(jnp.float32), preferred_element_type=jnp.float32)
        mine = jnp.where((place == row) & (left > 0.0), column, 0.0)
        index = jnp.sum(mine, axis=1, keepdims=True)
        index = jnp.sum(jnp.where(row == column, index, 0.0), axis=0, keepdims=True)
        return [index, jnp.broadcast_to(jnp.sum(left, axis=1, keepdims=True), left.shape)]

    def write_list(first, extra):
        asker = lax.broadcasted_iota(jnp.int32, (total, p_count), 0).astype(jnp.float32)
        rank = rank_ref[...] - first
        rows = [
            jnp.sum(jnp.where(rank == float(slot), asker, 0.0), axis=0, keepdims=True)
            for slot in range(SLOTS)
        ]
        rest = jnp.zeros((LIST_ROWS - SLOTS - len(extra), p_count), jnp.float32)
        list_ref[...] = jnp.concatenate(rows + extra + [rest], axis=0).astype(jnp.int32)
        copy = pltpu.make_async_copy(list_ref, scalar_ref, list_sem)
        copy.start()
        copy.wait()

    def unit(index):
        tokens = [query_ref[scalar_ref[slot, index]] for slot in range(SLOTS)]
        return token_max(passage_ref[pl.ds(index, 1)], jnp.concatenate(tokens, axis=0))

    def add_scores(first):
        sums = token_sum(best_ref[...], SLOTS)
        for index, out_ref in enumerate(out_refs):
            rank = rank_ref[index * q_count : (index + 1) * q_count] - first
            for slot in range(SLOTS):
                out_ref[...] = jnp.where(rank == float(slot), sums[slot : slot + 1], out_ref[...])

    for out_ref in out_refs:
        out_ref[...] = jnp.zeros_like(out_ref)
    write_list(0.0, [most])
    rounds = (scalar_ref[SLOTS, 0] + SLOTS - 1) // SLOTS

    @pl.loop(0, chunks)
    def _(chunk):
        fetch(chunk).wait()
        for start in range(0, CHUNK, 8):
            first = pl.multiple_of(chunk * CHUNK + start, 8)
            rows = [unit(first + offset) for offset in range(8)]
            best_ref[pl.ds(first, 8), :] = jnp.concatenate(rows, axis=0)

    add_scores(0.0)

    @pl.loop(1, rounds)
    def _(turn):
        done = (turn * SLOTS).astype(jnp.float32)
        write_list(done, left_over(done))

        @pl.loop(0, scalar_ref[SLOTS + 1, 0])
        def _(place):
            index = scalar_ref[SLOTS, place]
            best_ref[pl.ds(index, 1), :] = unit(index)

        add_scores(done)


def score_memory(packed, memory, q_count, slots):
    shards = len(packed)
    q_tokens = packed[0].shape[0] // q_count - 2
    _, p_count, p_tokens, depth = memory.shape
    total = shards * q_count
    vmem = pl.BlockSpec(memory_space=pltpu.VMEM)
    return pl.pallas_call(
        functools.partial(memory_kernel, shards, slots),
        in_specs=[vmem] * shards + [pl.BlockSpec(memory_space=pltpu.HBM)],
        out_specs=[vmem] * shards,
        out_shape=[jax.ShapeDtypeStruct((q_count, p_count), jnp.float32)] * shards,
        scratch_shapes=[
            pltpu.VMEM((p_count, p_tokens, depth), memory.dtype),
            pltpu.VMEM((total, q_tokens, depth), memory.dtype),
            pltpu.VMEM((total, p_count), jnp.float32),
            pltpu.VMEM((p_count, SLOTS * q_tokens), jnp.float32),
            pltpu.VMEM((LIST_ROWS, p_count), jnp.int32),
            pltpu.SMEM((LIST_ROWS, p_count), jnp.int32),
            pltpu.SemaphoreType.DMA((p_count // CHUNK,)),
            pltpu.SemaphoreType.DMA,
        ],
        compiler_params=pltpu.CompilerParams(vmem_limit_bytes=16 * MIB),
        cost_estimate=pl.CostEstimate(
            flops=2 * total * q_tokens * p_count * p_tokens * depth,
            bytes_accessed=2 * p_count * p_tokens * depth,
            transcendentals=0,
        ),
        name="score_memory",
    )(*packed, in_hbm(memory))


def batch_kernel(query_ref, *refs):
    passage_refs, (out_ref, best_ref) = refs[:-2], refs[-2:]
    _, queries, q_tokens, depth = query_ref.shape
    count = passage_refs[0].shape[1]
    if len(passage_refs) * count < best_ref.shape[0]:
        best_ref[...] = jnp.zeros_like(best_ref)
    tokens = query_ref[0].reshape(queries * q_tokens, depth)
    for chip, passage_ref in enumerate(passage_refs):
        best_ref[chip * count : (chip + 1) * count, :] = token_max(passage_ref[0], tokens)
    out_ref[...] = token_sum(best_ref[...], queries)


def score_batch(queries, positives):
    _, q_count, q_tokens, depth = queries.shape
    _, p_count, p_tokens, _ = positives[0].shape
    chips = len(positives)
    lanes = -(-chips * p_count // LANES) * LANES
    return pl.pallas_call(
        batch_kernel,
        out_shape=jax.ShapeDtypeStruct((q_count, lanes), jnp.float32),
        scratch_shapes=[pltpu.VMEM((lanes, q_count * q_tokens), jnp.float32)],
        compiler_params=pltpu.CompilerParams(vmem_limit_bytes=16 * MIB),
        cost_estimate=pl.CostEstimate(
            flops=2 * chips * q_count * q_tokens * p_count * p_tokens * depth,
            bytes_accessed=2 * chips * p_count * p_tokens * depth,
            transcendentals=0,
        ),
        name="score_batch",
    )(queries, *positives)


def loss_kernel(shards, own_batch, mate_batch, *refs):
    memory_refs = refs[:shards]
    candidate_ref, count_ref, batch_ref, memory_ref, loss_ref = refs[shards:]
    group, shard = lax.axis_index("group"), lax.axis_index("memory")
    chip, core = group // 2, group % 2
    _, q_count, slots = candidate_ref.shape
    p_count = memory_refs[0].shape[1]
    columns = batch_ref.shape[2]

    parts = []
    for first in range(0, columns, LANES):
        lane = lax.broadcasted_iota(jnp.int32, (q_count, LANES), 1) + first
        owner = lane // q_count
        source = (((owner // 2) ^ chip) * q_count + lane % q_count) % LANES
        own = jnp.take_along_axis(own_batch[...], source, axis=1)
        mate = jnp.take_along_axis(mate_batch[...], source, axis=1)
        parts.append(jnp.where(owner % 2 == core, own, mate))
    batch = jnp.concatenate(parts, axis=1)[:, :columns]
    batch_ref[0] = batch

    ids = candidate_ref[0]
    padded = jnp.concatenate([ids, jnp.zeros((q_count, p_count - slots), jnp.int32)], axis=1)
    holder, local = padded // p_count, padded % p_count
    picked = jnp.zeros((q_count, p_count), jnp.float32)
    for step in range(shards):
        found = jnp.take_along_axis(memory_refs[-step][...], local, axis=1)
        picked = jnp.where(holder == (shard ^ step), found, picked)

    valid = lax.broadcasted_iota(jnp.int32, (q_count, p_count), 1) < column_of(count_ref[...])
    memory_ref[0] = jnp.where(valid, picked, 0.0)[:, :slots]

    top = jnp.maximum(
        jnp.max(batch, axis=1, keepdims=True),
        jnp.max(jnp.where(valid, picked, -jnp.inf), axis=1, keepdims=True),
    )
    total = jnp.sum(jnp.exp(batch - top), axis=1, keepdims=True) + jnp.sum(
        jnp.where(valid, jnp.exp(picked - top), 0.0), axis=1, keepdims=True
    )
    column = lax.broadcasted_iota(jnp.int32, batch.shape, 1)
    own = group * q_count + lax.broadcasted_iota(jnp.int32, batch.shape, 0)
    target_score = jnp.sum(jnp.where(column == own, batch, 0.0), axis=1, keepdims=True)
    loss_ref[...] = row_of(top + jnp.log(total) - target_score)


def finish(own_batch, mate_batch, memory_parts, candidates, counts, columns):
    _, q_count, slots = candidates.shape
    return pl.pallas_call(
        functools.partial(loss_kernel, len(memory_parts)),
        out_shape=[
            jax.ShapeDtypeStruct((1, q_count, columns), jnp.float32),
            jax.ShapeDtypeStruct((1, q_count, slots), jnp.float32),
            jax.ShapeDtypeStruct((1, q_count), jnp.float32),
        ],
        compiler_params=pltpu.CompilerParams(vmem_limit_bytes=4 * MIB),
        name="finish",
    )(own_batch, mate_batch, *memory_parts, candidates, counts)


def body(queries, positives, memory, candidates, counts):
    shards = lax.axis_size("memory")
    groups = lax.axis_size("group")
    chips = groups // 2
    q_count = queries.shape[1]
    slots = candidates.shape[2] // 2

    def to_shard(array, step):
        return lax.ppermute(array, "memory", [(i, i ^ step) for i in range(shards)])

    def to_group(array, step):
        return lax.ppermute(array, "group", [(i, i ^ step) for i in range(groups)])

    own = pack(queries, candidates, counts, memory.shape[1])
    packed = [own] + [to_shard(own, step) for step in range(1, shards)]
    sent_positives, sent_queries, _ = lax.optimization_barrier((positives, queries, own))
    row = [positives] + [to_group(sent_positives, 2 * step) for step in range(1, chips)]
    mate_queries = to_group(sent_queries, 1)

    scores = score_memory(packed, memory, q_count, slots)
    returned = [to_shard(scores[step], step) for step in range(shards - 1, 0, -1)]
    mate_queries, _ = lax.optimization_barrier((mate_queries, scores[0]))
    mate_scores = score_batch(mate_queries, row)
    mate_batch = to_group(mate_scores, 1)
    own_queries, _ = lax.optimization_barrier((queries, mate_scores))
    own_batch = score_batch(own_queries, row)
    columns = groups * q_count
    return finish(
        own_batch, mate_batch, [scores[0]] + returned, candidates, counts, columns
    )


def solution(mesh):
    in_specs = (
        P("group", "memory", None, None),
        P("group", "memory", None, None),
        P("group", "memory", None, None),
        P("group", "memory", None),
        P("group", "memory"),
    )
    out_specs = (P("group", "memory", None), P("group", "memory", None), P("group", "memory"))
    return jax.shard_map(body, mesh=mesh, in_specs=in_specs, out_specs=out_specs, check_vma=False)
```

profile of v0, /device:TPU:0, one launch (start us, length us, event | category | flops | bytes accessed | tf_op | source)
XLA Modules:
  0.0 25.1 jit_solution(6049615595936945372)
XLA Ops:
  0.6 0.9 %pack.1.refs_0_ = bf16[272,128]{1,0:T(8,128)(2,1)S(1)} custom-call(bf16[1,8,32,128]{3,2,1,0:T(8,128)(2,1)} %query_ref.2, s32[1,8,64]{2,1,0:T(8,128)} %refs_4_.3, s32[1,8]{1,0:T(1,128)} %refs_5_.1), custom_call_target="tpu_custom_call" | custom-call | tf_op jit(solution)/shard_map/pack/pallas_call | solution.py:89
  1.5 0.0 copy-start
  1.5 0.0 copy-start.1
  1.5 0.0 copy-start.2
  1.5 0.0 copy-start.3
  1.6 5.1 %collective-permute-start.3 = (bf16[272,128]{1,0:T(8,128)(2,1)S(1)}, bf16[272,128]{1,0:T(8,128)(2,1)S(1)}, u32[]{:S(2)}, u32[]{:S(2)}) collective-permute-start(bf16[272,128]{1,0:T(8,128)(2,1)S(1)} %pack.1.refs_0_), channel_id=1, source_target_pairs={{0,24},{8,16},{16,8},{24,0},{1,25},{9,17},{17,9},{25,1},{2,26},{10... | collective-permute-start | bytes 208904 | tf_op jit(solution)/shard_map/ppermute | solution.py:333
  6.7 0.0 collective-permute-start.2
  6.7 0.6 %collective-permute-start.1 = (bf16[272,128]{1,0:T(8,128)(2,1)S(1)}, bf16[272,128]{1,0:T(8,128)(2,1)S(1)}, u32[]{:S(2)}, u32[]{:S(2)}) collective-permute-start(bf16[272,128]{1,0:T(8,128)(2,1)S(1)} %pack.1.refs_0_), channel_id=1, source_target_pairs={{0,8},{8,0},{16,24},{24,16},{1,9},{9,1},{17,25},{25,17},{2,10},{10... | collective-permute-start | bytes 208904 | tf_op jit(solution)/shard_map/ppermute | solution.py:333
  7.3 2.6 %collective-permute-start.6 = (bf16[1,8,128,128]{3,2,1,0:T(8,128)(2,1)}, bf16[1,8,128,128]{3,2,1,0:T(8,128)(2,1)S(1)}, u32[]{:S(2)}, u32[]{:S(2)}) collective-permute-start(bf16[1,8,128,128]{3,2,1,0:T(8,128)(2,1)} %refs_0_.3), channel_id=1, source_target_pairs={{0,6},{1,7},{2,4},{3,5},{4,2},{5,3},{6,0},{7,1},{8,14},{9,15},{10,... | collective-permute-start | bytes 786440 | tf_op jit(solution)/shard_map/ppermute | solution.py:336
  9.9 0.5 %collective-permute-start.5 = (bf16[1,8,128,128]{3,2,1,0:T(8,128)(2,1)}, bf16[1,8,128,128]{3,2,1,0:T(8,128)(2,1)S(1)}, u32[]{:S(2)}, u32[]{:S(2)}) collective-permute-start(bf16[1,8,128,128]{3,2,1,0:T(8,128)(2,1)} %refs_0_.3), channel_id=1, source_target_pairs={{0,4},{1,5},{2,6},{3,7},{4,0},{5,1},{6,2},{7,3},{8,12},{9,13},{10,... | collective-permute-start | bytes 786440 | tf_op jit(solution)/shard_map/ppermute | solution.py:336
  10.4 0.0 collective-permute-done.3.refs_3_
  10.4 0.8 %collective-permute-start.4 = (bf16[1,8,128,128]{3,2,1,0:T(8,128)(2,1)}, bf16[1,8,128,128]{3,2,1,0:T(8,128)(2,1)S(1)}, u32[]{:S(2)}, u32[]{:S(2)}) collective-permute-start(bf16[1,8,128,128]{3,2,1,0:T(8,128)(2,1)} %refs_0_.3), channel_id=1, source_target_pairs={{0,2},{1,3},{2,0},{3,1},{4,6},{5,7},{6,4},{7,5},{8,10},{9,11},{10,... | collective-permute-start | bytes 786440 | tf_op jit(solution)/shard_map/ppermute | solution.py:336
  11.2 1.4 %collective-permute-done.2.refs_2_ = bf16[272,128]{1,0:T(8,128)(2,1)S(1)} collective-permute-done((bf16[272,128]{1,0:T(8,128)(2,1)S(1)}, bf16[272,128]{1,0:T(8,128)(2,1)S(1)}, u32[]{:S(2)}, u32[]{:S(2)}) %collective-permute-start.2) | collective-permute-done | bytes 69664 | tf_op jit(solution)/shard_map/ppermute | solution.py:333
  12.6 0.0 collective-permute-start
  12.6 0.0 collective-permute-done.1.refs_1_
  12.6 4.4 %score_memory.1 = (f32[8,128]{1,0:T(8,128)S(1)}, f32[8,128]{1,0:T(8,128)S(1)}, f32[8,128]{1,0:T(8,128)S(1)}, f32[8,128]{1,0:T(8,128)S(1)}) custom-call(bf16[272,128]{1,0:T(8,128)(2,1)S(1)} %pack.1.refs_0_, bf16[272,128]{1,0:T(8,128)(2,1)S(1)} %collective-permute-done.1.refs_1_, bf16[272,128]{1,0:T(8,128)(2,1)S(1)} %collective-permute-done.2.refs_2_, ...), custom_call_target="tpu_custom_call" | custom-call | flops 4294967296 | bytes 4194304 | tf_op jit(solution)/shard_map/score_memory/pallas_call | solution.py:211
  17.0 0.0 collective-permute-done.query_ref
  17.0 2.8 %collective-permute-start.8 = (f32[8,128]{1,0:T(8,128)S(1)}, f32[8,128]{1,0:T(8,128)S(1)}, u32[]{:S(2)}, u32[]{:S(2)}) collective-permute-start(f32[8,128]{1,0:T(8,128)S(1)} %get-tuple-element.16), channel_id=1, source_target_pairs={{0,24},{8,16},{16,8},{24,0},{1,25},{9,17},{17,9},{25,1},{2,26},{10... | collective-permute-start | bytes 12296 | tf_op jit(solution)/shard_map/ppermute | solution.py:333
  19.8 0.0 collective-permute-start.9
  19.8 0.0 collective-permute-done.6.refs_3_
  19.8 1.7 %collective-permute-start.10 = (f32[8,128]{1,0:T(8,128)S(1)}, f32[8,128]{1,0:T(8,128)S(1)}, u32[]{:S(2)}, u32[]{:S(2)}) collective-permute-start(f32[8,128]{1,0:T(8,128)S(1)} %get-tuple-element.18), channel_id=1, source_target_pairs={{0,8},{8,0},{16,24},{24,16},{1,9},{9,1},{17,25},{25,17},{2,10},{10... | collective-permute-start | bytes 12296 | tf_op jit(solution)/shard_map/ppermute | solution.py:333
  21.5 0.0 collective-permute-done.5.refs_2_
  21.5 0.1 collective-permute-done.4.refs_1_
  21.6 0.0 copy-done
  21.6 0.8 %score_batch.2 = f32[8,128]{1,0:T(8,128)S(1)} custom-call(bf16[1,8,32,128]{3,2,1,0:T(8,128)(2,1)S(1)} %collective-permute-done.query_ref, bf16[1,8,128,128]{3,2,1,0:T(8,128)(2,1)S(1)} %copy-done, bf16[1,8,128,128]{3,2,1,0:T(8,128)(2,1)S(1)} %collective-permute-done.4.refs_1_, bf16[1,8,128,128]{3,2,1,0:T(8,128)(2,1)S(1)} %collective-permute-done.5.refs_2_, ...), custom_call_target="tpu_custom_call" | custom-call | flops 268435456 | bytes 1048576 | tf_op jit(solution)/shard_map/score_batch/pallas_call | solution.py:253
  22.5 0.0 collective-permute-start.7
  22.5 0.9 %score_batch.3.own_batch = f32[8,128]{1,0:T(8,128)S(1)} custom-call(bf16[1,8,32,128]{3,2,1,0:T(8,128)(2,1)S(1)} %copy-done.1, bf16[1,8,128,128]{3,2,1,0:T(8,128)(2,1)S(1)} %copy-done, bf16[1,8,128,128]{3,2,1,0:T(8,128)(2,1)S(1)} %collective-permute-done.4.refs_1_, bf16[1,8,128,128]{3,2,1,0:T(8,128)(2,1)S(1)} %collective-permute-done.5.refs_2_, ...), custom_call_target="tpu_custom_call" | custom-call | flops 268435456 | bytes 1048576 | tf_op jit(solution)/shard_map/score_batch/pallas_call | solution.py:253
  23.3 0.0 collective-permute-done.8.refs_1_
  23.3 1.0 %collective-permute-done.9.refs_2_ = f32[8,128]{1,0:T(8,128)S(1)} collective-permute-done((f32[8,128]{1,0:T(8,128)S(1)}, f32[8,128]{1,0:T(8,128)S(1)}, u32[]{:S(2)}, u32[]{:S(2)}) %collective-permute-start.9) | collective-permute-done | bytes 4128 | tf_op jit(solution)/shard_map/ppermute | solution.py:333
  24.3 0.0 collective-permute-done.10.refs_3_
  24.3 0.0 collective-permute-done.7.mate_batch
  24.3 0.8 %finish.1 = (f32[1,8,64]{2,1,0:T(8,128)}, f32[1,8,64]{2,1,0:T(8,128)}, f32[1,8]{1,0:T(1,128)}) custom-call(f32[8,128]{1,0:T(8,128)S(1)} %score_batch.3.own_batch, f32[8,128]{1,0:T(8,128)S(1)} %collective-permute-done.7.mate_batch, f32[8,128]{1,0:T(8,128)S(1)} %get-tuple-element.12.refs_0_, f32[8,128]{1,0:T(8,128)S(1)} %collective-permute-done.8.refs_1_, ...), custom_call_target="tpu_custom_call" | custom-call | tf_op jit(solution)/shard_map/finish/pallas_call | solution.py:313
  (3 shorter events, 0.0 us)
Async XLA Ops:
  1.5 20.1 %copy-start = (bf16[1,8,128,128]{3,2,1,0:T(8,128)(2,1)S(1)}, bf16[1,8,128,128]{3,2,1,0:T(8,128)(2,1)}, u32[]{:S(2)}) copy-start(bf16[1,8,128,128]{3,2,1,0:T(8,128)(2,1)} %refs_0_.3) | copy-start | bytes 786436
  1.5 21.0 %copy-start.1 = (bf16[1,8,32,128]{3,2,1,0:T(8,128)(2,1)S(1)}, bf16[1,8,32,128]{3,2,1,0:T(8,128)(2,1)}, u32[]{:S(2)}) copy-start(bf16[1,8,32,128]{3,2,1,0:T(8,128)(2,1)} %query_ref.2) | copy-start | bytes 196612
  1.5 22.8 %copy-start.2 = (s32[1,8,64]{2,1,0:T(8,128)S(1)}, s32[1,8,64]{2,1,0:T(8,128)}, u32[]{:S(2)}) copy-start(s32[1,8,64]{2,1,0:T(8,128)} %refs_4_.3) | copy-start | bytes 6148
  1.5 22.8 %copy-start.3 = (s32[1,8]{1,0:T(1,128)S(1)}, s32[1,8]{1,0:T(1,128)}, u32[]{:S(2)}) copy-start(s32[1,8]{1,0:T(1,128)} %refs_5_.1) | copy-start | bytes 100
  1.6 8.9 %collective-permute-start.3 = (bf16[272,128]{1,0:T(8,128)(2,1)S(1)}, bf16[272,128]{1,0:T(8,128)(2,1)S(1)}, u32[]{:S(2)}, u32[]{:S(2)}) collective-permute-start(bf16[272,128]{1,0:T(8,128)(2,1)S(1)} %pack.1.refs_0_), channel_id=1, source_target_pairs={{0,24},{8,16},{16,8},{24,0},{1,25},{9,17},{17,9},{25,1},{2,26},{10... | collective-permute-start | bytes 208904 | tf_op jit(solution)/shard_map/ppermute | solution.py:333
  6.7 5.9 %collective-permute-start.2 = (bf16[272,128]{1,0:T(8,128)(2,1)S(1)}, bf16[272,128]{1,0:T(8,128)(2,1)S(1)}, u32[]{:S(2)}, u32[]{:S(2)}) collective-permute-start(bf16[272,128]{1,0:T(8,128)(2,1)S(1)} %pack.1.refs_0_), channel_id=1, source_target_pairs={{0,16},{8,24},{16,0},{24,8},{1,17},{9,25},{17,1},{25,9},{2,18},{10... | collective-permute-start | bytes 208904 | tf_op jit(solution)/shard_map/ppermute | solution.py:333
  6.7 5.9 %collective-permute-start.1 = (bf16[272,128]{1,0:T(8,128)(2,1)S(1)}, bf16[272,128]{1,0:T(8,128)(2,1)S(1)}, u32[]{:S(2)}, u32[]{:S(2)}) collective-permute-start(bf16[272,128]{1,0:T(8,128)(2,1)S(1)} %pack.1.refs_0_), channel_id=1, source_target_pairs={{0,8},{8,0},{16,24},{24,16},{1,9},{9,1},{17,25},{25,17},{2,10},{10... | collective-permute-start | bytes 208904 | tf_op jit(solution)/shard_map/ppermute | solution.py:333
  7.3 12.5 %collective-permute-start.6 = (bf16[1,8,128,128]{3,2,1,0:T(8,128)(2,1)}, bf16[1,8,128,128]{3,2,1,0:T(8,128)(2,1)S(1)}, u32[]{:S(2)}, u32[]{:S(2)}) collective-permute-start(bf16[1,8,128,128]{3,2,1,0:T(8,128)(2,1)} %refs_0_.3), channel_id=1, source_target_pairs={{0,6},{1,7},{2,4},{3,5},{4,2},{5,3},{6,0},{7,1},{8,14},{9,15},{10,... | collective-permute-start | bytes 786440 | tf_op jit(solution)/shard_map/ppermute | solution.py:336
  9.9 11.6 %collective-permute-start.5 = (bf16[1,8,128,128]{3,2,1,0:T(8,128)(2,1)}, bf16[1,8,128,128]{3,2,1,0:T(8,128)(2,1)S(1)}, u32[]{:S(2)}, u32[]{:S(2)}) collective-permute-start(bf16[1,8,128,128]{3,2,1,0:T(8,128)(2,1)} %refs_0_.3), channel_id=1, source_target_pairs={{0,4},{1,5},{2,6},{3,7},{4,0},{5,1},{6,2},{7,3},{8,12},{9,13},{10,... | collective-permute-start | bytes 786440 | tf_op jit(solution)/shard_map/ppermute | solution.py:336
  10.4 11.2 %collective-permute-start.4 = (bf16[1,8,128,128]{3,2,1,0:T(8,128)(2,1)}, bf16[1,8,128,128]{3,2,1,0:T(8,128)(2,1)S(1)}, u32[]{:S(2)}, u32[]{:S(2)}) collective-permute-start(bf16[1,8,128,128]{3,2,1,0:T(8,128)(2,1)} %refs_0_.3), channel_id=1, source_target_pairs={{0,2},{1,3},{2,0},{3,1},{4,6},{5,7},{6,4},{7,5},{8,10},{9,11},{10,... | collective-permute-start | bytes 786440 | tf_op jit(solution)/shard_map/ppermute | solution.py:336
  12.6 4.4 %collective-permute-start = (bf16[1,8,32,128]{3,2,1,0:T(8,128)(2,1)}, bf16[1,8,32,128]{3,2,1,0:T(8,128)(2,1)S(1)}, u32[]{:S(2)}, u32[]{:S(2)}) collective-permute-start(bf16[1,8,32,128]{3,2,1,0:T(8,128)(2,1)} %query_ref.2), channel_id=1, source_target_pairs={{0,1},{1,0},{2,3},{3,2},{4,5},{5,4},{6,7},{7,6},{8,9},{9,8},{10,11... | collective-permute-start | bytes 196616 | tf_op jit(solution)/shard_map/ppermute | solution.py:336
  17.0 6.3 %collective-permute-start.8 = (f32[8,128]{1,0:T(8,128)S(1)}, f32[8,128]{1,0:T(8,128)S(1)}, u32[]{:S(2)}, u32[]{:S(2)}) collective-permute-start(f32[8,128]{1,0:T(8,128)S(1)} %get-tuple-element.16), channel_id=1, source_target_pairs={{0,24},{8,16},{16,8},{24,0},{1,25},{9,17},{17,9},{25,1},{2,26},{10... | collective-permute-start | bytes 12296 | tf_op jit(solution)/shard_map/ppermute | solution.py:333
  19.8 4.5 %collective-permute-start.9 = (f32[8,128]{1,0:T(8,128)S(1)}, f32[8,128]{1,0:T(8,128)S(1)}, u32[]{:S(2)}, u32[]{:S(2)}) collective-permute-start(f32[8,128]{1,0:T(8,128)S(1)} %get-tuple-element.17), channel_id=1, source_target_pairs={{0,16},{8,24},{16,0},{24,8},{1,17},{9,25},{17,1},{25,9},{2,18},{10... | collective-permute-start | bytes 12296 | tf_op jit(solution)/shard_map/ppermute | solution.py:333
  19.8 4.5 %collective-permute-start.10 = (f32[8,128]{1,0:T(8,128)S(1)}, f32[8,128]{1,0:T(8,128)S(1)}, u32[]{:S(2)}, u32[]{:S(2)}) collective-permute-start(f32[8,128]{1,0:T(8,128)S(1)} %get-tuple-element.18), channel_id=1, source_target_pairs={{0,8},{8,0},{16,24},{24,16},{1,9},{9,1},{17,25},{25,17},{2,10},{10... | collective-permute-start | bytes 12296 | tf_op jit(solution)/shard_map/ppermute | solution.py:333
  22.5 1.9 %collective-permute-start.7 = (f32[8,128]{1,0:T(8,128)S(1)}, f32[8,128]{1,0:T(8,128)S(1)}, u32[]{:S(2)}, u32[]{:S(2)}) collective-permute-start(f32[8,128]{1,0:T(8,128)S(1)} %score_batch.2), channel_id=1, source_target_pairs={{0,1},{1,0},{2,3},{3,2},{4,5},{5,4},{6,7},{7,6},{8,9},{9,8},{10,11... | collective-permute-start | bytes 12296 | tf_op jit(solution)/shard_map/ppermute | solution.py:336
where the time goes:
time: 25.3 us; the launch traced here: 25.1 us
  starting transfers between devices  14.1 us (56%)
  Pallas kernels  7.79 us (31%)
  waiting for transfers between devices  2.54 us (10%)
  between operations  0.71 us (3%)
    ppermute x6, starting transfers between devices, to_shard(): return lax.ppermute(array, 'memory', [(i, i ^ step) for i in range(shards)])  10.2 us
    pallas_call x1, Pallas kernels, score_memory(): pl.pallas_call(functools.partial(memory_kernel, shards, slots), in_specs=...  4.42 us
    ppermute x5, starting transfers between devices, to_group(): return lax.ppermute(array, 'group', [(i, i ^ step) for i in range(groups)])  3.88 us
    ppermute x6, waiting for transfers between devices, to_shard(): return lax.ppermute(array, 'memory', [(i, i ^ step) for i in range(shards)])  2.39 us
    pallas_call x2, Pallas kernels, score_batch(): pl.pallas_call(batch_kernel, out_shape=jax.ShapeDtypeStruct((q_count, lan...  1.7 us
    pallas_call x1, Pallas kernels, pack(): pl.pallas_call(functools.partial(pack_kernel, p_count), in_specs=[vmem, v...  0.87 us
    pallas_call x1, Pallas kernels, finish(): pl.pallas_call(functools.partial(loss_kernel, len(memory_parts)), out_sha...  0.8 us
  transfers between devices with their start and end apart: 11, of which 3 were waited for; matrix products, arithmetic and copies ran while one was open for 0% of the time, Pallas kernels for 24%

commit v1 on v0

--- a/solution.py
+++ b/solution.py
@@ -9,9 +9,10 @@
 
 LANES = 128
 MIB = 1024 * 1024
-SLOTS = 8
+SLOTS = 4
 CHUNK = 32
-LIST_ROWS = 16
+LIST_ROWS = 8
+STEP = 8
 
 
 def in_hbm(array):
@@ -32,8 +33,8 @@
 def token_sum(best, queries):
     tokens = best.shape[1]
     per_query = tokens // queries
-    row = lax.broadcasted_iota(jnp.int32, (queries, tokens), 0)
-    col = lax.broadcasted_iota(jnp.int32, (queries, tokens), 1)
+    row = lax.broadcasted_iota(jnp.int32, (max(queries, 8), tokens), 0)
+    col = lax.broadcasted_iota(jnp.int32, (max(queries, 8), tokens), 1)
     own = (col // per_query == row).astype(jnp.float32)
     return lax.dot_general(
         own,
@@ -98,9 +99,8 @@
 def memory_kernel(shards, slots, *refs):
     packed_refs, memory_ref = refs[:shards], refs[shards]
     out_refs = refs[shards + 1 : 2 * shards + 1]
-    passage_ref, query_ref, rank_ref, best_ref, list_ref, scalar_ref, copy_sems, list_sem = refs[
-        2 * shards + 1 :
-    ]
+    passage_ref, query_ref, rank_ref, best_ref, left_best_ref, *refs = refs[2 * shards + 1 :]
+    list_ref, scalar_ref, left_ref, left_scalar_ref, copy_sems, list_sems = refs
     q_count = out_refs[0].shape[0]
     p_count = passage_ref.shape[0]
     total, q_tokens, depth = query_ref.shape
@@ -138,68 +138,97 @@
     counts = jnp.sum(named, axis=0, keepdims=True)
     most = jnp.broadcast_to(jnp.max(counts, axis=1, keepdims=True), counts.shape)
 
-    def left_over(first):
+    asker = lax.broadcasted_iota(jnp.int32, (total, p_count), 0).astype(jnp.float32)
+
+    def ids_from(first):
+        rank = rank_ref[...] - first
+        return [
+            jnp.sum(jnp.where(rank == float(slot), asker, 0.0), axis=0, keepdims=True)
+            for slot in range(SLOTS)
+        ]
+
+    list_copy = pltpu.make_async_copy(list_ref, scalar_ref, list_sems.at[0])
+    left_copy = pltpu.make_async_copy(left_ref, left_scalar_ref, list_sems.at[1])
+
+    def write_list():
+        rest = jnp.zeros((LIST_ROWS - SLOTS - 1, p_count), jnp.float32)
+        rows = ids_from(0.0) + [most, rest]
+        list_ref[...] = jnp.concatenate(rows, axis=0).astype(jnp.int32)
+
+    def write_left(first):
         left = jnp.where(rank_ref[...] == first, 1.0, 0.0)
         left = jnp.sum(left, axis=0, keepdims=True)
         square = (p_count, p_count)
         row = lax.broadcasted_iota(jnp.int32, square, 0).astype(jnp.float32)
         column = lax.broadcasted_iota(jnp.int32, square, 1).astype(jnp.float32)
-        place = jnp.dot(left, (row < column).astype(jnp.float32), preferred_element_type=jnp.float32)
-        mine = jnp.where((place == row) & (left > 0.0), column, 0.0)
-        index = jnp.sum(mine, axis=1, keepdims=True)
-        index = jnp.sum(jnp.where(row == column, index, 0.0), axis=0, keepdims=True)
-        return [index, jnp.broadcast_to(jnp.sum(left, axis=1, keepdims=True), left.shape)]
-
-    def write_list(first, extra):
-        asker = lax.broadcasted_iota(jnp.int32, (total, p_count), 0).astype(jnp.float32)
-        rank = rank_ref[...] - first
-        rows = [
-            jnp.sum(jnp.where(rank == float(slot), asker, 0.0), axis=0, keepdims=True)
-            for slot in range(SLOTS)
-        ]
-        rest = jnp.zeros((LIST_ROWS - SLOTS - len(extra), p_count), jnp.float32)
-        list_ref[...] = jnp.concatenate(rows + extra + [rest], axis=0).astype(jnp.int32)
-        copy = pltpu.make_async_copy(list_ref, scalar_ref, list_sem)
-        copy.start()
-        copy.wait()
-
-    def unit(index):
-        tokens = [query_ref[scalar_ref[slot, index]] for slot in range(SLOTS)]
+        before = (row < column).astype(jnp.float32)
+        place = jnp.dot(left, before, preferred_element_type=jnp.float32)
+        chosen = jnp.where((place == row) & (left > 0.0), 1.0, 0.0)
+        rest = jnp.zeros((LIST_ROWS - SLOTS - 1, p_count), jnp.float32)
+        spread = jnp.concatenate(ids_from(first) + [column[:1], rest], axis=0)
+        close = lax.dot_general(
+            spread, chosen, (((1,), (1,)), ((), ())), preferred_element_type=jnp.float32
+        )
+        number = jnp.broadcast_to(jnp.sum(left, axis=1, keepdims=True), left.shape)
+        rows = [close[: SLOTS + 1], number, rest[1:]]
+        left_ref[...] = jnp.concatenate(rows, axis=0).astype(jnp.int32)
+
+    def unit(index, ids_ref, place):
+        tokens = [query_ref[ids_ref[slot, place]] for slot in range(SLOTS)]
         return token_max(passage_ref[pl.ds(index, 1)], jnp.concatenate(tokens, axis=0))
 
-    def add_scores(first):
-        sums = token_sum(best_ref[...], SLOTS)
+    def add_scores(best, first):
+        sums = token_sum(best, SLOTS)
         for index, out_ref in enumerate(out_refs):
             rank = rank_ref[index * q_count : (index + 1) * q_count] - first
+            scores = out_ref[...]
             for slot in range(SLOTS):
-                out_ref[...] = jnp.where(rank == float(slot), sums[slot : slot + 1], out_ref[...])
+                scores = jnp.where(rank == float(slot), sums[slot : slot + 1], scores)
+            out_ref[...] = scores
 
     for out_ref in out_refs:
         out_ref[...] = jnp.zeros_like(out_ref)
-    write_list(0.0, [most])
-    rounds = (scalar_ref[SLOTS, 0] + SLOTS - 1) // SLOTS
+    write_list()
+    list_copy.start()
+    write_left(float(SLOTS))
+    left_copy.start()
+    list_copy.wait()
 
     @pl.loop(0, chunks)
     def _(chunk):
         fetch(chunk).wait()
         for start in range(0, CHUNK, 8):
             first = pl.multiple_of(chunk * CHUNK + start, 8)
-            rows = [unit(first + offset) for offset in range(8)]
+            rows = [unit(first + offset, scalar_ref, first + offset) for offset in range(8)]
             best_ref[pl.ds(first, 8), :] = jnp.concatenate(rows, axis=0)
 
-    add_scores(0.0)
-
-    @pl.loop(1, rounds)
+    left_copy.wait()
+    add_scores(best_ref[...], 0.0)
+
+    @pl.loop(1, (scalar_ref[SLOTS, 0] + SLOTS - 1) // SLOTS)
     def _(turn):
         done = (turn * SLOTS).astype(jnp.float32)
-        write_list(done, left_over(done))
-
-        @pl.loop(0, scalar_ref[SLOTS + 1, 0])
-        def _(place):
-            index = scalar_ref[SLOTS, place]
-            best_ref[pl.ds(index, 1), :] = unit(index)
-
-        add_scores(done)
+
+        @pl.when(turn > 1)
+        def _():
+            write_left(done)
+            left_copy.start()
+            left_copy.wait()
+
+        number = left_scalar_ref[SLOTS + 1, 0]
+
+        @pl.loop(0, (number + STEP - 1) // STEP)
+        def _(block):
+            rows = []
+            for offset in range(STEP):
+                place = block * STEP + offset
+                index = left_scalar_ref[SLOTS, place]
+                rows.append((place, index, unit(index, left_scalar_ref, place)))
+            for place, index, row in rows:
+                kept = jnp.where(place < number, index, p_count)
+                left_best_ref[pl.ds(kept, 1), :] = row
+
+        add_scores(left_best_ref[:p_count], done)
 
 
 def score_memory(packed, memory, q_count, slots):
@@ -218,10 +247,13 @@
             pltpu.VMEM((total, q_tokens, depth), memory.dtype),
             pltpu.VMEM((total, p_count), jnp.float32),
             pltpu.VMEM((p_count, SLOTS * q_tokens), jnp.float32),
+            pltpu.VMEM((p_count + 8, SLOTS * q_tokens), jnp.float32),
+            pltpu.VMEM((LIST_ROWS, p_count), jnp.int32),
+            pltpu.SMEM((LIST_ROWS, p_count), jnp.int32),
             pltpu.VMEM((LIST_ROWS, p_count), jnp.int32),
             pltpu.SMEM((LIST_ROWS, p_count), jnp.int32),
             pltpu.SemaphoreType.DMA((p_count // CHUNK,)),
-            pltpu.SemaphoreType.DMA,
+            pltpu.SemaphoreType.DMA((2,)),
         ],
         compiler_params=pltpu.CompilerParams(vmem_limit_bytes=16 * MIB),
         cost_estimate=pl.CostEstimate(

time: 25.3 us -> 26.4 us (1.043)
  Pallas kernels: 7.79 us -> 8.33 us
  waiting for transfers between devices: 2.54 us -> 3.05 us
    ppermute x6, waiting for transfers between devices: 2.39 us -> 3.04 us  [to_shard(): return lax.ppermute(array, 'memory', [(i, i ^ step) for i in range(shards)])]
    pallas_call x1, Pallas kernels: 4.42 us -> 4.95 us  [score_memory(): pl.pallas_call(functools.partial(memory_kernel, shards, slots), in_specs=...]
  transfers between devices with their start and end apart: 11 -> 11, of which waited for: 3 -> 2; matrix products, arithmetic and copies ran while one was open for 0% -> 0% of each run, Pallas kernels for 24% -> 25%
where the time goes in v1:
time: 26.4 us; the launch traced here: 26.2 us
  starting transfers between devices  14.1 us (53%)
  Pallas kernels  8.33 us (32%)
  waiting for transfers between devices  3.05 us (12%)
  between operations  0.71 us (3%)
    ppermute x6, starting transfers between devices, to_shard(): return lax.ppermute(array, 'memory', [(i, i ^ step) for i in range(shards)])  10.2 us
    pallas_call x1, Pallas kernels, score_memory(): pl.pallas_call(functools.partial(memory_kernel, shards, slots), in_specs=...  4.95 us
    ppermute x5, starting transfers between devices, to_group(): return lax.ppermute(array, 'group', [(i, i ^ step) for i in range(groups)])  3.88 us
    ppermute x6, waiting for transfers between devices, to_shard(): return lax.ppermute(array, 'memory', [(i, i ^ step) for i in range(shards)])  3.04 us
    pallas_call x2, Pallas kernels, score_batch(): pl.pallas_call(batch_kernel, out_shape=jax.ShapeDtypeStruct((q_count, lan...  1.71 us
    pallas_call x1, Pallas kernels, pack(): pl.pallas_call(functools.partial(pack_kernel, p_count), in_specs=[vmem, v...  0.87 us
    pallas_call x1, Pallas kernels, finish(): pl.pallas_call(functools.partial(loss_kernel, len(memory_parts)), out_sha...  0.8 us
  transfers between devices with their start and end apart: 11, of which 2 were waited for; matrix products, arithmetic and copies ran while one was open for 0% of the time, Pallas kernels for 25%

profile of v1, /device:TPU:0, one launch (start us, length us, event | category | flops | bytes accessed | tf_op | source)
XLA Modules:
  0.0 26.2 jit_solution(5272722879506808946)
XLA Ops:
  0.6 0.9 %pack.1.refs_0_ = bf16[272,128]{1,0:T(8,128)(2,1)S(1)} custom-call(bf16[1,8,32,128]{3,2,1,0:T(8,128)(2,1)} %query_ref.2, s32[1,8,64]{2,1,0:T(8,128)} %refs_4_.3, s32[1,8]{1,0:T(1,128)} %refs_5_.1), custom_call_target="tpu_custom_call" | custom-call | tf_op jit(solution)/shard_map/pack/pallas_call | solution.py:90
  1.5 0.0 copy-start
  1.5 0.0 copy-start.1
  1.5 0.0 copy-start.2
  1.5 0.0 copy-start.3
  1.6 5.1 %collective-permute-start.3 = (bf16[272,128]{1,0:T(8,128)(2,1)S(1)}, bf16[272,128]{1,0:T(8,128)(2,1)S(1)}, u32[]{:S(2)}, u32[]{:S(2)}) collective-permute-start(bf16[272,128]{1,0:T(8,128)(2,1)S(1)} %pack.1.refs_0_), channel_id=1, source_target_pairs={{0,24},{8,16},{16,8},{24,0},{1,25},{9,17},{17,9},{25,1},{2,26},{10... | collective-permute-start | bytes 208904 | tf_op jit(solution)/shard_map/ppermute | solution.py:365
  6.7 0.0 collective-permute-start.2
  6.7 0.6 %collective-permute-start.1 = (bf16[272,128]{1,0:T(8,128)(2,1)S(1)}, bf16[272,128]{1,0:T(8,128)(2,1)S(1)}, u32[]{:S(2)}, u32[]{:S(2)}) collective-permute-start(bf16[272,128]{1,0:T(8,128)(2,1)S(1)} %pack.1.refs_0_), channel_id=1, source_target_pairs={{0,8},{8,0},{16,24},{24,16},{1,9},{9,1},{17,25},{25,17},{2,10},{10... | collective-permute-start | bytes 208904 | tf_op jit(solution)/shard_map/ppermute | solution.py:365
  7.3 2.6 %collective-permute-start.6 = (bf16[1,8,128,128]{3,2,1,0:T(8,128)(2,1)}, bf16[1,8,128,128]{3,2,1,0:T(8,128)(2,1)S(1)}, u32[]{:S(2)}, u32[]{:S(2)}) collective-permute-start(bf16[1,8,128,128]{3,2,1,0:T(8,128)(2,1)} %refs_0_.3), channel_id=1, source_target_pairs={{0,6},{1,7},{2,4},{3,5},{4,2},{5,3},{6,0},{7,1},{8,14},{9,15},{10,... | collective-permute-start | bytes 786440 | tf_op jit(solution)/shard_map/ppermute | solution.py:368
  9.9 0.5 %collective-permute-start.5 = (bf16[1,8,128,128]{3,2,1,0:T(8,128)(2,1)}, bf16[1,8,128,128]{3,2,1,0:T(8,128)(2,1)S(1)}, u32[]{:S(2)}, u32[]{:S(2)}) collective-permute-start(bf16[1,8,128,128]{3,2,1,0:T(8,128)(2,1)} %refs_0_.3), channel_id=1, source_target_pairs={{0,4},{1,5},{2,6},{3,7},{4,0},{5,1},{6,2},{7,3},{8,12},{9,13},{10,... | collective-permute-start | bytes 786440 | tf_op jit(solution)/shard_map/ppermute | solution.py:368
  10.4 0.0 collective-permute-done.3.refs_3_
  10.4 0.8 %collective-permute-start.4 = (bf16[1,8,128,128]{3,2,1,0:T(8,128)(2,1)}, bf16[1,8,128,128]{3,2,1,0:T(8,128)(2,1)S(1)}, u32[]{:S(2)}, u32[]{:S(2)}) collective-permute-start(bf16[1,8,128,128]{3,2,1,0:T(8,128)(2,1)} %refs_0_.3), channel_id=1, source_target_pairs={{0,2},{1,3},{2,0},{3,1},{4,6},{5,7},{6,4},{7,5},{8,10},{9,11},{10,... | collective-permute-start | bytes 786440 | tf_op jit(solution)/shard_map/ppermute | solution.py:368
  11.2 1.4 %collective-permute-done.2.refs_2_ = bf16[272,128]{1,0:T(8,128)(2,1)S(1)} collective-permute-done((bf16[272,128]{1,0:T(8,128)(2,1)S(1)}, bf16[272,128]{1,0:T(8,128)(2,1)S(1)}, u32[]{:S(2)}, u32[]{:S(2)}) %collective-permute-start.2) | collective-permute-done | bytes 69664 | tf_op jit(solution)/shard_map/ppermute | solution.py:365
  12.6 0.0 collective-permute-start
  12.6 0.0 collective-permute-done.1.refs_1_
  12.6 4.9 %score_memory.1 = (f32[8,128]{1,0:T(8,128)S(1)}, f32[8,128]{1,0:T(8,128)S(1)}, f32[8,128]{1,0:T(8,128)S(1)}, f32[8,128]{1,0:T(8,128)S(1)}) custom-call(bf16[272,128]{1,0:T(8,128)(2,1)S(1)} %pack.1.refs_0_, bf16[272,128]{1,0:T(8,128)(2,1)S(1)} %collective-permute-done.1.refs_1_, bf16[272,128]{1,0:T(8,128)(2,1)S(1)} %collective-permute-done.2.refs_2_, ...), custom_call_target="tpu_custom_call" | custom-call | flops 4294967296 | bytes 4194304 | tf_op jit(solution)/shard_map/score_memory/pallas_call | solution.py:240
  17.5 0.0 collective-permute-done.query_ref
  17.6 3.3 %collective-permute-start.8 = (f32[8,128]{1,0:T(8,128)S(1)}, f32[8,128]{1,0:T(8,128)S(1)}, u32[]{:S(2)}, u32[]{:S(2)}) collective-permute-start(f32[8,128]{1,0:T(8,128)S(1)} %get-tuple-element.16), channel_id=1, source_target_pairs={{0,24},{8,16},{16,8},{24,0},{1,25},{9,17},{17,9},{25,1},{2,26},{10... | collective-permute-start | bytes 12296 | tf_op jit(solution)/shard_map/ppermute | solution.py:365
  20.9 0.0 collective-permute-start.9
  20.9 0.0 collective-permute-done.6.refs_3_
  20.9 1.1 %collective-permute-start.10 = (f32[8,128]{1,0:T(8,128)S(1)}, f32[8,128]{1,0:T(8,128)S(1)}, u32[]{:S(2)}, u32[]{:S(2)}) collective-permute-start(f32[8,128]{1,0:T(8,128)S(1)} %get-tuple-element.18), channel_id=1, source_target_pairs={{0,8},{8,0},{16,24},{24,16},{1,9},{9,1},{17,25},{25,17},{2,10},{10... | collective-permute-start | bytes 12296 | tf_op jit(solution)/shard_map/ppermute | solution.py:365
  22.0 0.0 collective-permute-done.5.refs_2_
  22.0 0.0 collective-permute-done.4.refs_1_
  22.0 0.0 copy-done
  22.0 0.8 %score_batch.2 = f32[8,128]{1,0:T(8,128)S(1)} custom-call(bf16[1,8,32,128]{3,2,1,0:T(8,128)(2,1)S(1)} %collective-permute-done.query_ref, bf16[1,8,128,128]{3,2,1,0:T(8,128)(2,1)S(1)} %copy-done, bf16[1,8,128,128]{3,2,1,0:T(8,128)(2,1)S(1)} %collective-permute-done.4.refs_1_, bf16[1,8,128,128]{3,2,1,0:T(8,128)(2,1)S(1)} %collective-permute-done.5.refs_2_, ...), custom_call_target="tpu_custom_call" | custom-call | flops 268435456 | bytes 1048576 | tf_op jit(solution)/shard_map/score_batch/pallas_call | solution.py:285
  22.9 0.0 collective-permute-start.7
  22.9 0.9 %score_batch.3.own_batch = f32[8,128]{1,0:T(8,128)S(1)} custom-call(bf16[1,8,32,128]{3,2,1,0:T(8,128)(2,1)S(1)} %copy-done.1, bf16[1,8,128,128]{3,2,1,0:T(8,128)(2,1)S(1)} %copy-done, bf16[1,8,128,128]{3,2,1,0:T(8,128)(2,1)S(1)} %collective-permute-done.4.refs_1_, bf16[1,8,128,128]{3,2,1,0:T(8,128)(2,1)S(1)} %collective-permute-done.5.refs_2_, ...), custom_call_target="tpu_custom_call" | custom-call | flops 268435456 | bytes 1048576 | tf_op jit(solution)/shard_map/score_batch/pallas_call | solution.py:285
  23.7 0.0 collective-permute-done.8.refs_1_
  23.7 1.6 %collective-permute-done.9.refs_2_ = f32[8,128]{1,0:T(8,128)S(1)} collective-permute-done((f32[8,128]{1,0:T(8,128)S(1)}, f32[8,128]{1,0:T(8,128)S(1)}, u32[]{:S(2)}, u32[]{:S(2)}) %collective-permute-start.9) | collective-permute-done | bytes 4128 | tf_op jit(solution)/shard_map/ppermute | solution.py:365
  25.4 0.0 collective-permute-done.10.refs_3_
  25.4 0.0 collective-permute-done.7.mate_batch
  25.4 0.8 %finish.1 = (f32[1,8,64]{2,1,0:T(8,128)}, f32[1,8,64]{2,1,0:T(8,128)}, f32[1,8]{1,0:T(1,128)}) custom-call(f32[8,128]{1,0:T(8,128)S(1)} %score_batch.3.own_batch, f32[8,128]{1,0:T(8,128)S(1)} %collective-permute-done.7.mate_batch, f32[8,128]{1,0:T(8,128)S(1)} %get-tuple-element.12.refs_0_, f32[8,128]{1,0:T(8,128)S(1)} %collective-permute-done.8.refs_1_, ...), custom_call_target="tpu_custom_call" | custom-call | tf_op jit(solution)/shard_map/finish/pallas_call | solution.py:345
  (3 shorter events, 0.0 us)
Async XLA Ops:
  1.5 20.5 %copy-start = (bf16[1,8,128,128]{3,2,1,0:T(8,128)(2,1)S(1)}, bf16[1,8,128,128]{3,2,1,0:T(8,128)(2,1)}, u32[]{:S(2)}) copy-start(bf16[1,8,128,128]{3,2,1,0:T(8,128)(2,1)} %refs_0_.3) | copy-start | bytes 786436
  1.5 21.4 %copy-start.1 = (bf16[1,8,32,128]{3,2,1,0:T(8,128)(2,1)S(1)}, bf16[1,8,32,128]{3,2,1,0:T(8,128)(2,1)}, u32[]{:S(2)}) copy-start(bf16[1,8,32,128]{3,2,1,0:T(8,128)(2,1)} %query_ref.2) | copy-start | bytes 196612
  1.5 23.9 %copy-start.2 = (s32[1,8,64]{2,1,0:T(8,128)S(1)}, s32[1,8,64]{2,1,0:T(8,128)}, u32[]{:S(2)}) copy-start(s32[1,8,64]{2,1,0:T(8,128)} %refs_4_.3) | copy-start | bytes 6148
  1.5 23.9 %copy-start.3 = (s32[1,8]{1,0:T(1,128)S(1)}, s32[1,8]{1,0:T(1,128)}, u32[]{:S(2)}) copy-start(s32[1,8]{1,0:T(1,128)} %refs_5_.1) | copy-start | bytes 100
  1.6 8.9 %collective-permute-start.3 = (bf16[272,128]{1,0:T(8,128)(2,1)S(1)}, bf16[272,128]{1,0:T(8,128)(2,1)S(1)}, u32[]{:S(2)}, u32[]{:S(2)}) collective-permute-start(bf16[272,128]{1,0:T(8,128)(2,1)S(1)} %pack.1.refs_0_), channel_id=1, source_target_pairs={{0,24},{8,16},{16,8},{24,0},{1,25},{9,17},{17,9},{25,1},{2,26},{10... | collective-permute-start | bytes 208904 | tf_op jit(solution)/shard_map/ppermute | solution.py:365
  6.7 5.9 %collective-permute-start.2 = (bf16[272,128]{1,0:T(8,128)(2,1)S(1)}, bf16[272,128]{1,0:T(8,128)(2,1)S(1)}, u32[]{:S(2)}, u32[]{:S(2)}) collective-permute-start(bf16[272,128]{1,0:T(8,128)(2,1)S(1)} %pack.1.refs_0_), channel_id=1, source_target_pairs={{0,16},{8,24},{16,0},{24,8},{1,17},{9,25},{17,1},{25,9},{2,18},{10... | collective-permute-start | bytes 208904 | tf_op jit(solution)/shard_map/ppermute | solution.py:365
  6.7 5.9 %collective-permute-start.1 = (bf16[272,128]{1,0:T(8,128)(2,1)S(1)}, bf16[272,128]{1,0:T(8,128)(2,1)S(1)}, u32[]{:S(2)}, u32[]{:S(2)}) collective-permute-start(bf16[272,128]{1,0:T(8,128)(2,1)S(1)} %pack.1.refs_0_), channel_id=1, source_target_pairs={{0,8},{8,0},{16,24},{24,16},{1,9},{9,1},{17,25},{25,17},{2,10},{10... | collective-permute-start | bytes 208904 | tf_op jit(solution)/shard_map/ppermute | solution.py:365
  7.3 13.6 %collective-permute-start.6 = (bf16[1,8,128,128]{3,2,1,0:T(8,128)(2,1)}, bf16[1,8,128,128]{3,2,1,0:T(8,128)(2,1)S(1)}, u32[]{:S(2)}, u32[]{:S(2)}) collective-permute-start(bf16[1,8,128,128]{3,2,1,0:T(8,128)(2,1)} %refs_0_.3), channel_id=1, source_target_pairs={{0,6},{1,7},{2,4},{3,5},{4,2},{5,3},{6,0},{7,1},{8,14},{9,15},{10,... | collective-permute-start | bytes 786440 | tf_op jit(solution)/shard_map/ppermute | solution.py:368
  9.9 12.1 %collective-permute-start.5 = (bf16[1,8,128,128]{3,2,1,0:T(8,128)(2,1)}, bf16[1,8,128,128]{3,2,1,0:T(8,128)(2,1)S(1)}, u32[]{:S(2)}, u32[]{:S(2)}) collective-permute-start(bf16[1,8,128,128]{3,2,1,0:T(8,128)(2,1)} %refs_0_.3), channel_id=1, source_target_pairs={{0,4},{1,5},{2,6},{3,7},{4,0},{5,1},{6,2},{7,3},{8,12},{9,13},{10,... | collective-permute-start | bytes 786440 | tf_op jit(solution)/shard_map/ppermute | solution.py:368
  10.4 11.6 %collective-permute-start.4 = (bf16[1,8,128,128]{3,2,1,0:T(8,128)(2,1)}, bf16[1,8,128,128]{3,2,1,0:T(8,128)(2,1)S(1)}, u32[]{:S(2)}, u32[]{:S(2)}) collective-permute-start(bf16[1,8,128,128]{3,2,1,0:T(8,128)(2,1)} %refs_0_.3), channel_id=1, source_target_pairs={{0,2},{1,3},{2,0},{3,1},{4,6},{5,7},{6,4},{7,5},{8,10},{9,11},{10,... | collective-permute-start | bytes 786440 | tf_op jit(solution)/shard_map/ppermute | solution.py:368
  12.6 5.0 %collective-permute-start = (bf16[1,8,32,128]{3,2,1,0:T(8,128)(2,1)}, bf16[1,8,32,128]{3,2,1,0:T(8,128)(2,1)S(1)}, u32[]{:S(2)}, u32[]{:S(2)}) collective-permute-start(bf16[1,8,32,128]{3,2,1,0:T(8,128)(2,1)} %query_ref.2), channel_id=1, source_target_pairs={{0,1},{1,0},{2,3},{3,2},{4,5},{5,4},{6,7},{7,6},{8,9},{9,8},{10,11... | collective-permute-start | bytes 196616 | tf_op jit(solution)/shard_map/ppermute | solution.py:368
  17.6 6.2 %collective-permute-start.8 = (f32[8,128]{1,0:T(8,128)S(1)}, f32[8,128]{1,0:T(8,128)S(1)}, u32[]{:S(2)}, u32[]{:S(2)}) collective-permute-start(f32[8,128]{1,0:T(8,128)S(1)} %get-tuple-element.16), channel_id=1, source_target_pairs={{0,24},{8,16},{16,8},{24,0},{1,25},{9,17},{17,9},{25,1},{2,26},{10... | collective-permute-start | bytes 12296 | tf_op jit(solution)/shard_map/ppermute | solution.py:365
  20.9 4.5 %collective-permute-start.9 = (f32[8,128]{1,0:T(8,128)S(1)}, f32[8,128]{1,0:T(8,128)S(1)}, u32[]{:S(2)}, u32[]{:S(2)}) collective-permute-start(f32[8,128]{1,0:T(8,128)S(1)} %get-tuple-element.17), channel_id=1, source_target_pairs={{0,16},{8,24},{16,0},{24,8},{1,17},{9,25},{17,1},{25,9},{2,18},{10... | collective-permute-start | bytes 12296 | tf_op jit(solution)/shard_map/ppermute | solution.py:365
  20.9 4.5 %collective-permute-start.10 = (f32[8,128]{1,0:T(8,128)S(1)}, f32[8,128]{1,0:T(8,128)S(1)}, u32[]{:S(2)}, u32[]{:S(2)}) collective-permute-start(f32[8,128]{1,0:T(8,128)S(1)} %get-tuple-element.18), channel_id=1, source_target_pairs={{0,8},{8,0},{16,24},{24,16},{1,9},{9,1},{17,25},{25,17},{2,10},{10... | collective-permute-start | bytes 12296 | tf_op jit(solution)/shard_map/ppermute | solution.py:365
  22.9 2.5 %collective-permute-start.7 = (f32[8,128]{1,0:T(8,128)S(1)}, f32[8,128]{1,0:T(8,128)S(1)}, u32[]{:S(2)}, u32[]{:S(2)}) collective-permute-start(f32[8,128]{1,0:T(8,128)S(1)} %score_batch.2), channel_id=1, source_target_pairs={{0,1},{1,0},{2,3},{3,2},{4,5},{5,4},{6,7},{7,6},{8,9},{9,8},{10,11... | collective-permute-start | bytes 12296 | tf_op jit(solution)/shard_map/ppermute | solution.py:368

commit v2 on v1

--- a/solution.py
+++ b/solution.py
@@ -9,10 +9,10 @@
 
 LANES = 128
 MIB = 1024 * 1024
-SLOTS = 4
+SLOTS = 8
 CHUNK = 32
-LIST_ROWS = 8
-STEP = 8
+LIST_ROWS = 16
+STEP = 4
 
 
 def in_hbm(array):
@@ -63,6 +63,11 @@
     return jnp.sum(jnp.where(diagonal, jnp.broadcast_to(column, square), 0), axis=0, keepdims=True)
 
 
+def other_half(row):
+    half = row.shape[1] // 2
+    return jnp.concatenate([row[:, half:], row[:, :half]], axis=1)
+
+
 def split_ids(p_count, candidate_ref, count_ref):
     ids = candidate_ref[0]
     row = lax.broadcasted_iota(jnp.int32, ids.shape, 0)
@@ -103,23 +108,27 @@
     list_ref, scalar_ref, left_ref, left_scalar_ref, copy_sems, list_sems = refs
     q_count = out_refs[0].shape[0]
     p_count = passage_ref.shape[0]
-    total, q_tokens, depth = query_ref.shape
-    chunks = p_count // CHUNK
-
-    def fetch(chunk):
-        rows = pl.ds(pl.multiple_of(chunk * CHUNK, CHUNK), CHUNK)
+    total, q_tokens, depth = (size // parts for size, parts in zip(query_ref.shape, (2, 1, 2)))
+    half = p_count // 2
+    chunks = half // CHUNK
+
+    def fetch(chunk, side):
+        rows = pl.ds(pl.multiple_of(side * half + chunk * CHUNK, CHUNK), CHUNK)
         return pltpu.make_async_copy(
-            memory_ref.at[0, rows], passage_ref.at[rows], copy_sems.at[chunk]
+            memory_ref.at[0, rows], passage_ref.at[rows], copy_sems.at[chunk, side]
         )
 
     for chunk in range(chunks):
-        fetch(chunk).start()
+        for side in range(2):
+            fetch(chunk, side).start()
 
     me = lax.axis_index("memory").astype(jnp.float32)
     keys = []
     for index, packed_ref in enumerate(packed_refs):
         tokens = packed_ref[: q_count * q_tokens].reshape(q_count, q_tokens, depth)
-        query_ref[index * q_count : (index + 1) * q_count] = tokens
+        rows = slice(index * q_count, (index + 1) * q_count)
+        query_ref[rows] = jnp.concatenate([tokens, jnp.zeros_like(tokens)], axis=2)
+        query_ref[index * q_count + total : (index + 1) * q_count + total] = jnp.concatenate([jnp.zeros_like(tokens), tokens], axis=2)
         planes = packed_ref[q_count * q_tokens :].astype(jnp.float32)
         local, holder = planes[:q_count], planes[q_count:]
         keys.append(jnp.where(holder == me, local, -1.0))
@@ -134,18 +143,23 @@
         jnp.int32, square, 0
     )
     before = jnp.dot(earlier.astype(jnp.float32), named, preferred_element_type=jnp.float32)
+    counts = jnp.sum(named, axis=0, keepdims=True)
+    upper = passage >= half
+    before = before + jnp.where(upper, other_half(counts), 0.0)
     rank_ref[...] = jnp.where(named > 0.0, before, -1.0)
-    counts = jnp.sum(named, axis=0, keepdims=True)
-    most = jnp.broadcast_to(jnp.max(counts, axis=1, keepdims=True), counts.shape)
+    both = counts + other_half(counts)
+    most = jnp.broadcast_to(jnp.max(both, axis=1, keepdims=True), counts.shape)
 
     asker = lax.broadcasted_iota(jnp.int32, (total, p_count), 0).astype(jnp.float32)
+    asker = jnp.where(upper, asker + total, asker)
 
     def ids_from(first):
         rank = rank_ref[...] - first
-        return [
+        rows = [
             jnp.sum(jnp.where(rank == float(slot), asker, 0.0), axis=0, keepdims=True)
             for slot in range(SLOTS)
         ]
+        return [row + other_half(row) for row in rows]
 
     list_copy = pltpu.make_async_copy(list_ref, scalar_ref, list_sems.at[0])
     left_copy = pltpu.make_async_copy(left_ref, left_scalar_ref, list_sems.at[1])
@@ -158,6 +172,7 @@
     def write_left(first):
         left = jnp.where(rank_ref[...] == first, 1.0, 0.0)
         left = jnp.sum(left, axis=0, keepdims=True)
+        left = jnp.where(upper[:1], 0.0, left + other_half(left))
         square = (p_count, p_count)
         row = lax.broadcasted_iota(jnp.int32, square, 0).astype(jnp.float32)
         column = lax.broadcasted_iota(jnp.int32, square, 1).astype(jnp.float32)
@@ -175,10 +190,12 @@
 
     def unit(index, ids_ref, place):
         tokens = [query_ref[ids_ref[slot, place]] for slot in range(SLOTS)]
-        return token_max(passage_ref[pl.ds(index, 1)], jnp.concatenate(tokens, axis=0))
+        pair = [passage_ref[pl.ds(index + side * half, 1)] for side in range(2)]
+        return token_max(jnp.concatenate(pair, axis=2), jnp.concatenate(tokens, axis=0))
 
     def add_scores(best, first):
         sums = token_sum(best, SLOTS)
+        sums = jnp.concatenate([sums, sums], axis=1)
         for index, out_ref in enumerate(out_refs):
             rank = rank_ref[index * q_count : (index + 1) * q_count] - first
             scores = out_ref[...]
@@ -196,7 +213,8 @@
 
     @pl.loop(0, chunks)
     def _(chunk):
-        fetch(chunk).wait()
+        for side in range(2):
+            fetch(chunk, side).wait()
         for start in range(0, CHUNK, 8):
             first = pl.multiple_of(chunk * CHUNK + start, 8)
             rows = [unit(first + offset, scalar_ref, first + offset) for offset in range(8)]
@@ -225,10 +243,10 @@
                 index = left_scalar_ref[SLOTS, place]
                 rows.append((place, index, unit(index, left_scalar_ref, place)))
             for place, index, row in rows:
-                kept = jnp.where(place < number, index, p_count)
+                kept = jnp.where(place < number, index, half)
                 left_best_ref[pl.ds(kept, 1), :] = row
 
-        add_scores(left_best_ref[:p_count], done)
+        add_scores(left_best_ref[:half], done)
 
 
 def score_memory(packed, memory, q_count, slots):
@@ -244,18 +262,18 @@
         out_shape=[jax.ShapeDtypeStruct((q_count, p_count), jnp.float32)] * shards,
         scratch_shapes=[
             pltpu.VMEM((p_count, p_tokens, depth), memory.dtype),
-            pltpu.VMEM((total, q_tokens, depth), memory.dtype),
+            pltpu.VMEM((2 * total, q_tokens, 2 * depth), memory.dtype),
             pltpu.VMEM((total, p_count), jnp.float32),
-            pltpu.VMEM((p_count, SLOTS * q_tokens), jnp.float32),
-            pltpu.VMEM((p_count + 8, SLOTS * q_tokens), jnp.float32),
+            pltpu.VMEM((p_count // 2, SLOTS * q_tokens), jnp.float32),
+            pltpu.VMEM((p_count // 2 + 8, SLOTS * q_tokens), jnp.float32),
             pltpu.VMEM((LIST_ROWS, p_count), jnp.int32),
             pltpu.SMEM((LIST_ROWS, p_count), jnp.int32),
             pltpu.VMEM((LIST_ROWS, p_count), jnp.int32),
             pltpu.SMEM((LIST_ROWS, p_count), jnp.int32),
-            pltpu.SemaphoreType.DMA((p_count // CHUNK,)),
+            pltpu.SemaphoreType.DMA((p_count // 2 // CHUNK, 2)),
             pltpu.SemaphoreType.DMA((2,)),
         ],
-        compiler_params=pltpu.CompilerParams(vmem_limit_bytes=16 * MIB),
+        compiler_params=pltpu.CompilerParams(vmem_limit_bytes=20 * MIB),
         cost_estimate=pl.CostEstimate(
             flops=2 * total * q_tokens * p_count * p_tokens * depth,
             bytes_accessed=2 * p_count * p_tokens * depth,

time: 26.4 us -> 25.8 us (0.977)
  waiting for transfers between devices: 3.05 us -> 2.53 us
    ppermute x6, waiting for transfers between devices: 3.04 us -> 2.52 us  [to_shard(): return lax.ppermute(array, 'memory', [(i, i ^ step) for i in range(shards)])]
  transfers between devices with their start and end apart: 11 -> 11, of which waited for: 2 -> 2; matrix products, arithmetic and copies ran while one was open for 0% -> 0% of each run, Pallas kernels for 25% -> 26%
where the time goes in v2:
time: 25.8 us; the launch traced here: 25.6 us
  starting transfers between devices  14.1 us (55%)
  Pallas kernels  8.28 us (32%)
  waiting for transfers between devices  2.53 us (10%)
  between operations  0.71 us (3%)
    ppermute x6, starting transfers between devices, to_shard(): return lax.ppermute(array, 'memory', [(i, i ^ step) for i in range(shards)])  10.2 us
    pallas_call x1, Pallas kernels, score_memory(): pl.pallas_call(functools.partial(memory_kernel, shards, slots), in_specs=...  4.92 us
    ppermute x5, starting transfers between devices, to_group(): return lax.ppermute(array, 'group', [(i, i ^ step) for i in range(groups)])  3.88 us
    ppermute x6, waiting for transfers between devices, to_shard(): return lax.ppermute(array, 'memory', [(i, i ^ step) for i in range(shards)])  2.52 us
    pallas_call x2, Pallas kernels, score_batch(): pl.pallas_call(batch_kernel, out_shape=jax.ShapeDtypeStruct((q_count, lan...  1.69 us
    pallas_call x1, Pallas kernels, pack(): pl.pallas_call(functools.partial(pack_kernel, p_count), in_specs=[vmem, v...  0.87 us
    pallas_call x1, Pallas kernels, finish(): pl.pallas_call(functools.partial(loss_kernel, len(memory_parts)), out_sha...  0.8 us
  transfers between devices with their start and end apart: 11, of which 2 were waited for; matrix products, arithmetic and copies ran while one was open for 0% of the time, Pallas kernels for 26%

profile of v2, /device:TPU:0, one launch (start us, length us, event | category | flops | bytes accessed | tf_op | source)
XLA Modules:
  0.0 25.6 jit_solution(2751179645625206470)
XLA Ops:
  0.6 0.9 %pack.1.refs_0_ = bf16[272,128]{1,0:T(8,128)(2,1)S(1)} custom-call(bf16[1,8,32,128]{3,2,1,0:T(8,128)(2,1)} %query_ref.2, s32[1,8,64]{2,1,0:T(8,128)} %refs_4_.3, s32[1,8]{1,0:T(1,128)} %refs_5_.1), custom_call_target="tpu_custom_call" | custom-call | tf_op jit(solution)/shard_map/pack/pallas_call | solution.py:95
  1.5 0.0 copy-start
  1.5 0.0 copy-start.1
  1.5 0.0 copy-start.2
  1.5 0.0 copy-start.3
  1.6 5.1 %collective-permute-start.3 = (bf16[272,128]{1,0:T(8,128)(2,1)S(1)}, bf16[272,128]{1,0:T(8,128)(2,1)S(1)}, u32[]{:S(2)}, u32[]{:S(2)}) collective-permute-start(bf16[272,128]{1,0:T(8,128)(2,1)S(1)} %pack.1.refs_0_), channel_id=1, source_target_pairs={{0,24},{8,16},{16,8},{24,0},{1,25},{9,17},{17,9},{25,1},{2,26},{10... | collective-permute-start | bytes 208904 | tf_op jit(solution)/shard_map/ppermute | solution.py:383
  6.7 0.0 collective-permute-start.2
  6.7 0.6 %collective-permute-start.1 = (bf16[272,128]{1,0:T(8,128)(2,1)S(1)}, bf16[272,128]{1,0:T(8,128)(2,1)S(1)}, u32[]{:S(2)}, u32[]{:S(2)}) collective-permute-start(bf16[272,128]{1,0:T(8,128)(2,1)S(1)} %pack.1.refs_0_), channel_id=1, source_target_pairs={{0,8},{8,0},{16,24},{24,16},{1,9},{9,1},{17,25},{25,17},{2,10},{10... | collective-permute-start | bytes 208904 | tf_op jit(solution)/shard_map/ppermute | solution.py:383
  7.3 2.6 %collective-permute-start.6 = (bf16[1,8,128,128]{3,2,1,0:T(8,128)(2,1)}, bf16[1,8,128,128]{3,2,1,0:T(8,128)(2,1)S(1)}, u32[]{:S(2)}, u32[]{:S(2)}) collective-permute-start(bf16[1,8,128,128]{3,2,1,0:T(8,128)(2,1)} %refs_0_.3), channel_id=1, source_target_pairs={{0,6},{1,7},{2,4},{3,5},{4,2},{5,3},{6,0},{7,1},{8,14},{9,15},{10,... | collective-permute-start | bytes 786440 | tf_op jit(solution)/shard_map/ppermute | solution.py:386
  9.9 0.5 %collective-permute-start.5 = (bf16[1,8,128,128]{3,2,1,0:T(8,128)(2,1)}, bf16[1,8,128,128]{3,2,1,0:T(8,128)(2,1)S(1)}, u32[]{:S(2)}, u32[]{:S(2)}) collective-permute-start(bf16[1,8,128,128]{3,2,1,0:T(8,128)(2,1)} %refs_0_.3), channel_id=1, source_target_pairs={{0,4},{1,5},{2,6},{3,7},{4,0},{5,1},{6,2},{7,3},{8,12},{9,13},{10,... | collective-permute-start | bytes 786440 | tf_op jit(solution)/shard_map/ppermute | solution.py:386
  10.4 0.0 collective-permute-done.3.refs_3_
  10.4 0.8 %collective-permute-start.4 = (bf16[1,8,128,128]{3,2,1,0:T(8,128)(2,1)}, bf16[1,8,128,128]{3,2,1,0:T(8,128)(2,1)S(1)}, u32[]{:S(2)}, u32[]{:S(2)}) collective-permute-start(bf16[1,8,128,128]{3,2,1,0:T(8,128)(2,1)} %refs_0_.3), channel_id=1, source_target_pairs={{0,2},{1,3},{2,0},{3,1},{4,6},{5,7},{6,4},{7,5},{8,10},{9,11},{10,... | collective-permute-start | bytes 786440 | tf_op jit(solution)/shard_map/ppermute | solution.py:386
  11.2 1.4 %collective-permute-done.2.refs_2_ = bf16[272,128]{1,0:T(8,128)(2,1)S(1)} collective-permute-done((bf16[272,128]{1,0:T(8,128)(2,1)S(1)}, bf16[272,128]{1,0:T(8,128)(2,1)S(1)}, u32[]{:S(2)}, u32[]{:S(2)}) %collective-permute-start.2) | collective-permute-done | bytes 69664 | tf_op jit(solution)/shard_map/ppermute | solution.py:383
  12.6 0.0 collective-permute-start
  12.6 0.0 collective-permute-done.1.refs_1_
  12.6 4.9 %score_memory.1 = (f32[8,128]{1,0:T(8,128)S(1)}, f32[8,128]{1,0:T(8,128)S(1)}, f32[8,128]{1,0:T(8,128)S(1)}, f32[8,128]{1,0:T(8,128)S(1)}) custom-call(bf16[272,128]{1,0:T(8,128)(2,1)S(1)} %pack.1.refs_0_, bf16[272,128]{1,0:T(8,128)(2,1)S(1)} %collective-permute-done.1.refs_1_, bf16[272,128]{1,0:T(8,128)(2,1)S(1)} %collective-permute-done.2.refs_2_, ...), custom_call_target="tpu_custom_call" | custom-call | flops 4294967296 | bytes 4194304 | tf_op jit(solution)/shard_map/score_memory/pallas_call | solution.py:258
  17.5 0.0 collective-permute-done.query_ref
  17.5 2.8 %collective-permute-start.8 = (f32[8,128]{1,0:T(8,128)S(1)}, f32[8,128]{1,0:T(8,128)S(1)}, u32[]{:S(2)}, u32[]{:S(2)}) collective-permute-start(f32[8,128]{1,0:T(8,128)S(1)} %get-tuple-element.16), channel_id=1, source_target_pairs={{0,24},{8,16},{16,8},{24,0},{1,25},{9,17},{17,9},{25,1},{2,26},{10... | collective-permute-start | bytes 12296 | tf_op jit(solution)/shard_map/ppermute | solution.py:383
  20.3 0.0 collective-permute-start.9
  20.3 0.0 collective-permute-done.6.refs_3_
  20.3 1.7 %collective-permute-start.10 = (f32[8,128]{1,0:T(8,128)S(1)}, f32[8,128]{1,0:T(8,128)S(1)}, u32[]{:S(2)}, u32[]{:S(2)}) collective-permute-start(f32[8,128]{1,0:T(8,128)S(1)} %get-tuple-element.18), channel_id=1, source_target_pairs={{0,8},{8,0},{16,24},{24,16},{1,9},{9,1},{17,25},{25,17},{2,10},{10... | collective-permute-start | bytes 12296 | tf_op jit(solution)/shard_map/ppermute | solution.py:383
  22.0 0.0 collective-permute-done.5.refs_2_
  22.0 0.0 collective-permute-done.4.refs_1_
  22.0 0.8 %score_batch.2 = f32[8,128]{1,0:T(8,128)S(1)} custom-call(bf16[1,8,32,128]{3,2,1,0:T(8,128)(2,1)S(1)} %collective-permute-done.query_ref, bf16[1,8,128,128]{3,2,1,0:T(8,128)(2,1)S(1)} %copy-done, bf16[1,8,128,128]{3,2,1,0:T(8,128)(2,1)S(1)} %collective-permute-done.4.refs_1_, bf16[1,8,128,128]{3,2,1,0:T(8,128)(2,1)S(1)} %collective-permute-done.5.refs_2_, ...), custom_call_target="tpu_custom_call" | custom-call | flops 268435456 | bytes 1048576 | tf_op jit(solution)/shard_map/score_batch/pallas_call | solution.py:303
  22.8 0.0 collective-permute-start.7
  22.8 0.0 copy-done.1
  22.8 0.9 %score_batch.3.own_batch = f32[8,128]{1,0:T(8,128)S(1)} custom-call(bf16[1,8,32,128]{3,2,1,0:T(8,128)(2,1)S(1)} %copy-done.1, bf16[1,8,128,128]{3,2,1,0:T(8,128)(2,1)S(1)} %copy-done, bf16[1,8,128,128]{3,2,1,0:T(8,128)(2,1)S(1)} %collective-permute-done.4.refs_1_, bf16[1,8,128,128]{3,2,1,0:T(8,128)(2,1)S(1)} %collective-permute-done.5.refs_2_, ...), custom_call_target="tpu_custom_call" | custom-call | flops 268435456 | bytes 1048576 | tf_op jit(solution)/shard_map/score_batch/pallas_call | solution.py:303
  23.7 0.0 collective-permute-done.8.refs_1_
  23.7 1.1 %collective-permute-done.9.refs_2_ = f32[8,128]{1,0:T(8,128)S(1)} collective-permute-done((f32[8,128]{1,0:T(8,128)S(1)}, f32[8,128]{1,0:T(8,128)S(1)}, u32[]{:S(2)}, u32[]{:S(2)}) %collective-permute-start.9) | collective-permute-done | bytes 4128 | tf_op jit(solution)/shard_map/ppermute | solution.py:383
  24.8 0.0 collective-permute-done.10.refs_3_
  24.8 0.0 collective-permute-done.7.mate_batch
  24.8 0.8 %finish.1 = (f32[1,8,64]{2,1,0:T(8,128)}, f32[1,8,64]{2,1,0:T(8,128)}, f32[1,8]{1,0:T(1,128)}) custom-call(f32[8,128]{1,0:T(8,128)S(1)} %score_batch.3.own_batch, f32[8,128]{1,0:T(8,128)S(1)} %collective-permute-done.7.mate_batch, f32[8,128]{1,0:T(8,128)S(1)} %get-tuple-element.12.refs_0_, f32[8,128]{1,0:T(8,128)S(1)} %collective-permute-done.8.refs_1_, ...), custom_call_target="tpu_custom_call" | custom-call | tf_op jit(solution)/shard_map/finish/pallas_call | solution.py:363
  (3 shorter events, 0.0 us)
Async XLA Ops:
  1.5 20.5 %copy-start = (bf16[1,8,128,128]{3,2,1,0:T(8,128)(2,1)S(1)}, bf16[1,8,128,128]{3,2,1,0:T(8,128)(2,1)}, u32[]{:S(2)}) copy-start(bf16[1,8,128,128]{3,2,1,0:T(8,128)(2,1)} %refs_0_.3) | copy-start | bytes 786436
  1.5 21.3 %copy-start.1 = (bf16[1,8,32,128]{3,2,1,0:T(8,128)(2,1)S(1)}, bf16[1,8,32,128]{3,2,1,0:T(8,128)(2,1)}, u32[]{:S(2)}) copy-start(bf16[1,8,32,128]{3,2,1,0:T(8,128)(2,1)} %query_ref.2) | copy-start | bytes 196612
  1.5 23.3 %copy-start.2 = (s32[1,8,64]{2,1,0:T(8,128)S(1)}, s32[1,8,64]{2,1,0:T(8,128)}, u32[]{:S(2)}) copy-start(s32[1,8,64]{2,1,0:T(8,128)} %refs_4_.3) | copy-start | bytes 6148
  1.5 23.3 %copy-start.3 = (s32[1,8]{1,0:T(1,128)S(1)}, s32[1,8]{1,0:T(1,128)}, u32[]{:S(2)}) copy-start(s32[1,8]{1,0:T(1,128)} %refs_5_.1) | copy-start | bytes 100
  1.6 8.9 %collective-permute-start.3 = (bf16[272,128]{1,0:T(8,128)(2,1)S(1)}, bf16[272,128]{1,0:T(8,128)(2,1)S(1)}, u32[]{:S(2)}, u32[]{:S(2)}) collective-permute-start(bf16[272,128]{1,0:T(8,128)(2,1)S(1)} %pack.1.refs_0_), channel_id=1, source_target_pairs={{0,24},{8,16},{16,8},{24,0},{1,25},{9,17},{17,9},{25,1},{2,26},{10... | collective-permute-start | bytes 208904 | tf_op jit(solution)/shard_map/ppermute | solution.py:383
  6.7 5.9 %collective-permute-start.2 = (bf16[272,128]{1,0:T(8,128)(2,1)S(1)}, bf16[272,128]{1,0:T(8,128)(2,1)S(1)}, u32[]{:S(2)}, u32[]{:S(2)}) collective-permute-start(bf16[272,128]{1,0:T(8,128)(2,1)S(1)} %pack.1.refs_0_), channel_id=1, source_target_pairs={{0,16},{8,24},{16,0},{24,8},{1,17},{9,25},{17,1},{25,9},{2,18},{10... | collective-permute-start | bytes 208904 | tf_op jit(solution)/shard_map/ppermute | solution.py:383
  6.7 5.9 %collective-permute-start.1 = (bf16[272,128]{1,0:T(8,128)(2,1)S(1)}, bf16[272,128]{1,0:T(8,128)(2,1)S(1)}, u32[]{:S(2)}, u32[]{:S(2)}) collective-permute-start(bf16[272,128]{1,0:T(8,128)(2,1)S(1)} %pack.1.refs_0_), channel_id=1, source_target_pairs={{0,8},{8,0},{16,24},{24,16},{1,9},{9,1},{17,25},{25,17},{2,10},{10... | collective-permute-start | bytes 208904 | tf_op jit(solution)/shard_map/ppermute | solution.py:383
  7.3 13.0 %collective-permute-start.6 = (bf16[1,8,128,128]{3,2,1,0:T(8,128)(2,1)}, bf16[1,8,128,128]{3,2,1,0:T(8,128)(2,1)S(1)}, u32[]{:S(2)}, u32[]{:S(2)}) collective-permute-start(bf16[1,8,128,128]{3,2,1,0:T(8,128)(2,1)} %refs_0_.3), channel_id=1, source_target_pairs={{0,6},{1,7},{2,4},{3,5},{4,2},{5,3},{6,0},{7,1},{8,14},{9,15},{10,... | collective-permute-start | bytes 786440 | tf_op jit(solution)/shard_map/ppermute | solution.py:386
  9.9 12.1 %collective-permute-start.5 = (bf16[1,8,128,128]{3,2,1,0:T(8,128)(2,1)}, bf16[1,8,128,128]{3,2,1,0:T(8,128)(2,1)S(1)}, u32[]{:S(2)}, u32[]{:S(2)}) collective-permute-start(bf16[1,8,128,128]{3,2,1,0:T(8,128)(2,1)} %refs_0_.3), channel_id=1, source_target_pairs={{0,4},{1,5},{2,6},{3,7},{4,0},{5,1},{6,2},{7,3},{8,12},{9,13},{10,... | collective-permute-start | bytes 786440 | tf_op jit(solution)/shard_map/ppermute | solution.py:386
  10.4 11.6 %collective-permute-start.4 = (bf16[1,8,128,128]{3,2,1,0:T(8,128)(2,1)}, bf16[1,8,128,128]{3,2,1,0:T(8,128)(2,1)S(1)}, u32[]{:S(2)}, u32[]{:S(2)}) collective-permute-start(bf16[1,8,128,128]{3,2,1,0:T(8,128)(2,1)} %refs_0_.3), channel_id=1, source_target_pairs={{0,2},{1,3},{2,0},{3,1},{4,6},{5,7},{6,4},{7,5},{8,10},{9,11},{10,... | collective-permute-start | bytes 786440 | tf_op jit(solution)/shard_map/ppermute | solution.py:386
  12.6 4.9 %collective-permute-start = (bf16[1,8,32,128]{3,2,1,0:T(8,128)(2,1)}, bf16[1,8,32,128]{3,2,1,0:T(8,128)(2,1)S(1)}, u32[]{:S(2)}, u32[]{:S(2)}) collective-permute-start(bf16[1,8,32,128]{3,2,1,0:T(8,128)(2,1)} %query_ref.2), channel_id=1, source_target_pairs={{0,1},{1,0},{2,3},{3,2},{4,5},{5,4},{6,7},{7,6},{8,9},{9,8},{10,11... | collective-permute-start | bytes 196616 | tf_op jit(solution)/shard_map/ppermute | solution.py:386
  17.5 6.2 %collective-permute-start.8 = (f32[8,128]{1,0:T(8,128)S(1)}, f32[8,128]{1,0:T(8,128)S(1)}, u32[]{:S(2)}, u32[]{:S(2)}) collective-permute-start(f32[8,128]{1,0:T(8,128)S(1)} %get-tuple-element.16), channel_id=1, source_target_pairs={{0,24},{8,16},{16,8},{24,0},{1,25},{9,17},{17,9},{25,1},{2,26},{10... | collective-permute-start | bytes 12296 | tf_op jit(solution)/shard_map/ppermute | solution.py:383
  20.3 4.5 %collective-permute-start.9 = (f32[8,128]{1,0:T(8,128)S(1)}, f32[8,128]{1,0:T(8,128)S(1)}, u32[]{:S(2)}, u32[]{:S(2)}) collective-permute-start(f32[8,128]{1,0:T(8,128)S(1)} %get-tuple-element.17), channel_id=1, source_target_pairs={{0,16},{8,24},{16,0},{24,8},{1,17},{9,25},{17,1},{25,9},{2,18},{10... | collective-permute-start | bytes 12296 | tf_op jit(solution)/shard_map/ppermute | solution.py:383
  20.3 4.5 %collective-permute-start.10 = (f32[8,128]{1,0:T(8,128)S(1)}, f32[8,128]{1,0:T(8,128)S(1)}, u32[]{:S(2)}, u32[]{:S(2)}) collective-permute-start(f32[8,128]{1,0:T(8,128)S(1)} %get-tuple-element.18), channel_id=1, source_target_pairs={{0,8},{8,0},{16,24},{24,16},{1,9},{9,1},{17,25},{25,17},{2,10},{10... | collective-permute-start | bytes 12296 | tf_op jit(solution)/shard_map/ppermute | solution.py:383
  22.8 2.0 %collective-permute-start.7 = (f32[8,128]{1,0:T(8,128)S(1)}, f32[8,128]{1,0:T(8,128)S(1)}, u32[]{:S(2)}, u32[]{:S(2)}) collective-permute-start(f32[8,128]{1,0:T(8,128)S(1)} %score_batch.2), channel_id=1, source_target_pairs={{0,1},{1,0},{2,3},{3,2},{4,5},{5,4},{6,7},{7,6},{8,9},{9,8},{10,11... | collective-permute-start | bytes 12296 | tf_op jit(solution)/shard_map/ppermute | solution.py:386

commit v3 on v0

--- a/solution.py
+++ b/solution.py
@@ -10,8 +10,8 @@
 LANES = 128
 MIB = 1024 * 1024
 SLOTS = 8
+LOW = 256
 CHUNK = 32
-LIST_ROWS = 16
 
 
 def in_hbm(array):
@@ -34,12 +34,15 @@
     per_query = tokens // queries
     row = lax.broadcasted_iota(jnp.int32, (queries, tokens), 0)
     col = lax.broadcasted_iota(jnp.int32, (queries, tokens), 1)
-    own = (col // per_query == row).astype(jnp.float32)
+    own = (col // per_query == row).astype(jnp.bfloat16)
+    high = best.astype(jnp.bfloat16)
+    rest = best - high.astype(jnp.float32)
+    middle = rest.astype(jnp.bfloat16)
+    low = (rest - middle.astype(jnp.float32)).astype(jnp.bfloat16)
     return lax.dot_general(
-        own,
-        best,
+        jnp.concatenate([own] * 3, axis=1),
+        jnp.concatenate([high, middle, low], axis=1),
         (((1,), (1,)), ((), ())),
-        precision=lax.Precision.HIGHEST,
         preferred_element_type=jnp.float32,
     )
 
@@ -157,27 +160,28 @@
             jnp.sum(jnp.where(rank == float(slot), asker, 0.0), axis=0, keepdims=True)
             for slot in range(SLOTS)
         ]
-        rest = jnp.zeros((LIST_ROWS - SLOTS - len(extra), p_count), jnp.float32)
-        list_ref[...] = jnp.concatenate(rows + extra + [rest], axis=0).astype(jnp.int32)
+        for slot, above in enumerate(extra):
+            rows[slot] = rows[slot] + LOW * above
+        list_ref[...] = jnp.concatenate(rows, axis=0).astype(jnp.int32)
         copy = pltpu.make_async_copy(list_ref, scalar_ref, list_sem)
         copy.start()
         copy.wait()
 
     def unit(index):
-        tokens = [query_ref[scalar_ref[slot, index]] for slot in range(SLOTS)]
+        tokens = [query_ref[scalar_ref[slot, index] & (LOW - 1)] for slot in range(SLOTS)]
         return token_max(passage_ref[pl.ds(index, 1)], jnp.concatenate(tokens, axis=0))
 
-    def add_scores(first):
+    def add_scores(first, scores):
         sums = token_sum(best_ref[...], SLOTS)
         for index, out_ref in enumerate(out_refs):
             rank = rank_ref[index * q_count : (index + 1) * q_count] - first
+            total_scores = scores[index]
             for slot in range(SLOTS):
-                out_ref[...] = jnp.where(rank == float(slot), sums[slot : slot + 1], out_ref[...])
-
-    for out_ref in out_refs:
-        out_ref[...] = jnp.zeros_like(out_ref)
+                total_scores = jnp.where(rank == float(slot), sums[slot : slot + 1], total_scores)
+            out_ref[...] = total_scores
+
     write_list(0.0, [most])
-    rounds = (scalar_ref[SLOTS, 0] + SLOTS - 1) // SLOTS
+    rounds = (scalar_ref[0, 0] // LOW + SLOTS - 1) // SLOTS
 
     @pl.loop(0, chunks)
     def _(chunk):
@@ -187,19 +191,19 @@
             rows = [unit(first + offset) for offset in range(8)]
             best_ref[pl.ds(first, 8), :] = jnp.concatenate(rows, axis=0)
 
-    add_scores(0.0)
+    add_scores(0.0, [jnp.zeros((q_count, p_count), jnp.float32)] * shards)
 
     @pl.loop(1, rounds)
     def _(turn):
         done = (turn * SLOTS).astype(jnp.float32)
         write_list(done, left_over(done))
 
-        @pl.loop(0, scalar_ref[SLOTS + 1, 0])
+        @pl.loop(0, scalar_ref[1, 0] // LOW)
         def _(place):
-            index = scalar_ref[SLOTS, place]
+            index = scalar_ref[0, place] // LOW
             best_ref[pl.ds(index, 1), :] = unit(index)
 
-        add_scores(done)
+        add_scores(done, [out_ref[...] for out_ref in out_refs])
 
 
 def score_memory(packed, memory, q_count, slots):
@@ -218,8 +222,8 @@
             pltpu.VMEM((total, q_tokens, depth), memory.dtype),
             pltpu.VMEM((total, p_count), jnp.float32),
             pltpu.VMEM((p_count, SLOTS * q_tokens), jnp.float32),
-            pltpu.VMEM((LIST_ROWS, p_count), jnp.int32),
-            pltpu.SMEM((LIST_ROWS, p_count), jnp.int32),
+            pltpu.VMEM((SLOTS, p_count), jnp.int32),
+            pltpu.SMEM((SLOTS, p_count), jnp.int32),
             pltpu.SemaphoreType.DMA((p_count // CHUNK,)),
             pltpu.SemaphoreType.DMA,
         ],
@@ -237,12 +241,12 @@
     passage_refs, (out_ref, best_ref) = refs[:-2], refs[-2:]
     _, queries, q_tokens, depth = query_ref.shape
     count = passage_refs[0].shape[1]
-    if len(passage_refs) * count < best_ref.shape[0]:
-        best_ref[...] = jnp.zeros_like(best_ref)
     tokens = query_ref[0].reshape(queries * q_tokens, depth)
     for chip, passage_ref in enumerate(passage_refs):
         best_ref[chip * count : (chip + 1) * count, :] = token_max(passage_ref[0], tokens)
-    out_ref[...] = token_sum(best_ref[...], queries)
+    sums = token_sum(best_ref[...], queries)
+    empty = jnp.zeros((queries, out_ref.shape[1] - sums.shape[1]), jnp.float32)
+    out_ref[...] = jnp.concatenate([sums, empty], axis=1) if empty.size else sums
 
 
 def score_batch(queries, positives):
@@ -253,7 +257,7 @@
     return pl.pallas_call(
         batch_kernel,
         out_shape=jax.ShapeDtypeStruct((q_count, lanes), jnp.float32),
-        scratch_shapes=[pltpu.VMEM((lanes, q_count * q_tokens), jnp.float32)],
+        scratch_shapes=[pltpu.VMEM((chips * p_count, q_count * q_tokens), jnp.float32)],
         compiler_params=pltpu.CompilerParams(vmem_limit_bytes=16 * MIB),
         cost_estimate=pl.CostEstimate(
             flops=2 * chips * q_count * q_tokens * p_count * p_tokens * depth,

time: 25.3 us -> 25.3 us (level)
  transfers between devices with their start and end apart: 11 -> 11, of which waited for: 3 -> 4; matrix products, arithmetic and copies ran while one was open for 0% -> 0% of each run, Pallas kernels for 24% -> 24%
where the time goes in v3:
time: 25.3 us; the launch traced here: 25.1 us
  starting transfers between devices  14.1 us (56%)
  Pallas kernels  7.75 us (31%)
  waiting for transfers between devices  2.55 us (10%)
  between operations  0.72 us (3%)
    ppermute x6, starting transfers between devices, to_shard(): return lax.ppermute(array, 'memory', [(i, i ^ step) for i in range(shards)])  10.2 us
    pallas_call x1, Pallas kernels, score_memory(): pl.pallas_call(functools.partial(memory_kernel, shards, slots), in_specs=...  4.41 us
    ppermute x5, starting transfers between devices, to_group(): return lax.ppermute(array, 'group', [(i, i ^ step) for i in range(groups)])  3.88 us
    ppermute x6, waiting for transfers between devices, to_shard(): return lax.ppermute(array, 'memory', [(i, i ^ step) for i in range(shards)])  2.39 us
    pallas_call x2, Pallas kernels, score_batch(): pl.pallas_call(batch_kernel, out_shape=jax.ShapeDtypeStruct((q_count, lan...  1.66 us
    pallas_call x1, Pallas kernels, pack(): pl.pallas_call(functools.partial(pack_kernel, p_count), in_specs=[vmem, v...  0.87 us
    pallas_call x1, Pallas kernels, finish(): pl.pallas_call(functools.partial(loss_kernel, len(memory_parts)), out_sha...  0.8 us
  transfers between devices with their start and end apart: 11, of which 4 were waited for; matrix products, arithmetic and copies ran while one was open for 0% of the time, Pallas kernels for 24%

profile of v3, /device:TPU:0, one launch (start us, length us, event | category | flops | bytes accessed | tf_op | source)
XLA Modules:
  0.0 25.1 jit_solution(3316746323751209379)
XLA Ops:
  0.6 0.9 %pack.1.refs_0_ = bf16[272,128]{1,0:T(8,128)(2,1)S(1)} custom-call(bf16[1,8,32,128]{3,2,1,0:T(8,128)(2,1)} %query_ref.2, s32[1,8,64]{2,1,0:T(8,128)} %refs_4_.3, s32[1,8]{1,0:T(1,128)} %refs_5_.1), custom_call_target="tpu_custom_call" | custom-call | tf_op jit(solution)/shard_map/pack/pallas_call | solution.py:92
  1.5 0.0 copy-start
  1.5 0.0 copy-start.1
  1.5 0.0 copy-start.2
  1.5 0.0 copy-start.3
  1.6 5.1 %collective-permute-start.3 = (bf16[272,128]{1,0:T(8,128)(2,1)S(1)}, bf16[272,128]{1,0:T(8,128)(2,1)S(1)}, u32[]{:S(2)}, u32[]{:S(2)}) collective-permute-start(bf16[272,128]{1,0:T(8,128)(2,1)S(1)} %pack.1.refs_0_), channel_id=1, source_target_pairs={{0,24},{8,16},{16,8},{24,0},{1,25},{9,17},{17,9},{25,1},{2,26},{10... | collective-permute-start | bytes 208904 | tf_op jit(solution)/shard_map/ppermute | solution.py:337
  6.7 0.0 collective-permute-start.2
  6.7 0.6 %collective-permute-start.1 = (bf16[272,128]{1,0:T(8,128)(2,1)S(1)}, bf16[272,128]{1,0:T(8,128)(2,1)S(1)}, u32[]{:S(2)}, u32[]{:S(2)}) collective-permute-start(bf16[272,128]{1,0:T(8,128)(2,1)S(1)} %pack.1.refs_0_), channel_id=1, source_target_pairs={{0,8},{8,0},{16,24},{24,16},{1,9},{9,1},{17,25},{25,17},{2,10},{10... | collective-permute-start | bytes 208904 | tf_op jit(solution)/shard_map/ppermute | solution.py:337
  7.3 2.6 %collective-permute-start.6 = (bf16[1,8,128,128]{3,2,1,0:T(8,128)(2,1)}, bf16[1,8,128,128]{3,2,1,0:T(8,128)(2,1)S(1)}, u32[]{:S(2)}, u32[]{:S(2)}) collective-permute-start(bf16[1,8,128,128]{3,2,1,0:T(8,128)(2,1)} %refs_0_.3), channel_id=1, source_target_pairs={{0,6},{1,7},{2,4},{3,5},{4,2},{5,3},{6,0},{7,1},{8,14},{9,15},{10,... | collective-permute-start | bytes 786440 | tf_op jit(solution)/shard_map/ppermute | solution.py:340
  9.9 0.5 %collective-permute-start.5 = (bf16[1,8,128,128]{3,2,1,0:T(8,128)(2,1)}, bf16[1,8,128,128]{3,2,1,0:T(8,128)(2,1)S(1)}, u32[]{:S(2)}, u32[]{:S(2)}) collective-permute-start(bf16[1,8,128,128]{3,2,1,0:T(8,128)(2,1)} %refs_0_.3), channel_id=1, source_target_pairs={{0,4},{1,5},{2,6},{3,7},{4,0},{5,1},{6,2},{7,3},{8,12},{9,13},{10,... | collective-permute-start | bytes 786440 | tf_op jit(solution)/shard_map/ppermute | solution.py:340
  10.4 0.0 collective-permute-done.3.refs_3_
  10.4 0.8 %collective-permute-start.4 = (bf16[1,8,128,128]{3,2,1,0:T(8,128)(2,1)}, bf16[1,8,128,128]{3,2,1,0:T(8,128)(2,1)S(1)}, u32[]{:S(2)}, u32[]{:S(2)}) collective-permute-start(bf16[1,8,128,128]{3,2,1,0:T(8,128)(2,1)} %refs_0_.3), channel_id=1, source_target_pairs={{0,2},{1,3},{2,0},{3,1},{4,6},{5,7},{6,4},{7,5},{8,10},{9,11},{10,... | collective-permute-start | bytes 786440 | tf_op jit(solution)/shard_map/ppermute | solution.py:340
  11.2 1.4 %collective-permute-done.2.refs_2_ = bf16[272,128]{1,0:T(8,128)(2,1)S(1)} collective-permute-done((bf16[272,128]{1,0:T(8,128)(2,1)S(1)}, bf16[272,128]{1,0:T(8,128)(2,1)S(1)}, u32[]{:S(2)}, u32[]{:S(2)}) %collective-permute-start.2) | collective-permute-done | bytes 69664 | tf_op jit(solution)/shard_map/ppermute | solution.py:337
  12.6 0.0 collective-permute-start
  12.6 0.0 collective-permute-done.1.refs_1_
  12.6 4.4 %score_memory.1 = (f32[8,128]{1,0:T(8,128)S(1)}, f32[8,128]{1,0:T(8,128)S(1)}, f32[8,128]{1,0:T(8,128)S(1)}, f32[8,128]{1,0:T(8,128)S(1)}) custom-call(bf16[272,128]{1,0:T(8,128)(2,1)S(1)} %pack.1.refs_0_, bf16[272,128]{1,0:T(8,128)(2,1)S(1)} %collective-permute-done.1.refs_1_, bf16[272,128]{1,0:T(8,128)(2,1)S(1)} %collective-permute-done.2.refs_2_, ...), custom_call_target="tpu_custom_call" | custom-call | flops 4294967296 | bytes 4194304 | tf_op jit(solution)/shard_map/score_memory/pallas_call | solution.py:215
  17.0 0.0 collective-permute-done.query_ref
  17.0 2.8 %collective-permute-start.8 = (f32[8,128]{1,0:T(8,128)S(1)}, f32[8,128]{1,0:T(8,128)S(1)}, u32[]{:S(2)}, u32[]{:S(2)}) collective-permute-start(f32[8,128]{1,0:T(8,128)S(1)} %get-tuple-element.16), channel_id=1, source_target_pairs={{0,24},{8,16},{16,8},{24,0},{1,25},{9,17},{17,9},{25,1},{2,26},{10... | collective-permute-start | bytes 12296 | tf_op jit(solution)/shard_map/ppermute | solution.py:337
  19.8 0.0 collective-permute-start.9
  19.8 0.0 collective-permute-done.6.refs_3_
  19.8 1.7 %collective-permute-start.10 = (f32[8,128]{1,0:T(8,128)S(1)}, f32[8,128]{1,0:T(8,128)S(1)}, u32[]{:S(2)}, u32[]{:S(2)}) collective-permute-start(f32[8,128]{1,0:T(8,128)S(1)} %get-tuple-element.18), channel_id=1, source_target_pairs={{0,8},{8,0},{16,24},{24,16},{1,9},{9,1},{17,25},{25,17},{2,10},{10... | collective-permute-start | bytes 12296 | tf_op jit(solution)/shard_map/ppermute | solution.py:337
  21.5 0.1 collective-permute-done.5.refs_2_
  21.5 0.1 collective-permute-done.4.refs_1_
  21.6 0.8 %score_batch.2 = f32[8,128]{1,0:T(8,128)S(1)} custom-call(bf16[1,8,32,128]{3,2,1,0:T(8,128)(2,1)S(1)} %collective-permute-done.query_ref, bf16[1,8,128,128]{3,2,1,0:T(8,128)(2,1)S(1)} %copy-done, bf16[1,8,128,128]{3,2,1,0:T(8,128)(2,1)S(1)} %collective-permute-done.4.refs_1_, bf16[1,8,128,128]{3,2,1,0:T(8,128)(2,1)S(1)} %collective-permute-done.5.refs_2_, ...), custom_call_target="tpu_custom_call" | custom-call | flops 268435456 | bytes 1048576 | tf_op jit(solution)/shard_map/score_batch/pallas_call | solution.py:257
  22.5 0.0 collective-permute-start.7
  22.5 0.0 copy-done.1
  22.5 0.8 %score_batch.3.own_batch = f32[8,128]{1,0:T(8,128)S(1)} custom-call(bf16[1,8,32,128]{3,2,1,0:T(8,128)(2,1)S(1)} %copy-done.1, bf16[1,8,128,128]{3,2,1,0:T(8,128)(2,1)S(1)} %copy-done, bf16[1,8,128,128]{3,2,1,0:T(8,128)(2,1)S(1)} %collective-permute-done.4.refs_1_, bf16[1,8,128,128]{3,2,1,0:T(8,128)(2,1)S(1)} %collective-permute-done.5.refs_2_, ...), custom_call_target="tpu_custom_call" | custom-call | flops 268435456 | bytes 1048576 | tf_op jit(solution)/shard_map/score_batch/pallas_call | solution.py:257
  23.3 0.0 collective-permute-done.8.refs_1_
  23.3 1.0 %collective-permute-done.9.refs_2_ = f32[8,128]{1,0:T(8,128)S(1)} collective-permute-done((f32[8,128]{1,0:T(8,128)S(1)}, f32[8,128]{1,0:T(8,128)S(1)}, u32[]{:S(2)}, u32[]{:S(2)}) %collective-permute-start.9) | collective-permute-done | bytes 4128 | tf_op jit(solution)/shard_map/ppermute | solution.py:337
  24.3 0.0 collective-permute-done.10.refs_3_
  24.3 0.0 collective-permute-done.7.mate_batch
  24.3 0.8 %finish.1 = (f32[1,8,64]{2,1,0:T(8,128)}, f32[1,8,64]{2,1,0:T(8,128)}, f32[1,8]{1,0:T(1,128)}) custom-call(f32[8,128]{1,0:T(8,128)S(1)} %score_batch.3.own_batch, f32[8,128]{1,0:T(8,128)S(1)} %collective-permute-done.7.mate_batch, f32[8,128]{1,0:T(8,128)S(1)} %get-tuple-element.12.refs_0_, f32[8,128]{1,0:T(8,128)S(1)} %collective-permute-done.8.refs_1_, ...), custom_call_target="tpu_custom_call" | custom-call | tf_op jit(solution)/shard_map/finish/pallas_call | solution.py:317
  (3 shorter events, 0.0 us)
Async XLA Ops:
  1.5 20.1 %copy-start = (bf16[1,8,128,128]{3,2,1,0:T(8,128)(2,1)S(1)}, bf16[1,8,128,128]{3,2,1,0:T(8,128)(2,1)}, u32[]{:S(2)}) copy-start(bf16[1,8,128,128]{3,2,1,0:T(8,128)(2,1)} %refs_0_.3) | copy-start | bytes 786436
  1.5 21.0 %copy-start.1 = (bf16[1,8,32,128]{3,2,1,0:T(8,128)(2,1)S(1)}, bf16[1,8,32,128]{3,2,1,0:T(8,128)(2,1)}, u32[]{:S(2)}) copy-start(bf16[1,8,32,128]{3,2,1,0:T(8,128)(2,1)} %query_ref.2) | copy-start | bytes 196612
  1.5 22.8 %copy-start.2 = (s32[1,8,64]{2,1,0:T(8,128)S(1)}, s32[1,8,64]{2,1,0:T(8,128)}, u32[]{:S(2)}) copy-start(s32[1,8,64]{2,1,0:T(8,128)} %refs_4_.3) | copy-start | bytes 6148
  1.5 22.8 %copy-start.3 = (s32[1,8]{1,0:T(1,128)S(1)}, s32[1,8]{1,0:T(1,128)}, u32[]{:S(2)}) copy-start(s32[1,8]{1,0:T(1,128)} %refs_5_.1) | copy-start | bytes 100
  1.6 8.9 %collective-permute-start.3 = (bf16[272,128]{1,0:T(8,128)(2,1)S(1)}, bf16[272,128]{1,0:T(8,128)(2,1)S(1)}, u32[]{:S(2)}, u32[]{:S(2)}) collective-permute-start(bf16[272,128]{1,0:T(8,128)(2,1)S(1)} %pack.1.refs_0_), channel_id=1, source_target_pairs={{0,24},{8,16},{16,8},{24,0},{1,25},{9,17},{17,9},{25,1},{2,26},{10... | collective-permute-start | bytes 208904 | tf_op jit(solution)/shard_map/ppermute | solution.py:337
  6.7 5.9 %collective-permute-start.2 = (bf16[272,128]{1,0:T(8,128)(2,1)S(1)}, bf16[272,128]{1,0:T(8,128)(2,1)S(1)}, u32[]{:S(2)}, u32[]{:S(2)}) collective-permute-start(bf16[272,128]{1,0:T(8,128)(2,1)S(1)} %pack.1.refs_0_), channel_id=1, source_target_pairs={{0,16},{8,24},{16,0},{24,8},{1,17},{9,25},{17,1},{25,9},{2,18},{10... | collective-permute-start | bytes 208904 | tf_op jit(solution)/shard_map/ppermute | solution.py:337
  6.7 5.9 %collective-permute-start.1 = (bf16[272,128]{1,0:T(8,128)(2,1)S(1)}, bf16[272,128]{1,0:T(8,128)(2,1)S(1)}, u32[]{:S(2)}, u32[]{:S(2)}) collective-permute-start(bf16[272,128]{1,0:T(8,128)(2,1)S(1)} %pack.1.refs_0_), channel_id=1, source_target_pairs={{0,8},{8,0},{16,24},{24,16},{1,9},{9,1},{17,25},{25,17},{2,10},{10... | collective-permute-start | bytes 208904 | tf_op jit(solution)/shard_map/ppermute | solution.py:337
  7.3 12.5 %collective-permute-start.6 = (bf16[1,8,128,128]{3,2,1,0:T(8,128)(2,1)}, bf16[1,8,128,128]{3,2,1,0:T(8,128)(2,1)S(1)}, u32[]{:S(2)}, u32[]{:S(2)}) collective-permute-start(bf16[1,8,128,128]{3,2,1,0:T(8,128)(2,1)} %refs_0_.3), channel_id=1, source_target_pairs={{0,6},{1,7},{2,4},{3,5},{4,2},{5,3},{6,0},{7,1},{8,14},{9,15},{10,... | collective-permute-start | bytes 786440 | tf_op jit(solution)/shard_map/ppermute | solution.py:340
  9.9 11.6 %collective-permute-start.5 = (bf16[1,8,128,128]{3,2,1,0:T(8,128)(2,1)}, bf16[1,8,128,128]{3,2,1,0:T(8,128)(2,1)S(1)}, u32[]{:S(2)}, u32[]{:S(2)}) collective-permute-start(bf16[1,8,128,128]{3,2,1,0:T(8,128)(2,1)} %refs_0_.3), channel_id=1, source_target_pairs={{0,4},{1,5},{2,6},{3,7},{4,0},{5,1},{6,2},{7,3},{8,12},{9,13},{10,... | collective-permute-start | bytes 786440 | tf_op jit(solution)/shard_map/ppermute | solution.py:340
  10.4 11.2 %collective-permute-start.4 = (bf16[1,8,128,128]{3,2,1,0:T(8,128)(2,1)}, bf16[1,8,128,128]{3,2,1,0:T(8,128)(2,1)S(1)}, u32[]{:S(2)}, u32[]{:S(2)}) collective-permute-start(bf16[1,8,128,128]{3,2,1,0:T(8,128)(2,1)} %refs_0_.3), channel_id=1, source_target_pairs={{0,2},{1,3},{2,0},{3,1},{4,6},{5,7},{6,4},{7,5},{8,10},{9,11},{10,... | collective-permute-start | bytes 786440 | tf_op jit(solution)/shard_map/ppermute | solution.py:340
  12.6 4.4 %collective-permute-start = (bf16[1,8,32,128]{3,2,1,0:T(8,128)(2,1)}, bf16[1,8,32,128]{3,2,1,0:T(8,128)(2,1)S(1)}, u32[]{:S(2)}, u32[]{:S(2)}) collective-permute-start(bf16[1,8,32,128]{3,2,1,0:T(8,128)(2,1)} %query_ref.2), channel_id=1, source_target_pairs={{0,1},{1,0},{2,3},{3,2},{4,5},{5,4},{6,7},{7,6},{8,9},{9,8},{10,11... | collective-permute-start | bytes 196616 | tf_op jit(solution)/shard_map/ppermute | solution.py:340
  17.0 6.3 %collective-permute-start.8 = (f32[8,128]{1,0:T(8,128)S(1)}, f32[8,128]{1,0:T(8,128)S(1)}, u32[]{:S(2)}, u32[]{:S(2)}) collective-permute-start(f32[8,128]{1,0:T(8,128)S(1)} %get-tuple-element.16), channel_id=1, source_target_pairs={{0,24},{8,16},{16,8},{24,0},{1,25},{9,17},{17,9},{25,1},{2,26},{10... | collective-permute-start | bytes 12296 | tf_op jit(solution)/shard_map/ppermute | solution.py:337
  19.8 4.5 %collective-permute-start.9 = (f32[8,128]{1,0:T(8,128)S(1)}, f32[8,128]{1,0:T(8,128)S(1)}, u32[]{:S(2)}, u32[]{:S(2)}) collective-permute-start(f32[8,128]{1,0:T(8,128)S(1)} %get-tuple-element.17), channel_id=1, source_target_pairs={{0,16},{8,24},{16,0},{24,8},{1,17},{9,25},{17,1},{25,9},{2,18},{10... | collective-permute-start | bytes 12296 | tf_op jit(solution)/shard_map/ppermute | solution.py:337
  19.8 4.5 %collective-permute-start.10 = (f32[8,128]{1,0:T(8,128)S(1)}, f32[8,128]{1,0:T(8,128)S(1)}, u32[]{:S(2)}, u32[]{:S(2)}) collective-permute-start(f32[8,128]{1,0:T(8,128)S(1)} %get-tuple-element.18), channel_id=1, source_target_pairs={{0,8},{8,0},{16,24},{24,16},{1,9},{9,1},{17,25},{25,17},{2,10},{10... | collective-permute-start | bytes 12296 | tf_op jit(solution)/shard_map/ppermute | solution.py:337
  22.5 1.9 %collective-permute-start.7 = (f32[8,128]{1,0:T(8,128)S(1)}, f32[8,128]{1,0:T(8,128)S(1)}, u32[]{:S(2)}, u32[]{:S(2)}) collective-permute-start(f32[8,128]{1,0:T(8,128)S(1)} %score_batch.2), channel_id=1, source_target_pairs={{0,1},{1,0},{2,3},{3,2},{4,5},{5,4},{6,7},{7,6},{8,9},{9,8},{10,11... | collective-permute-start | bytes 12296 | tf_op jit(solution)/shard_map/ppermute | solution.py:340

commit v4 on v3

--- a/solution.py
+++ b/solution.py
@@ -11,6 +11,8 @@
 MIB = 1024 * 1024
 SLOTS = 8
 LOW = 256
+PACK_FLOPS = 10**10
+PACK_BYTES = 2**24
 CHUNK = 32
 
 
@@ -94,29 +96,21 @@
         in_specs=[vmem, vmem, pl.BlockSpec(memory_space=pltpu.SMEM)],
         out_shape=jax.ShapeDtypeStruct((q_count * (q_tokens + 2), depth), queries.dtype),
         compiler_params=pltpu.CompilerParams(vmem_limit_bytes=4 * MIB),
+        cost_estimate=pl.CostEstimate(
+            flops=PACK_FLOPS, bytes_accessed=PACK_BYTES, transcendentals=0
+        ),
         name="pack",
     )(in_hbm(queries), in_hbm(candidates), in_hbm(counts))
 
 
 def memory_kernel(shards, slots, *refs):
-    packed_refs, memory_ref = refs[:shards], refs[shards]
+    packed_refs, passage_ref = refs[:shards], refs[shards].at[0]
     out_refs = refs[shards + 1 : 2 * shards + 1]
-    passage_ref, query_ref, rank_ref, best_ref, list_ref, scalar_ref, copy_sems, list_sem = refs[
-        2 * shards + 1 :
-    ]
+    query_ref, rank_ref, best_ref, list_ref, scalar_ref, list_sem = refs[2 * shards + 1 :]
     q_count = out_refs[0].shape[0]
     p_count = passage_ref.shape[0]
     total, q_tokens, depth = query_ref.shape
     chunks = p_count // CHUNK
-
-    def fetch(chunk):
-        rows = pl.ds(pl.multiple_of(chunk * CHUNK, CHUNK), CHUNK)
-        return pltpu.make_async_copy(
-            memory_ref.at[0, rows], passage_ref.at[rows], copy_sems.at[chunk]
-        )
-
-    for chunk in range(chunks):
-        fetch(chunk).start()
 
     me = lax.axis_index("memory").astype(jnp.float32)
     keys = []
@@ -185,7 +179,6 @@
 
     @pl.loop(0, chunks)
     def _(chunk):
-        fetch(chunk).wait()
         for start in range(0, CHUNK, 8):
             first = pl.multiple_of(chunk * CHUNK + start, 8)
             rows = [unit(first + offset) for offset in range(8)]
@@ -214,17 +207,15 @@
     vmem = pl.BlockSpec(memory_space=pltpu.VMEM)
     return pl.pallas_call(
         functools.partial(memory_kernel, shards, slots),
-        in_specs=[vmem] * shards + [pl.BlockSpec(memory_space=pltpu.HBM)],
+        in_specs=[vmem] * (shards + 1),
         out_specs=[vmem] * shards,
         out_shape=[jax.ShapeDtypeStruct((q_count, p_count), jnp.float32)] * shards,
         scratch_shapes=[
-            pltpu.VMEM((p_count, p_tokens, depth), memory.dtype),
             pltpu.VMEM((total, q_tokens, depth), memory.dtype),
             pltpu.VMEM((total, p_count), jnp.float32),
             pltpu.VMEM((p_count, SLOTS * q_tokens), jnp.float32),
             pltpu.VMEM((SLOTS, p_count), jnp.int32),
             pltpu.SMEM((SLOTS, p_count), jnp.int32),
-            pltpu.SemaphoreType.DMA((p_count // CHUNK,)),
             pltpu.SemaphoreType.DMA,
         ],
         compiler_params=pltpu.CompilerParams(vmem_limit_bytes=16 * MIB),
@@ -234,7 +225,7 @@
             transcendentals=0,
         ),
         name="score_memory",
-    )(*packed, in_hbm(memory))
+    )(*packed, memory)
 
 
 def batch_kernel(query_ref, *refs):

time: 25.3 us -> 25.2 us (level)
    pallas_call x1, Pallas kernels: 4.41 us -> 4.14 us  [score_memory(): pl.pallas_call(functools.partial(memory_kernel, shards, slots), in_specs=...]
  transfers between devices with their start and end apart: 11 -> 11, of which waited for: 4 -> 4; matrix products, arithmetic and copies ran while one was open for 0% -> 0% of each run, Pallas kernels for 24% -> 23%
where the time goes in v4:
time: 25.2 us; the launch traced here: 25 us
  starting transfers between devices  14.1 us (56%)
  Pallas kernels  7.63 us (30%)
  waiting for transfers between devices  2.56 us (10%)
  between operations  0.73 us (3%)
    ppermute x6, starting transfers between devices, to_shard(): return lax.ppermute(array, 'memory', [(i, i ^ step) for i in range(shards)])  10.2 us
    pallas_call x1, Pallas kernels, score_memory(): pl.pallas_call(functools.partial(memory_kernel, shards, slots), in_specs=...  4.14 us
    ppermute x5, starting transfers between devices, to_group(): return lax.ppermute(array, 'group', [(i, i ^ step) for i in range(groups)])  3.88 us
    ppermute x6, waiting for transfers between devices, to_shard(): return lax.ppermute(array, 'memory', [(i, i ^ step) for i in range(shards)])  2.35 us
    pallas_call x2, Pallas kernels, score_batch(): pl.pallas_call(batch_kernel, out_shape=jax.ShapeDtypeStruct((q_count, lan...  1.67 us
    pallas_call x1, Pallas kernels, pack(): pl.pallas_call(functools.partial(pack_kernel, p_count), in_specs=[vmem, v...  1.02 us
    pallas_call x1, Pallas kernels, finish(): pl.pallas_call(functools.partial(loss_kernel, len(memory_parts)), out_sha...  0.8 us
  transfers between devices with their start and end apart: 11, of which 4 were waited for; matrix products, arithmetic and copies ran while one was open for 0% of the time, Pallas kernels for 23%

profile of v4, /device:TPU:0, one launch (start us, length us, event | category | flops | bytes accessed | tf_op | source)
XLA Modules:
  0.0 25.0 jit_solution(5303154582574263018)
XLA Ops:
  0.6 0.0 copy-start.1
  0.6 0.0 copy-start
  0.7 0.0 copy-start.4
  0.7 1.0 %pack.1.refs_0_ = bf16[272,128]{1,0:T(8,128)(2,1)S(1)} custom-call(bf16[1,8,32,128]{3,2,1,0:T(8,128)(2,1)} %query_ref.2, s32[1,8,64]{2,1,0:T(8,128)} %refs_4_.3, s32[1,8]{1,0:T(1,128)} %refs_5_.1), custom_call_target="tpu_custom_call" | custom-call | flops 10000000000 | bytes 16777216 | tf_op jit(solution)/shard_map/pack/pallas_call | solution.py:94
  1.7 0.0 copy-start.2
  1.7 0.0 copy-start.3
  1.7 5.1 %collective-permute-start.3 = (bf16[272,128]{1,0:T(8,128)(2,1)S(1)}, bf16[272,128]{1,0:T(8,128)(2,1)S(1)}, u32[]{:S(2)}, u32[]{:S(2)}) collective-permute-start(bf16[272,128]{1,0:T(8,128)(2,1)S(1)} %pack.1.refs_0_), channel_id=1, source_target_pairs={{0,24},{8,16},{16,8},{24,0},{1,25},{9,17},{17,9},{25,1},{2,26},{10... | collective-permute-start | bytes 208904 | tf_op jit(solution)/shard_map/ppermute | solution.py:328
  6.8 0.0 collective-permute-start.2
  6.8 0.6 %collective-permute-start.1 = (bf16[272,128]{1,0:T(8,128)(2,1)S(1)}, bf16[272,128]{1,0:T(8,128)(2,1)S(1)}, u32[]{:S(2)}, u32[]{:S(2)}) collective-permute-start(bf16[272,128]{1,0:T(8,128)(2,1)S(1)} %pack.1.refs_0_), channel_id=1, source_target_pairs={{0,8},{8,0},{16,24},{24,16},{1,9},{9,1},{17,25},{25,17},{2,10},{10... | collective-permute-start | bytes 208904 | tf_op jit(solution)/shard_map/ppermute | solution.py:328
  7.5 2.6 %collective-permute-start.6 = (bf16[1,8,128,128]{3,2,1,0:T(8,128)(2,1)S(1)}, bf16[1,8,128,128]{3,2,1,0:T(8,128)(2,1)S(1)}, u32[]{:S(2)}, u32[]{:S(2)}) collective-permute-start(bf16[1,8,128,128]{3,2,1,0:T(8,128)(2,1)S(1)} %copy-done), channel_id=1, source_target_pairs={{0,6},{1,7},{2,4},{3,5},{4,2},{5,3},{6,0},{7,1},{8,14},{9,15},{10,... | collective-permute-start | bytes 786440 | tf_op jit(solution)/shard_map/ppermute | solution.py:331
  10.1 0.5 %collective-permute-start.5 = (bf16[1,8,128,128]{3,2,1,0:T(8,128)(2,1)S(1)}, bf16[1,8,128,128]{3,2,1,0:T(8,128)(2,1)S(1)}, u32[]{:S(2)}, u32[]{:S(2)}) collective-permute-start(bf16[1,8,128,128]{3,2,1,0:T(8,128)(2,1)S(1)} %copy-done), channel_id=1, source_target_pairs={{0,4},{1,5},{2,6},{3,7},{4,0},{5,1},{6,2},{7,3},{8,12},{9,13},{10,... | collective-permute-start | bytes 786440 | tf_op jit(solution)/shard_map/ppermute | solution.py:331
  10.6 0.0 collective-permute-done.3.refs_3_
  10.6 0.8 %collective-permute-start.4 = (bf16[1,8,128,128]{3,2,1,0:T(8,128)(2,1)S(1)}, bf16[1,8,128,128]{3,2,1,0:T(8,128)(2,1)S(1)}, u32[]{:S(2)}, u32[]{:S(2)}) collective-permute-start(bf16[1,8,128,128]{3,2,1,0:T(8,128)(2,1)S(1)} %copy-done), channel_id=1, source_target_pairs={{0,2},{1,3},{2,0},{3,1},{4,6},{5,7},{6,4},{7,5},{8,10},{9,11},{10,... | collective-permute-start | bytes 786440 | tf_op jit(solution)/shard_map/ppermute | solution.py:331
  11.3 1.4 %collective-permute-done.2.refs_2_ = bf16[272,128]{1,0:T(8,128)(2,1)S(1)} collective-permute-done((bf16[272,128]{1,0:T(8,128)(2,1)S(1)}, bf16[272,128]{1,0:T(8,128)(2,1)S(1)}, u32[]{:S(2)}, u32[]{:S(2)}) %collective-permute-start.2) | collective-permute-done | bytes 69664 | tf_op jit(solution)/shard_map/ppermute | solution.py:328
  12.7 0.0 collective-permute-start
  12.7 0.0 collective-permute-done.1.refs_1_
  12.8 4.1 %score_memory.1 = (f32[8,128]{1,0:T(8,128)S(1)}, f32[8,128]{1,0:T(8,128)S(1)}, f32[8,128]{1,0:T(8,128)S(1)}, f32[8,128]{1,0:T(8,128)S(1)}) custom-call(bf16[272,128]{1,0:T(8,128)(2,1)S(1)} %pack.1.refs_0_, bf16[272,128]{1,0:T(8,128)(2,1)S(1)} %collective-permute-done.1.refs_1_, bf16[272,128]{1,0:T(8,128)(2,1)S(1)} %collective-permute-done.2.refs_2_, ...), custom_call_target="tpu_custom_call" | custom-call | flops 4294967296 | bytes 4194304 | tf_op jit(solution)/shard_map/score_memory/pallas_call | solution.py:208
  16.9 0.0 collective-permute-done.query_ref
  16.9 2.8 %collective-permute-start.8 = (f32[8,128]{1,0:T(8,128)S(1)}, f32[8,128]{1,0:T(8,128)S(1)}, u32[]{:S(2)}, u32[]{:S(2)}) collective-permute-start(f32[8,128]{1,0:T(8,128)S(1)} %get-tuple-element.16), channel_id=1, source_target_pairs={{0,24},{8,16},{16,8},{24,0},{1,25},{9,17},{17,9},{25,1},{2,26},{10... | collective-permute-start | bytes 12296 | tf_op jit(solution)/shard_map/ppermute | solution.py:328
  19.7 0.0 collective-permute-start.9
  19.7 0.0 collective-permute-done.6.refs_3_
  19.7 1.7 %collective-permute-start.10 = (f32[8,128]{1,0:T(8,128)S(1)}, f32[8,128]{1,0:T(8,128)S(1)}, u32[]{:S(2)}, u32[]{:S(2)}) collective-permute-start(f32[8,128]{1,0:T(8,128)S(1)} %get-tuple-element.18), channel_id=1, source_target_pairs={{0,8},{8,0},{16,24},{24,16},{1,9},{9,1},{17,25},{25,17},{2,10},{10... | collective-permute-start | bytes 12296 | tf_op jit(solution)/shard_map/ppermute | solution.py:328
  21.4 0.1 collective-permute-done.5.refs_2_
  21.5 0.1 collective-permute-done.4.refs_1_
  21.6 0.8 %score_batch.2 = f32[8,128]{1,0:T(8,128)S(1)} custom-call(bf16[1,8,32,128]{3,2,1,0:T(8,128)(2,1)S(1)} %collective-permute-done.query_ref, bf16[1,8,128,128]{3,2,1,0:T(8,128)(2,1)S(1)} %copy-done, bf16[1,8,128,128]{3,2,1,0:T(8,128)(2,1)S(1)} %collective-permute-done.4.refs_1_, bf16[1,8,128,128]{3,2,1,0:T(8,128)(2,1)S(1)} %collective-permute-done.5.refs_2_, ...), custom_call_target="tpu_custom_call" | custom-call | flops 268435456 | bytes 1048576 | tf_op jit(solution)/shard_map/score_batch/pallas_call | solution.py:248
  22.4 0.0 collective-permute-start.7
  22.4 0.9 %score_batch.3.own_batch = f32[8,128]{1,0:T(8,128)S(1)} custom-call(bf16[1,8,32,128]{3,2,1,0:T(8,128)(2,1)S(1)} %copy-done.1, bf16[1,8,128,128]{3,2,1,0:T(8,128)(2,1)S(1)} %copy-done, bf16[1,8,128,128]{3,2,1,0:T(8,128)(2,1)S(1)} %collective-permute-done.4.refs_1_, bf16[1,8,128,128]{3,2,1,0:T(8,128)(2,1)S(1)} %collective-permute-done.5.refs_2_, ...), custom_call_target="tpu_custom_call" | custom-call | flops 268435456 | bytes 1048576 | tf_op jit(solution)/shard_map/score_batch/pallas_call | solution.py:248
  23.2 0.0 collective-permute-done.8.refs_1_
  23.3 0.9 %collective-permute-done.9.refs_2_ = f32[8,128]{1,0:T(8,128)S(1)} collective-permute-done((f32[8,128]{1,0:T(8,128)S(1)}, f32[8,128]{1,0:T(8,128)S(1)}, u32[]{:S(2)}, u32[]{:S(2)}) %collective-permute-start.9) | collective-permute-done | bytes 4128 | tf_op jit(solution)/shard_map/ppermute | solution.py:328
  24.2 0.0 collective-permute-done.10.refs_3_
  24.2 0.0 collective-permute-done.7.mate_batch
  24.2 0.8 %finish.1 = (f32[1,8,64]{2,1,0:T(8,128)}, f32[1,8,64]{2,1,0:T(8,128)}, f32[1,8]{1,0:T(1,128)}) custom-call(f32[8,128]{1,0:T(8,128)S(1)} %score_batch.3.own_batch, f32[8,128]{1,0:T(8,128)S(1)} %collective-permute-done.7.mate_batch, f32[8,128]{1,0:T(8,128)S(1)} %get-tuple-element.12.refs_0_, f32[8,128]{1,0:T(8,128)S(1)} %collective-permute-done.8.refs_1_, ...), custom_call_target="tpu_custom_call" | custom-call | tf_op jit(solution)/shard_map/finish/pallas_call | solution.py:308
  (5 shorter events, 0.0 us)
Async XLA Ops:
  0.6 12.1 %copy-start.1 = (bf16[1,8,32,128]{3,2,1,0:T(8,128)(2,1)S(1)}, bf16[1,8,32,128]{3,2,1,0:T(8,128)(2,1)}, u32[]{:S(2)}) copy-start(bf16[1,8,32,128]{3,2,1,0:T(8,128)(2,1)} %query_ref.2) | copy-start | bytes 196612
  0.6 6.8 %copy-start = (bf16[1,8,128,128]{3,2,1,0:T(8,128)(2,1)S(1)}, bf16[1,8,128,128]{3,2,1,0:T(8,128)(2,1)}, u32[]{:S(2)}) copy-start(bf16[1,8,128,128]{3,2,1,0:T(8,128)(2,1)} %refs_0_.3) | copy-start | bytes 786436
  0.7 12.1 %copy-start.4 = (bf16[1,128,128,128]{3,2,1,0:T(8,128)(2,1)S(1)}, bf16[1,128,128,128]{3,2,1,0:T(8,128)(2,1)}, u32[]{:S(2)}) copy-start(bf16[1,128,128,128]{3,2,1,0:T(8,128)(2,1)} %refs_4_.2) | copy-start | bytes 12582916
  1.7 22.5 %copy-start.2 = (s32[1,8,64]{2,1,0:T(8,128)S(1)}, s32[1,8,64]{2,1,0:T(8,128)}, u32[]{:S(2)}) copy-start(s32[1,8,64]{2,1,0:T(8,128)} %refs_4_.3) | copy-start | bytes 6148
  1.7 22.5 %copy-start.3 = (s32[1,8]{1,0:T(1,128)S(1)}, s32[1,8]{1,0:T(1,128)}, u32[]{:S(2)}) copy-start(s32[1,8]{1,0:T(1,128)} %refs_5_.1) | copy-start | bytes 100
  1.7 8.9 %collective-permute-start.3 = (bf16[272,128]{1,0:T(8,128)(2,1)S(1)}, bf16[272,128]{1,0:T(8,128)(2,1)S(1)}, u32[]{:S(2)}, u32[]{:S(2)}) collective-permute-start(bf16[272,128]{1,0:T(8,128)(2,1)S(1)} %pack.1.refs_0_), channel_id=1, source_target_pairs={{0,24},{8,16},{16,8},{24,0},{1,25},{9,17},{17,9},{25,1},{2,26},{10... | collective-permute-start | bytes 208904 | tf_op jit(solution)/shard_map/ppermute | solution.py:328
  6.8 5.9 %collective-permute-start.2 = (bf16[272,128]{1,0:T(8,128)(2,1)S(1)}, bf16[272,128]{1,0:T(8,128)(2,1)S(1)}, u32[]{:S(2)}, u32[]{:S(2)}) collective-permute-start(bf16[272,128]{1,0:T(8,128)(2,1)S(1)} %pack.1.refs_0_), channel_id=1, source_target_pairs={{0,16},{8,24},{16,0},{24,8},{1,17},{9,25},{17,1},{25,9},{2,18},{10... | collective-permute-start | bytes 208904 | tf_op jit(solution)/shard_map/ppermute | solution.py:328
  6.8 5.9 %collective-permute-start.1 = (bf16[272,128]{1,0:T(8,128)(2,1)S(1)}, bf16[272,128]{1,0:T(8,128)(2,1)S(1)}, u32[]{:S(2)}, u32[]{:S(2)}) collective-permute-start(bf16[272,128]{1,0:T(8,128)(2,1)S(1)} %pack.1.refs_0_), channel_id=1, source_target_pairs={{0,8},{8,0},{16,24},{24,16},{1,9},{9,1},{17,25},{25,17},{2,10},{10... | collective-permute-start | bytes 208904 | tf_op jit(solution)/shard_map/ppermute | solution.py:328
  7.5 12.2 %collective-permute-start.6 = (bf16[1,8,128,128]{3,2,1,0:T(8,128)(2,1)S(1)}, bf16[1,8,128,128]{3,2,1,0:T(8,128)(2,1)S(1)}, u32[]{:S(2)}, u32[]{:S(2)}) collective-permute-start(bf16[1,8,128,128]{3,2,1,0:T(8,128)(2,1)S(1)} %copy-done), channel_id=1, source_target_pairs={{0,6},{1,7},{2,4},{3,5},{4,2},{5,3},{6,0},{7,1},{8,14},{9,15},{10,... | collective-permute-start | bytes 786440 | tf_op jit(solution)/shard_map/ppermute | solution.py:331
  10.1 11.4 %collective-permute-start.5 = (bf16[1,8,128,128]{3,2,1,0:T(8,128)(2,1)S(1)}, bf16[1,8,128,128]{3,2,1,0:T(8,128)(2,1)S(1)}, u32[]{:S(2)}, u32[]{:S(2)}) collective-permute-start(bf16[1,8,128,128]{3,2,1,0:T(8,128)(2,1)S(1)} %copy-done), channel_id=1, source_target_pairs={{0,4},{1,5},{2,6},{3,7},{4,0},{5,1},{6,2},{7,3},{8,12},{9,13},{10,... | collective-permute-start | bytes 786440 | tf_op jit(solution)/shard_map/ppermute | solution.py:331
  10.6 11.0 %collective-permute-start.4 = (bf16[1,8,128,128]{3,2,1,0:T(8,128)(2,1)S(1)}, bf16[1,8,128,128]{3,2,1,0:T(8,128)(2,1)S(1)}, u32[]{:S(2)}, u32[]{:S(2)}) collective-permute-start(bf16[1,8,128,128]{3,2,1,0:T(8,128)(2,1)S(1)} %copy-done), channel_id=1, source_target_pairs={{0,2},{1,3},{2,0},{3,1},{4,6},{5,7},{6,4},{7,5},{8,10},{9,11},{10,... | collective-permute-start | bytes 786440 | tf_op jit(solution)/shard_map/ppermute | solution.py:331
  12.7 4.2 %collective-permute-start = (bf16[1,8,32,128]{3,2,1,0:T(8,128)(2,1)S(1)}, bf16[1,8,32,128]{3,2,1,0:T(8,128)(2,1)S(1)}, u32[]{:S(2)}, u32[]{:S(2)}) collective-permute-start(bf16[1,8,32,128]{3,2,1,0:T(8,128)(2,1)S(1)} %copy-done.1), channel_id=1, source_target_pairs={{0,1},{1,0},{2,3},{3,2},{4,5},{5,4},{6,7},{7,6},{8,9},{9,8},{10,11... | collective-permute-start | bytes 196616 | tf_op jit(solution)/shard_map/ppermute | solution.py:331
  16.9 6.3 %collective-permute-start.8 = (f32[8,128]{1,0:T(8,128)S(1)}, f32[8,128]{1,0:T(8,128)S(1)}, u32[]{:S(2)}, u32[]{:S(2)}) collective-permute-start(f32[8,128]{1,0:T(8,128)S(1)} %get-tuple-element.16), channel_id=1, source_target_pairs={{0,24},{8,16},{16,8},{24,0},{1,25},{9,17},{17,9},{25,1},{2,26},{10... | collective-permute-start | bytes 12296 | tf_op jit(solution)/shard_map/ppermute | solution.py:328
  19.7 4.5 %collective-permute-start.9 = (f32[8,128]{1,0:T(8,128)S(1)}, f32[8,128]{1,0:T(8,128)S(1)}, u32[]{:S(2)}, u32[]{:S(2)}) collective-permute-start(f32[8,128]{1,0:T(8,128)S(1)} %get-tuple-element.17), channel_id=1, source_target_pairs={{0,16},{8,24},{16,0},{24,8},{1,17},{9,25},{17,1},{25,9},{2,18},{10... | collective-permute-start | bytes 12296 | tf_op jit(solution)/shard_map/ppermute | solution.py:328
  19.7 4.5 %collective-permute-start.10 = (f32[8,128]{1,0:T(8,128)S(1)}, f32[8,128]{1,0:T(8,128)S(1)}, u32[]{:S(2)}, u32[]{:S(2)}) collective-permute-start(f32[8,128]{1,0:T(8,128)S(1)} %get-tuple-element.18), channel_id=1, source_target_pairs={{0,8},{8,0},{16,24},{24,16},{1,9},{9,1},{17,25},{25,17},{2,10},{10... | collective-permute-start | bytes 12296 | tf_op jit(solution)/shard_map/ppermute | solution.py:328
  22.4 1.8 %collective-permute-start.7 = (f32[8,128]{1,0:T(8,128)S(1)}, f32[8,128]{1,0:T(8,128)S(1)}, u32[]{:S(2)}, u32[]{:S(2)}) collective-permute-start(f32[8,128]{1,0:T(8,128)S(1)} %score_batch.2), channel_id=1, source_target_pairs={{0,1},{1,0},{2,3},{3,2},{4,5},{5,4},{6,7},{7,6},{8,9},{9,8},{10,11... | collective-permute-start | bytes 12296 | tf_op jit(solution)/shard_map/ppermute | solution.py:331

commit v5 on v4

--- a/solution.py
+++ b/solution.py
@@ -105,14 +105,15 @@
 
 def memory_kernel(shards, slots, *refs):
     packed_refs, passage_ref = refs[:shards], refs[shards].at[0]
-    out_refs = refs[shards + 1 : 2 * shards + 1]
-    query_ref, rank_ref, best_ref, list_ref, scalar_ref, list_sem = refs[2 * shards + 1 :]
-    q_count = out_refs[0].shape[0]
+    score_ref, query_ref, rank_ref, best_ref, list_ref, scalar_ref, list_sem = refs[shards + 1 :]
+    place = lax.axis_index("memory")
+    out_refs = [score_ref.at[place ^ step] for step in range(shards)]
+    q_count = score_ref.shape[1]
     p_count = passage_ref.shape[0]
     total, q_tokens, depth = query_ref.shape
     chunks = p_count // CHUNK
 
-    me = lax.axis_index("memory").astype(jnp.float32)
+    me = place.astype(jnp.float32)
     keys = []
     for index, packed_ref in enumerate(packed_refs):
         tokens = packed_ref[: q_count * q_tokens].reshape(q_count, q_tokens, depth)
@@ -208,8 +209,8 @@
     return pl.pallas_call(
         functools.partial(memory_kernel, shards, slots),
         in_specs=[vmem] * (shards + 1),
-        out_specs=[vmem] * shards,
-        out_shape=[jax.ShapeDtypeStruct((q_count, p_count), jnp.float32)] * shards,
+        out_specs=vmem,
+        out_shape=jax.ShapeDtypeStruct((shards, q_count, p_count), jnp.float32),
         scratch_shapes=[
             pltpu.VMEM((total, q_tokens, depth), memory.dtype),
             pltpu.VMEM((total, p_count), jnp.float32),
@@ -259,13 +260,12 @@
     )(queries, *positives)
 
 
-def loss_kernel(shards, own_batch, mate_batch, *refs):
-    memory_refs = refs[:shards]
-    candidate_ref, count_ref, batch_ref, memory_ref, loss_ref = refs[shards:]
-    group, shard = lax.axis_index("group"), lax.axis_index("memory")
+def loss_kernel(own_batch, mate_batch, part_ref, candidate_ref, count_ref, *out_refs):
+    batch_ref, memory_ref, loss_ref = out_refs
+    group = lax.axis_index("group")
     chip, core = group // 2, group % 2
     _, q_count, slots = candidate_ref.shape
-    p_count = memory_refs[0].shape[1]
+    shards, _, p_count = part_ref.shape
     columns = batch_ref.shape[2]
 
     parts = []
@@ -283,9 +283,9 @@
     padded = jnp.concatenate([ids, jnp.zeros((q_count, p_count - slots), jnp.int32)], axis=1)
     holder, local = padded // p_count, padded % p_count
     picked = jnp.zeros((q_count, p_count), jnp.float32)
-    for step in range(shards):
-        found = jnp.take_along_axis(memory_refs[-step][...], local, axis=1)
-        picked = jnp.where(holder == (shard ^ step), found, picked)
+    for shard in range(shards):
+        found = jnp.take_along_axis(part_ref[shard], local, axis=1)
+        picked = jnp.where(holder == shard, found, picked)
 
     valid = lax.broadcasted_iota(jnp.int32, (q_count, p_count), 1) < column_of(count_ref[...])
     memory_ref[0] = jnp.where(valid, picked, 0.0)[:, :slots]
@@ -306,7 +306,7 @@
 def finish(own_batch, mate_batch, memory_parts, candidates, counts, columns):
     _, q_count, slots = candidates.shape
     return pl.pallas_call(
-        functools.partial(loss_kernel, len(memory_parts)),
+        loss_kernel,
         out_shape=[
             jax.ShapeDtypeStruct((1, q_count, columns), jnp.float32),
             jax.ShapeDtypeStruct((1, q_count, slots), jnp.float32),
@@ -314,7 +314,7 @@
         ],
         compiler_params=pltpu.CompilerParams(vmem_limit_bytes=4 * MIB),
         name="finish",
-    )(own_batch, mate_batch, *memory_parts, candidates, counts)
+    )(own_batch, mate_batch, memory_parts, candidates, counts)
 
 
 def body(queries, positives, memory, candidates, counts):
@@ -337,16 +337,14 @@
     mate_queries = to_group(sent_queries, 1)
 
     scores = score_memory(packed, memory, q_count, slots)
-    returned = [to_shard(scores[step], step) for step in range(shards - 1, 0, -1)]
-    mate_queries, _ = lax.optimization_barrier((mate_queries, scores[0]))
+    returned = lax.all_to_all(scores, "memory", split_axis=0, concat_axis=0, tiled=True)
+    mate_queries, _ = lax.optimization_barrier((mate_queries, scores))
     mate_scores = score_batch(mate_queries, row)
     mate_batch = to_group(mate_scores, 1)
     own_queries, _ = lax.optimization_barrier((queries, mate_scores))
     own_batch = score_batch(own_queries, row)
     columns = groups * q_count
-    return finish(
-        own_batch, mate_batch, [scores[0]] + returned, candidates, counts, columns
-    )
+    return finish(own_batch, mate_batch, returned, candidates, counts, columns)
 
 
 def solution(mesh):

time: 25.2 us -> 28.1 us (1.12)
  waiting for transfers between devices: 2.56 us -> 5.16 us
  Pallas kernels: 7.63 us -> 8.2 us
  starting transfers between devices: 14.1 us -> 13.8 us
    ppermute x6 -> x3, starting transfers between devices: 10.2 us -> 5.76 us  [to_shard(): return lax.ppermute(array, 'memory', [(i, i ^ step) for i in range(shards)])]
    all_to_all x0 -> x1, starting transfers between devices: none -> 4 us  [body(): lax.all_to_all(scores, 'memory', split_axis=0, concat_axis=0, tiled=True)]
    all_to_all x0 -> x1, waiting for transfers between devices: none -> 3.69 us  [body(): lax.all_to_all(scores, 'memory', split_axis=0, concat_axis=0, tiled=True)]
    ppermute x6 -> x3, waiting for transfers between devices: 2.35 us -> 1.39 us  [to_shard(): return lax.ppermute(array, 'memory', [(i, i ^ step) for i in range(shards)])]
    pallas_call x1, Pallas kernels: 4.14 us -> 4.73 us  [score_memory(): pl.pallas_call(functools.partial(memory_kernel, shards, slots), in_specs=...]
  transfers between devices with their start and end apart: 11 -> 9, of which waited for: 4 -> 3; matrix products, arithmetic and copies ran while one was open for 0% -> 0% of each run, Pallas kernels for 23% -> 23%
where the time goes in v5:
time: 28.1 us; the launch traced here: 27.9 us
  starting transfers between devices  13.8 us (49%)
  Pallas kernels  8.2 us (29%)
  waiting for transfers between devices  5.16 us (18%)
  between operations  0.72 us (3%)
    ppermute x3, starting transfers between devices, to_shard(): return lax.ppermute(array, 'memory', [(i, i ^ step) for i in range(shards)])  5.76 us
    pallas_call x1, Pallas kernels, score_memory(): pl.pallas_call(functools.partial(memory_kernel, shards, slots), in_specs=...  4.73 us
    ppermute x5, starting transfers between devices, to_group(): return lax.ppermute(array, 'group', [(i, i ^ step) for i in range(groups)])  4.06 us
    all_to_all x1, starting transfers between devices, body(): lax.all_to_all(scores, 'memory', split_axis=0, concat_axis=0, tiled=True)  4 us
    all_to_all x1, waiting for transfers between devices, body(): lax.all_to_all(scores, 'memory', split_axis=0, concat_axis=0, tiled=True)  3.69 us
    pallas_call x2, Pallas kernels, score_batch(): pl.pallas_call(batch_kernel, out_shape=jax.ShapeDtypeStruct((q_count, lan...  1.65 us
    ppermute x3, waiting for transfers between devices, to_shard(): return lax.ppermute(array, 'memory', [(i, i ^ step) for i in range(shards)])  1.39 us
    pallas_call x1, Pallas kernels, pack(): pl.pallas_call(functools.partial(pack_kernel, p_count), in_specs=[vmem, v...  1.02 us
  transfers between devices with their start and end apart: 9, of which 3 were waited for; matrix products, arithmetic and copies ran while one was open for 0% of the time, Pallas kernels for 23%

profile of v5, /device:TPU:0, one launch (start us, length us, event | category | flops | bytes accessed | tf_op | source)
XLA Modules:
  0.0 27.9 jit_solution(16099393010121748946)
XLA Ops:
  0.6 0.0 copy-start.1
  0.6 0.0 copy-start
  0.7 0.0 copy-start.4
  0.7 1.0 %pack.1.refs_0_ = bf16[272,128]{1,0:T(8,128)(2,1)S(1)} custom-call(bf16[1,8,32,128]{3,2,1,0:T(8,128)(2,1)} %query_ref.2, s32[1,8,64]{2,1,0:T(8,128)} %candidate_ref.3, s32[1,8]{1,0:T(1,128)} %count_ref.3), custom_call_target="tpu_custom_call" | custom-call | flops 10000000000 | bytes 16777216 | tf_op jit(solution)/shard_map/pack/pallas_call | solution.py:94
  1.7 0.0 copy-start.2
  1.7 0.0 copy-start.3
  1.7 5.1 %collective-permute-start.3 = (bf16[272,128]{1,0:T(8,128)(2,1)S(1)}, bf16[272,128]{1,0:T(8,128)(2,1)S(1)}, u32[]{:S(2)}, u32[]{:S(2)}) collective-permute-start(bf16[272,128]{1,0:T(8,128)(2,1)S(1)} %pack.1.refs_0_), channel_id=1, source_target_pairs={{0,24},{8,16},{16,8},{24,0},{1,25},{9,17},{17,9},{25,1},{2,26},{10... | collective-permute-start | bytes 208904 | tf_op jit(solution)/shard_map/ppermute | solution.py:328
  6.8 0.0 collective-permute-start.2
  6.8 0.6 %collective-permute-start.1 = (bf16[272,128]{1,0:T(8,128)(2,1)S(1)}, bf16[272,128]{1,0:T(8,128)(2,1)S(1)}, u32[]{:S(2)}, u32[]{:S(2)}) collective-permute-start(bf16[272,128]{1,0:T(8,128)(2,1)S(1)} %pack.1.refs_0_), channel_id=1, source_target_pairs={{0,8},{8,0},{16,24},{24,16},{1,9},{9,1},{17,25},{25,17},{2,10},{10... | collective-permute-start | bytes 208904 | tf_op jit(solution)/shard_map/ppermute | solution.py:328
  7.5 0.0 copy-done
  7.5 2.6 %collective-permute-start.6 = (bf16[1,8,128,128]{3,2,1,0:T(8,128)(2,1)S(1)}, bf16[1,8,128,128]{3,2,1,0:T(8,128)(2,1)S(1)}, u32[]{:S(2)}, u32[]{:S(2)}) collective-permute-start(bf16[1,8,128,128]{3,2,1,0:T(8,128)(2,1)S(1)} %copy-done), channel_id=1, source_target_pairs={{0,6},{1,7},{2,4},{3,5},{4,2},{5,3},{6,0},{7,1},{8,14},{9,15},{10,... | collective-permute-start | bytes 786440 | tf_op jit(solution)/shard_map/ppermute | solution.py:331
  10.1 0.5 %collective-permute-start.5 = (bf16[1,8,128,128]{3,2,1,0:T(8,128)(2,1)S(1)}, bf16[1,8,128,128]{3,2,1,0:T(8,128)(2,1)S(1)}, u32[]{:S(2)}, u32[]{:S(2)}) collective-permute-start(bf16[1,8,128,128]{3,2,1,0:T(8,128)(2,1)S(1)} %copy-done), channel_id=1, source_target_pairs={{0,4},{1,5},{2,6},{3,7},{4,0},{5,1},{6,2},{7,3},{8,12},{9,13},{10,... | collective-permute-start | bytes 786440 | tf_op jit(solution)/shard_map/ppermute | solution.py:331
  10.6 0.0 collective-permute-done.3.refs_3_
  10.6 0.8 %collective-permute-start.4 = (bf16[1,8,128,128]{3,2,1,0:T(8,128)(2,1)S(1)}, bf16[1,8,128,128]{3,2,1,0:T(8,128)(2,1)S(1)}, u32[]{:S(2)}, u32[]{:S(2)}) collective-permute-start(bf16[1,8,128,128]{3,2,1,0:T(8,128)(2,1)S(1)} %copy-done), channel_id=1, source_target_pairs={{0,2},{1,3},{2,0},{3,1},{4,6},{5,7},{6,4},{7,5},{8,10},{9,11},{10,... | collective-permute-start | bytes 786440 | tf_op jit(solution)/shard_map/ppermute | solution.py:331
  11.3 1.4 %collective-permute-done.2.refs_2_ = bf16[272,128]{1,0:T(8,128)(2,1)S(1)} collective-permute-done((bf16[272,128]{1,0:T(8,128)(2,1)S(1)}, bf16[272,128]{1,0:T(8,128)(2,1)S(1)}, u32[]{:S(2)}, u32[]{:S(2)}) %collective-permute-start.2) | collective-permute-done | bytes 69664 | tf_op jit(solution)/shard_map/ppermute | solution.py:328
  12.7 0.0 copy-done.1
  12.7 0.0 collective-permute-start
  12.7 0.0 collective-permute-done.1.refs_1_
  12.7 0.0 copy-done.4
  12.8 4.7 %score_memory.1 = f32[4,8,128]{2,1,0:T(8,128)} custom-call(bf16[272,128]{1,0:T(8,128)(2,1)S(1)} %pack.1.refs_0_, bf16[272,128]{1,0:T(8,128)(2,1)S(1)} %collective-permute-done.1.refs_1_, bf16[272,128]{1,0:T(8,128)(2,1)S(1)} %collective-permute-done.2.refs_2_, bf16[272,128]{1,0:T(8,128)(2,1)S(1)} %collective-permute-done.3.refs_3_, ...), custom_call_target="tpu_custom_call" | custom-call | flops 4294967296 | bytes 4194304 | tf_op jit(solution)/shard_map/score_memory/pallas_call | solution.py:209
  17.5 4.0 %all-to-all-start = ((f32[4,8,128]{2,1,0:T(8,128)}), f32[4,8,128]{2,1,0:T(8,128)S(1)}, u32[]{:S(2)}, u32[]{:S(2)}) async-start(f32[4,8,128]{2,1,0:T(8,128)} %score_memory.1), calls=%async_computation | async-start | bytes 32768 | tf_op jit(solution)/shard_map/all_to_all | solution.py:340
  21.5 0.0 collective-permute-done.query_ref
  21.5 0.0 collective-permute-done.6.refs_3_
  21.5 0.0 collective-permute-done.5.refs_2_
  21.5 0.1 collective-permute-done.4.refs_1_
  21.6 0.8 %score_batch.2 = f32[8,128]{1,0:T(8,128)S(1)} custom-call(bf16[1,8,32,128]{3,2,1,0:T(8,128)(2,1)S(1)} %collective-permute-done.query_ref, bf16[1,8,128,128]{3,2,1,0:T(8,128)(2,1)S(1)} %copy-done, bf16[1,8,128,128]{3,2,1,0:T(8,128)(2,1)S(1)} %collective-permute-done.4.refs_1_, bf16[1,8,128,128]{3,2,1,0:T(8,128)(2,1)S(1)} %collective-permute-done.5.refs_2_, ...), custom_call_target="tpu_custom_call" | custom-call | flops 268435456 | bytes 1048576 | tf_op jit(solution)/shard_map/score_batch/pallas_call | solution.py:249
  22.4 0.2 collective-permute-start.7
  22.6 0.8 %score_batch.3.own_batch = f32[8,128]{1,0:T(8,128)S(1)} custom-call(bf16[1,8,32,128]{3,2,1,0:T(8,128)(2,1)S(1)} %copy-done.1, bf16[1,8,128,128]{3,2,1,0:T(8,128)(2,1)S(1)} %copy-done, bf16[1,8,128,128]{3,2,1,0:T(8,128)(2,1)S(1)} %collective-permute-done.4.refs_1_, bf16[1,8,128,128]{3,2,1,0:T(8,128)(2,1)S(1)} %collective-permute-done.5.refs_2_, ...), custom_call_target="tpu_custom_call" | custom-call | flops 268435456 | bytes 1048576 | tf_op jit(solution)/shard_map/score_batch/pallas_call | solution.py:249
  23.4 3.7 %all-to-all-done.part_ref = f32[4,8,128]{2,1,0:T(8,128)S(1)} async-done(((f32[4,8,128]{2,1,0:T(8,128)}), f32[4,8,128]{2,1,0:T(8,128)S(1)}, u32[]{:S(2)}, u32[]{:S(2)}) %all-to-all-start) | async-done | bytes 16416 | tf_op jit(solution)/shard_map/all_to_all | solution.py:340
  27.1 0.0 collective-permute-done.7.mate_batch
  27.1 0.0 copy-done.2
  27.1 0.8 %finish.1 = (f32[1,8,64]{2,1,0:T(8,128)}, f32[1,8,64]{2,1,0:T(8,128)}, f32[1,8]{1,0:T(1,128)}) custom-call(f32[8,128]{1,0:T(8,128)S(1)} %score_batch.3.own_batch, f32[8,128]{1,0:T(8,128)S(1)} %collective-permute-done.7.mate_batch, f32[4,8,128]{2,1,0:T(8,128)S(1)} %all-to-all-done.part_ref, s32[1,8,64]{2,1,0:T(8,128)S(1)} %copy-done.2, s32[1,8]{1,0:T(1,128)S(1)} %copy-done.3), custom_call_target="tpu_custom_call" | custom-call | tf_op jit(solution)/shard_map/finish/pallas_call | solution.py:308
  (1 shorter events, 0.0 us)
Async XLA Ops:
  0.6 12.1 %copy-start.1 = (bf16[1,8,32,128]{3,2,1,0:T(8,128)(2,1)S(1)}, bf16[1,8,32,128]{3,2,1,0:T(8,128)(2,1)}, u32[]{:S(2)}) copy-start(bf16[1,8,32,128]{3,2,1,0:T(8,128)(2,1)} %query_ref.2) | copy-start | bytes 196612
  0.6 6.8 %copy-start = (bf16[1,8,128,128]{3,2,1,0:T(8,128)(2,1)S(1)}, bf16[1,8,128,128]{3,2,1,0:T(8,128)(2,1)}, u32[]{:S(2)}) copy-start(bf16[1,8,128,128]{3,2,1,0:T(8,128)(2,1)} %refs_0_.3) | copy-start | bytes 786436
  0.7 12.1 %copy-start.4 = (bf16[1,128,128,128]{3,2,1,0:T(8,128)(2,1)S(1)}, bf16[1,128,128,128]{3,2,1,0:T(8,128)(2,1)}, u32[]{:S(2)}) copy-start(bf16[1,128,128,128]{3,2,1,0:T(8,128)(2,1)} %refs_4_.1) | copy-start | bytes 12582916
  1.7 25.4 %copy-start.2 = (s32[1,8,64]{2,1,0:T(8,128)S(1)}, s32[1,8,64]{2,1,0:T(8,128)}, u32[]{:S(2)}) copy-start(s32[1,8,64]{2,1,0:T(8,128)} %candidate_ref.3) | copy-start | bytes 6148
  1.7 25.4 %copy-start.3 = (s32[1,8]{1,0:T(1,128)S(1)}, s32[1,8]{1,0:T(1,128)}, u32[]{:S(2)}) copy-start(s32[1,8]{1,0:T(1,128)} %count_ref.3) | copy-start | bytes 100
  1.7 8.9 %collective-permute-start.3 = (bf16[272,128]{1,0:T(8,128)(2,1)S(1)}, bf16[272,128]{1,0:T(8,128)(2,1)S(1)}, u32[]{:S(2)}, u32[]{:S(2)}) collective-permute-start(bf16[272,128]{1,0:T(8,128)(2,1)S(1)} %pack.1.refs_0_), channel_id=1, source_target_pairs={{0,24},{8,16},{16,8},{24,0},{1,25},{9,17},{17,9},{25,1},{2,26},{10... | collective-permute-start | bytes 208904 | tf_op jit(solution)/shard_map/ppermute | solution.py:328
  6.8 5.9 %collective-permute-start.2 = (bf16[272,128]{1,0:T(8,128)(2,1)S(1)}, bf16[272,128]{1,0:T(8,128)(2,1)S(1)}, u32[]{:S(2)}, u32[]{:S(2)}) collective-permute-start(bf16[272,128]{1,0:T(8,128)(2,1)S(1)} %pack.1.refs_0_), channel_id=1, source_target_pairs={{0,16},{8,24},{16,0},{24,8},{1,17},{9,25},{17,1},{25,9},{2,18},{10... | collective-permute-start | bytes 208904 | tf_op jit(solution)/shard_map/ppermute | solution.py:328
  6.8 5.9 %collective-permute-start.1 = (bf16[272,128]{1,0:T(8,128)(2,1)S(1)}, bf16[272,128]{1,0:T(8,128)(2,1)S(1)}, u32[]{:S(2)}, u32[]{:S(2)}) collective-permute-start(bf16[272,128]{1,0:T(8,128)(2,1)S(1)} %pack.1.refs_0_), channel_id=1, source_target_pairs={{0,8},{8,0},{16,24},{24,16},{1,9},{9,1},{17,25},{25,17},{2,10},{10... | collective-permute-start | bytes 208904 | tf_op jit(solution)/shard_map/ppermute | solution.py:328
  7.5 14.0 %collective-permute-start.6 = (bf16[1,8,128,128]{3,2,1,0:T(8,128)(2,1)S(1)}, bf16[1,8,128,128]{3,2,1,0:T(8,128)(2,1)S(1)}, u32[]{:S(2)}, u32[]{:S(2)}) collective-permute-start(bf16[1,8,128,128]{3,2,1,0:T(8,128)(2,1)S(1)} %copy-done), channel_id=1, source_target_pairs={{0,6},{1,7},{2,4},{3,5},{4,2},{5,3},{6,0},{7,1},{8,14},{9,15},{10,... | collective-permute-start | bytes 786440 | tf_op jit(solution)/shard_map/ppermute | solution.py:331
  10.1 11.4 %collective-permute-start.5 = (bf16[1,8,128,128]{3,2,1,0:T(8,128)(2,1)S(1)}, bf16[1,8,128,128]{3,2,1,0:T(8,128)(2,1)S(1)}, u32[]{:S(2)}, u32[]{:S(2)}) collective-permute-start(bf16[1,8,128,128]{3,2,1,0:T(8,128)(2,1)S(1)} %copy-done), channel_id=1, source_target_pairs={{0,4},{1,5},{2,6},{3,7},{4,0},{5,1},{6,2},{7,3},{8,12},{9,13},{10,... | collective-permute-start | bytes 786440 | tf_op jit(solution)/shard_map/ppermute | solution.py:331
  10.6 11.0 %collective-permute-start.4 = (bf16[1,8,128,128]{3,2,1,0:T(8,128)(2,1)S(1)}, bf16[1,8,128,128]{3,2,1,0:T(8,128)(2,1)S(1)}, u32[]{:S(2)}, u32[]{:S(2)}) collective-permute-start(bf16[1,8,128,128]{3,2,1,0:T(8,128)(2,1)S(1)} %copy-done), channel_id=1, source_target_pairs={{0,2},{1,3},{2,0},{3,1},{4,6},{5,7},{6,4},{7,5},{8,10},{9,11},{10,... | collective-permute-start | bytes 786440 | tf_op jit(solution)/shard_map/ppermute | solution.py:331
  12.7 8.8 %collective-permute-start = (bf16[1,8,32,128]{3,2,1,0:T(8,128)(2,1)S(1)}, bf16[1,8,32,128]{3,2,1,0:T(8,128)(2,1)S(1)}, u32[]{:S(2)}, u32[]{:S(2)}) collective-permute-start(bf16[1,8,32,128]{3,2,1,0:T(8,128)(2,1)S(1)} %copy-done.1), channel_id=1, source_target_pairs={{0,1},{1,0},{2,3},{3,2},{4,5},{5,4},{6,7},{7,6},{8,9},{9,8},{10,11... | collective-permute-start | bytes 196616 | tf_op jit(solution)/shard_map/ppermute | solution.py:331
  17.5 9.6 %all-to-all-start = ((f32[4,8,128]{2,1,0:T(8,128)}), f32[4,8,128]{2,1,0:T(8,128)S(1)}, u32[]{:S(2)}, u32[]{:S(2)}) async-start(f32[4,8,128]{2,1,0:T(8,128)} %score_memory.1), calls=%async_computation | async-start | bytes 32768 | tf_op jit(solution)/shard_map/all_to_all | solution.py:340
  22.4 4.7 %collective-permute-start.7 = (f32[8,128]{1,0:T(8,128)S(1)}, f32[8,128]{1,0:T(8,128)S(1)}, u32[]{:S(2)}, u32[]{:S(2)}) collective-permute-start(f32[8,128]{1,0:T(8,128)S(1)} %score_batch.2), channel_id=1, source_target_pairs={{0,1},{1,0},{2,3},{3,2},{4,5},{5,4},{6,7},{7,6},{8,9},{9,8},{10,11... | collective-permute-start | bytes 12296 | tf_op jit(solution)/shard_map/ppermute | solution.py:331

commit v6 on v2

--- a/solution.py
+++ b/solution.py
@@ -13,6 +13,8 @@
 CHUNK = 32
 LIST_ROWS = 16
 STEP = 4
+PACK_FLOPS = 10**10
+PACK_BYTES = 2**24
 
 
 def in_hbm(array):
@@ -33,14 +35,17 @@
 def token_sum(best, queries):
     tokens = best.shape[1]
     per_query = tokens // queries
-    row = lax.broadcasted_iota(jnp.int32, (max(queries, 8), tokens), 0)
-    col = lax.broadcasted_iota(jnp.int32, (max(queries, 8), tokens), 1)
-    own = (col // per_query == row).astype(jnp.float32)
+    row = lax.broadcasted_iota(jnp.int32, (queries, tokens), 0)
+    col = lax.broadcasted_iota(jnp.int32, (queries, tokens), 1)
+    own = (col // per_query == row).astype(jnp.bfloat16)
+    high = best.astype(jnp.bfloat16)
+    rest = best - high.astype(jnp.float32)
+    middle = rest.astype(jnp.bfloat16)
+    low = (rest - middle.astype(jnp.float32)).astype(jnp.bfloat16)
     return lax.dot_general(
-        own,
-        best,
+        jnp.concatenate([own] * 3, axis=1),
+        jnp.concatenate([high, middle, low], axis=1),
         (((1,), (1,)), ((), ())),
-        precision=lax.Precision.HIGHEST,
         preferred_element_type=jnp.float32,
     )
 
@@ -97,30 +102,23 @@
         in_specs=[vmem, vmem, pl.BlockSpec(memory_space=pltpu.SMEM)],
         out_shape=jax.ShapeDtypeStruct((q_count * (q_tokens + 2), depth), queries.dtype),
         compiler_params=pltpu.CompilerParams(vmem_limit_bytes=4 * MIB),
+        cost_estimate=pl.CostEstimate(
+            flops=PACK_FLOPS, bytes_accessed=PACK_BYTES, transcendentals=0
+        ),
         name="pack",
     )(in_hbm(queries), in_hbm(candidates), in_hbm(counts))
 
 
 def memory_kernel(shards, slots, *refs):
-    packed_refs, memory_ref = refs[:shards], refs[shards]
+    packed_refs, passage_ref = refs[:shards], refs[shards].at[0]
     out_refs = refs[shards + 1 : 2 * shards + 1]
-    passage_ref, query_ref, rank_ref, best_ref, left_best_ref, *refs = refs[2 * shards + 1 :]
-    list_ref, scalar_ref, left_ref, left_scalar_ref, copy_sems, list_sems = refs
+    query_ref, rank_ref, best_ref, left_best_ref, *refs = refs[2 * shards + 1 :]
+    list_ref, scalar_ref, left_ref, left_scalar_ref, list_sems = refs
     q_count = out_refs[0].shape[0]
     p_count = passage_ref.shape[0]
     total, q_tokens, depth = (size // parts for size, parts in zip(query_ref.shape, (2, 1, 2)))
     half = p_count // 2
     chunks = half // CHUNK
-
-    def fetch(chunk, side):
-        rows = pl.ds(pl.multiple_of(side * half + chunk * CHUNK, CHUNK), CHUNK)
-        return pltpu.make_async_copy(
-            memory_ref.at[0, rows], passage_ref.at[rows], copy_sems.at[chunk, side]
-        )
-
-    for chunk in range(chunks):
-        for side in range(2):
-            fetch(chunk, side).start()
 
     me = lax.axis_index("memory").astype(jnp.float32)
     keys = []
@@ -213,8 +211,6 @@
 
     @pl.loop(0, chunks)
     def _(chunk):
-        for side in range(2):
-            fetch(chunk, side).wait()
         for start in range(0, CHUNK, 8):
             first = pl.multiple_of(chunk * CHUNK + start, 8)
             rows = [unit(first + offset, scalar_ref, first + offset) for offset in range(8)]
@@ -257,11 +253,10 @@
     vmem = pl.BlockSpec(memory_space=pltpu.VMEM)
     return pl.pallas_call(
         functools.partial(memory_kernel, shards, slots),
-        in_specs=[vmem] * shards + [pl.BlockSpec(memory_space=pltpu.HBM)],
+        in_specs=[vmem] * (shards + 1),
         out_specs=[vmem] * shards,
         out_shape=[jax.ShapeDtypeStruct((q_count, p_count), jnp.float32)] * shards,
         scratch_shapes=[
-            pltpu.VMEM((p_count, p_tokens, depth), memory.dtype),
             pltpu.VMEM((2 * total, q_tokens, 2 * depth), memory.dtype),
             pltpu.VMEM((total, p_count), jnp.float32),
             pltpu.VMEM((p_count // 2, SLOTS * q_tokens), jnp.float32),
@@ -270,29 +265,28 @@
             pltpu.SMEM((LIST_ROWS, p_count), jnp.int32),
             pltpu.VMEM((LIST_ROWS, p_count), jnp.int32),
             pltpu.SMEM((LIST_ROWS, p_count), jnp.int32),
-            pltpu.SemaphoreType.DMA((p_count // 2 // CHUNK, 2)),
             pltpu.SemaphoreType.DMA((2,)),
         ],
-        compiler_params=pltpu.CompilerParams(vmem_limit_bytes=20 * MIB),
+        compiler_params=pltpu.CompilerParams(vmem_limit_bytes=16 * MIB),
         cost_estimate=pl.CostEstimate(
             flops=2 * total * q_tokens * p_count * p_tokens * depth,
             bytes_accessed=2 * p_count * p_tokens * depth,
             transcendentals=0,
         ),
         name="score_memory",
-    )(*packed, in_hbm(memory))
+    )(*packed, memory)
 
 
 def batch_kernel(query_ref, *refs):
     passage_refs, (out_ref, best_ref) = refs[:-2], refs[-2:]
     _, queries, q_tokens, depth = query_ref.shape
     count = passage_refs[0].shape[1]
-    if len(passage_refs) * count < best_ref.shape[0]:
-        best_ref[...] = jnp.zeros_like(best_ref)
     tokens = query_ref[0].reshape(queries * q_tokens, depth)
     for chip, passage_ref in enumerate(passage_refs):
         best_ref[chip * count : (chip + 1) * count, :] = token_max(passage_ref[0], tokens)
-    out_ref[...] = token_sum(best_ref[...], queries)
+    sums = token_sum(best_ref[...], queries)
+    empty = jnp.zeros((queries, out_ref.shape[1] - sums.shape[1]), jnp.float32)
+    out_ref[...] = jnp.concatenate([sums, empty], axis=1) if empty.size else sums
 
 
 def score_batch(queries, positives):
@@ -303,7 +297,7 @@
     return pl.pallas_call(
         batch_kernel,
         out_shape=jax.ShapeDtypeStruct((q_count, lanes), jnp.float32),
-        scratch_shapes=[pltpu.VMEM((lanes, q_count * q_tokens), jnp.float32)],
+        scratch_shapes=[pltpu.VMEM((chips * p_count, q_count * q_tokens), jnp.float32)],
         compiler_params=pltpu.CompilerParams(vmem_limit_bytes=16 * MIB),
         cost_estimate=pl.CostEstimate(
             flops=2 * chips * q_count * q_tokens * p_count * p_tokens * depth,

time: 25.8 us -> 25.5 us (0.988)
  Pallas kernels: 8.28 us -> 7.95 us
    pallas_call x1, Pallas kernels: 4.92 us -> 4.48 us  [score_memory(): pl.pallas_call(functools.partial(memory_kernel, shards, slots), in_specs=...]
  transfers between devices with their start and end apart: 11 -> 11, of which waited for: 2 -> 2; matrix products, arithmetic and copies ran while one was open for 0% -> 0% of each run, Pallas kernels for 26% -> 24%
where the time goes in v6:
time: 25.5 us; the launch traced here: 25.4 us
  starting transfers between devices  14.3 us (56%)
  Pallas kernels  7.95 us (31%)
  waiting for transfers between devices  2.37 us (9%)
  between operations  0.73 us (3%)
    ppermute x6, starting transfers between devices, to_shard(): return lax.ppermute(array, 'memory', [(i, i ^ step) for i in range(shards)])  10.2 us
    pallas_call x1, Pallas kernels, score_memory(): pl.pallas_call(functools.partial(memory_kernel, shards, slots), in_specs=...  4.48 us
    ppermute x5, starting transfers between devices, to_group(): return lax.ppermute(array, 'group', [(i, i ^ step) for i in range(groups)])  4.1 us
    ppermute x6, waiting for transfers between devices, to_shard(): return lax.ppermute(array, 'memory', [(i, i ^ step) for i in range(shards)])  2.36 us
    pallas_call x2, Pallas kernels, score_batch(): pl.pallas_call(batch_kernel, out_shape=jax.ShapeDtypeStruct((q_count, lan...  1.64 us
    pallas_call x1, Pallas kernels, pack(): pl.pallas_call(functools.partial(pack_kernel, p_count), in_specs=[vmem, v...  1.02 us
    pallas_call x1, Pallas kernels, finish(): pl.pallas_call(functools.partial(loss_kernel, len(memory_parts)), out_sha...  0.8 us
  transfers between devices with their start and end apart: 11, of which 2 were waited for; matrix products, arithmetic and copies ran while one was open for 0% of the time, Pallas kernels for 24%

profile of v6, /device:TPU:0, one launch (start us, length us, event | category | flops | bytes accessed | tf_op | source)
XLA Modules:
  0.0 25.4 jit_solution(3267021651158478336)
XLA Ops:
  0.6 0.0 copy-start.1
  0.6 0.0 copy-start
  0.7 0.0 copy-start.4
  0.7 1.0 %pack.1.refs_0_ = bf16[272,128]{1,0:T(8,128)(2,1)S(1)} custom-call(bf16[1,8,32,128]{3,2,1,0:T(8,128)(2,1)} %query_ref.2, s32[1,8,64]{2,1,0:T(8,128)} %refs_4_.3, s32[1,8]{1,0:T(1,128)} %refs_5_.1), custom_call_target="tpu_custom_call" | custom-call | flops 10000000000 | bytes 16777216 | tf_op jit(solution)/shard_map/pack/pallas_call | solution.py:100
  1.7 0.0 copy-start.2
  1.7 0.0 copy-start.3
  1.7 5.1 %collective-permute-start.3 = (bf16[272,128]{1,0:T(8,128)(2,1)S(1)}, bf16[272,128]{1,0:T(8,128)(2,1)S(1)}, u32[]{:S(2)}, u32[]{:S(2)}) collective-permute-start(bf16[272,128]{1,0:T(8,128)(2,1)S(1)} %pack.1.refs_0_), channel_id=1, source_target_pairs={{0,24},{8,16},{16,8},{24,0},{1,25},{9,17},{17,9},{25,1},{2,26},{10... | collective-permute-start | bytes 208904 | tf_op jit(solution)/shard_map/ppermute | solution.py:377
  6.8 0.0 collective-permute-start.2
  6.8 0.6 %collective-permute-start.1 = (bf16[272,128]{1,0:T(8,128)(2,1)S(1)}, bf16[272,128]{1,0:T(8,128)(2,1)S(1)}, u32[]{:S(2)}, u32[]{:S(2)}) collective-permute-start(bf16[272,128]{1,0:T(8,128)(2,1)S(1)} %pack.1.refs_0_), channel_id=1, source_target_pairs={{0,8},{8,0},{16,24},{24,16},{1,9},{9,1},{17,25},{25,17},{2,10},{10... | collective-permute-start | bytes 208904 | tf_op jit(solution)/shard_map/ppermute | solution.py:377
  7.5 2.6 %collective-permute-start.6 = (bf16[1,8,128,128]{3,2,1,0:T(8,128)(2,1)S(1)}, bf16[1,8,128,128]{3,2,1,0:T(8,128)(2,1)S(1)}, u32[]{:S(2)}, u32[]{:S(2)}) collective-permute-start(bf16[1,8,128,128]{3,2,1,0:T(8,128)(2,1)S(1)} %copy-done), channel_id=1, source_target_pairs={{0,6},{1,7},{2,4},{3,5},{4,2},{5,3},{6,0},{7,1},{8,14},{9,15},{10,... | collective-permute-start | bytes 786440 | tf_op jit(solution)/shard_map/ppermute | solution.py:380
  10.1 0.5 %collective-permute-start.5 = (bf16[1,8,128,128]{3,2,1,0:T(8,128)(2,1)S(1)}, bf16[1,8,128,128]{3,2,1,0:T(8,128)(2,1)S(1)}, u32[]{:S(2)}, u32[]{:S(2)}) collective-permute-start(bf16[1,8,128,128]{3,2,1,0:T(8,128)(2,1)S(1)} %copy-done), channel_id=1, source_target_pairs={{0,4},{1,5},{2,6},{3,7},{4,0},{5,1},{6,2},{7,3},{8,12},{9,13},{10,... | collective-permute-start | bytes 786440 | tf_op jit(solution)/shard_map/ppermute | solution.py:380
  10.6 0.0 collective-permute-done.3.refs_3_
  10.6 0.8 %collective-permute-start.4 = (bf16[1,8,128,128]{3,2,1,0:T(8,128)(2,1)S(1)}, bf16[1,8,128,128]{3,2,1,0:T(8,128)(2,1)S(1)}, u32[]{:S(2)}, u32[]{:S(2)}) collective-permute-start(bf16[1,8,128,128]{3,2,1,0:T(8,128)(2,1)S(1)} %copy-done), channel_id=1, source_target_pairs={{0,2},{1,3},{2,0},{3,1},{4,6},{5,7},{6,4},{7,5},{8,10},{9,11},{10,... | collective-permute-start | bytes 786440 | tf_op jit(solution)/shard_map/ppermute | solution.py:380
  11.3 1.4 %collective-permute-done.2.refs_2_ = bf16[272,128]{1,0:T(8,128)(2,1)S(1)} collective-permute-done((bf16[272,128]{1,0:T(8,128)(2,1)S(1)}, bf16[272,128]{1,0:T(8,128)(2,1)S(1)}, u32[]{:S(2)}, u32[]{:S(2)}) %collective-permute-start.2) | collective-permute-done | bytes 69664 | tf_op jit(solution)/shard_map/ppermute | solution.py:377
  12.7 0.0 collective-permute-start
  12.7 0.0 collective-permute-done.1.refs_1_
  12.8 4.5 %score_memory.1 = (f32[8,128]{1,0:T(8,128)S(1)}, f32[8,128]{1,0:T(8,128)S(1)}, f32[8,128]{1,0:T(8,128)S(1)}, f32[8,128]{1,0:T(8,128)S(1)}) custom-call(bf16[272,128]{1,0:T(8,128)(2,1)S(1)} %pack.1.refs_0_, bf16[272,128]{1,0:T(8,128)(2,1)S(1)} %collective-permute-done.1.refs_1_, bf16[272,128]{1,0:T(8,128)(2,1)S(1)} %collective-permute-done.2.refs_2_, ...), custom_call_target="tpu_custom_call" | custom-call | flops 4294967296 | bytes 4194304 | tf_op jit(solution)/shard_map/score_memory/pallas_call | solution.py:254
  17.2 0.0 collective-permute-done.query_ref
  17.3 2.8 %collective-permute-start.8 = (f32[8,128]{1,0:T(8,128)S(1)}, f32[8,128]{1,0:T(8,128)S(1)}, u32[]{:S(2)}, u32[]{:S(2)}) collective-permute-start(f32[8,128]{1,0:T(8,128)S(1)} %get-tuple-element.16), channel_id=1, source_target_pairs={{0,24},{8,16},{16,8},{24,0},{1,25},{9,17},{17,9},{25,1},{2,26},{10... | collective-permute-start | bytes 12296 | tf_op jit(solution)/shard_map/ppermute | solution.py:377
  20.0 0.3 %collective-permute-start.9 = (f32[8,128]{1,0:T(8,128)S(1)}, f32[8,128]{1,0:T(8,128)S(1)}, u32[]{:S(2)}, u32[]{:S(2)}) collective-permute-start(f32[8,128]{1,0:T(8,128)S(1)} %get-tuple-element.17), channel_id=1, source_target_pairs={{0,16},{8,24},{16,0},{24,8},{1,17},{9,25},{17,1},{25,9},{2,18},{10... | collective-permute-start | bytes 12296 | tf_op jit(solution)/shard_map/ppermute | solution.py:377
  20.4 0.0 collective-permute-done.6.refs_3_
  20.4 1.3 %collective-permute-start.10 = (f32[8,128]{1,0:T(8,128)S(1)}, f32[8,128]{1,0:T(8,128)S(1)}, u32[]{:S(2)}, u32[]{:S(2)}) collective-permute-start(f32[8,128]{1,0:T(8,128)S(1)} %get-tuple-element.18), channel_id=1, source_target_pairs={{0,8},{8,0},{16,24},{24,16},{1,9},{9,1},{17,25},{25,17},{2,10},{10... | collective-permute-start | bytes 12296 | tf_op jit(solution)/shard_map/ppermute | solution.py:377
  21.7 0.0 collective-permute-done.5.refs_2_
  21.7 0.0 collective-permute-done.4.refs_1_
  21.7 0.8 %score_batch.2 = f32[8,128]{1,0:T(8,128)S(1)} custom-call(bf16[1,8,32,128]{3,2,1,0:T(8,128)(2,1)S(1)} %collective-permute-done.query_ref, bf16[1,8,128,128]{3,2,1,0:T(8,128)(2,1)S(1)} %copy-done, bf16[1,8,128,128]{3,2,1,0:T(8,128)(2,1)S(1)} %collective-permute-done.4.refs_1_, bf16[1,8,128,128]{3,2,1,0:T(8,128)(2,1)S(1)} %collective-permute-done.5.refs_2_, ...), custom_call_target="tpu_custom_call" | custom-call | flops 268435456 | bytes 1048576 | tf_op jit(solution)/shard_map/score_batch/pallas_call | solution.py:297
  22.5 0.2 collective-permute-start.7
  22.8 0.8 %score_batch.3.own_batch = f32[8,128]{1,0:T(8,128)S(1)} custom-call(bf16[1,8,32,128]{3,2,1,0:T(8,128)(2,1)S(1)} %copy-done.1, bf16[1,8,128,128]{3,2,1,0:T(8,128)(2,1)S(1)} %copy-done, bf16[1,8,128,128]{3,2,1,0:T(8,128)(2,1)S(1)} %collective-permute-done.4.refs_1_, bf16[1,8,128,128]{3,2,1,0:T(8,128)(2,1)S(1)} %collective-permute-done.5.refs_2_, ...), custom_call_target="tpu_custom_call" | custom-call | flops 268435456 | bytes 1048576 | tf_op jit(solution)/shard_map/score_batch/pallas_call | solution.py:297
  23.6 0.0 collective-permute-done.8.refs_1_
  23.6 1.0 %collective-permute-done.9.refs_2_ = f32[8,128]{1,0:T(8,128)S(1)} collective-permute-done((f32[8,128]{1,0:T(8,128)S(1)}, f32[8,128]{1,0:T(8,128)S(1)}, u32[]{:S(2)}, u32[]{:S(2)}) %collective-permute-start.9) | collective-permute-done | bytes 4128 | tf_op jit(solution)/shard_map/ppermute | solution.py:377
  24.6 0.0 collective-permute-done.10.refs_3_
  24.6 0.0 collective-permute-done.7.mate_batch
  24.6 0.8 %finish.1 = (f32[1,8,64]{2,1,0:T(8,128)}, f32[1,8,64]{2,1,0:T(8,128)}, f32[1,8]{1,0:T(1,128)}) custom-call(f32[8,128]{1,0:T(8,128)S(1)} %score_batch.3.own_batch, f32[8,128]{1,0:T(8,128)S(1)} %collective-permute-done.7.mate_batch, f32[8,128]{1,0:T(8,128)S(1)} %get-tuple-element.12.refs_0_, f32[8,128]{1,0:T(8,128)S(1)} %collective-permute-done.8.refs_1_, ...), custom_call_target="tpu_custom_call" | custom-call | tf_op jit(solution)/shard_map/finish/pallas_call | solution.py:357
  (5 shorter events, 0.0 us)
Async XLA Ops:
  0.6 12.1 %copy-start.1 = (bf16[1,8,32,128]{3,2,1,0:T(8,128)(2,1)S(1)}, bf16[1,8,32,128]{3,2,1,0:T(8,128)(2,1)}, u32[]{:S(2)}) copy-start(bf16[1,8,32,128]{3,2,1,0:T(8,128)(2,1)} %query_ref.2) | copy-start | bytes 196612
  0.6 6.8 %copy-start = (bf16[1,8,128,128]{3,2,1,0:T(8,128)(2,1)S(1)}, bf16[1,8,128,128]{3,2,1,0:T(8,128)(2,1)}, u32[]{:S(2)}) copy-start(bf16[1,8,128,128]{3,2,1,0:T(8,128)(2,1)} %refs_0_.3) | copy-start | bytes 786436
  0.7 12.1 %copy-start.4 = (bf16[1,128,128,128]{3,2,1,0:T(8,128)(2,1)S(1)}, bf16[1,128,128,128]{3,2,1,0:T(8,128)(2,1)}, u32[]{:S(2)}) copy-start(bf16[1,128,128,128]{3,2,1,0:T(8,128)(2,1)} %refs_4_.2) | copy-start | bytes 12582916
  1.7 22.9 %copy-start.2 = (s32[1,8,64]{2,1,0:T(8,128)S(1)}, s32[1,8,64]{2,1,0:T(8,128)}, u32[]{:S(2)}) copy-start(s32[1,8,64]{2,1,0:T(8,128)} %refs_4_.3) | copy-start | bytes 6148
  1.7 22.9 %copy-start.3 = (s32[1,8]{1,0:T(1,128)S(1)}, s32[1,8]{1,0:T(1,128)}, u32[]{:S(2)}) copy-start(s32[1,8]{1,0:T(1,128)} %refs_5_.1) | copy-start | bytes 100
  1.7 8.9 %collective-permute-start.3 = (bf16[272,128]{1,0:T(8,128)(2,1)S(1)}, bf16[272,128]{1,0:T(8,128)(2,1)S(1)}, u32[]{:S(2)}, u32[]{:S(2)}) collective-permute-start(bf16[272,128]{1,0:T(8,128)(2,1)S(1)} %pack.1.refs_0_), channel_id=1, source_target_pairs={{0,24},{8,16},{16,8},{24,0},{1,25},{9,17},{17,9},{25,1},{2,26},{10... | collective-permute-start | bytes 208904 | tf_op jit(solution)/shard_map/ppermute | solution.py:377
  6.8 5.9 %collective-permute-start.2 = (bf16[272,128]{1,0:T(8,128)(2,1)S(1)}, bf16[272,128]{1,0:T(8,128)(2,1)S(1)}, u32[]{:S(2)}, u32[]{:S(2)}) collective-permute-start(bf16[272,128]{1,0:T(8,128)(2,1)S(1)} %pack.1.refs_0_), channel_id=1, source_target_pairs={{0,16},{8,24},{16,0},{24,8},{1,17},{9,25},{17,1},{25,9},{2,18},{10... | collective-permute-start | bytes 208904 | tf_op jit(solution)/shard_map/ppermute | solution.py:377
  6.8 5.9 %collective-permute-start.1 = (bf16[272,128]{1,0:T(8,128)(2,1)S(1)}, bf16[272,128]{1,0:T(8,128)(2,1)S(1)}, u32[]{:S(2)}, u32[]{:S(2)}) collective-permute-start(bf16[272,128]{1,0:T(8,128)(2,1)S(1)} %pack.1.refs_0_), channel_id=1, source_target_pairs={{0,8},{8,0},{16,24},{24,16},{1,9},{9,1},{17,25},{25,17},{2,10},{10... | collective-permute-start | bytes 208904 | tf_op jit(solution)/shard_map/ppermute | solution.py:377
  7.5 12.9 %collective-permute-start.6 = (bf16[1,8,128,128]{3,2,1,0:T(8,128)(2,1)S(1)}, bf16[1,8,128,128]{3,2,1,0:T(8,128)(2,1)S(1)}, u32[]{:S(2)}, u32[]{:S(2)}) collective-permute-start(bf16[1,8,128,128]{3,2,1,0:T(8,128)(2,1)S(1)} %copy-done), channel_id=1, source_target_pairs={{0,6},{1,7},{2,4},{3,5},{4,2},{5,3},{6,0},{7,1},{8,14},{9,15},{10,... | collective-permute-start | bytes 786440 | tf_op jit(solution)/shard_map/ppermute | solution.py:380
  10.1 11.7 %collective-permute-start.5 = (bf16[1,8,128,128]{3,2,1,0:T(8,128)(2,1)S(1)}, bf16[1,8,128,128]{3,2,1,0:T(8,128)(2,1)S(1)}, u32[]{:S(2)}, u32[]{:S(2)}) collective-permute-start(bf16[1,8,128,128]{3,2,1,0:T(8,128)(2,1)S(1)} %copy-done), channel_id=1, source_target_pairs={{0,4},{1,5},{2,6},{3,7},{4,0},{5,1},{6,2},{7,3},{8,12},{9,13},{10,... | collective-permute-start | bytes 786440 | tf_op jit(solution)/shard_map/ppermute | solution.py:380
  10.6 11.2 %collective-permute-start.4 = (bf16[1,8,128,128]{3,2,1,0:T(8,128)(2,1)S(1)}, bf16[1,8,128,128]{3,2,1,0:T(8,128)(2,1)S(1)}, u32[]{:S(2)}, u32[]{:S(2)}) collective-permute-start(bf16[1,8,128,128]{3,2,1,0:T(8,128)(2,1)S(1)} %copy-done), channel_id=1, source_target_pairs={{0,2},{1,3},{2,0},{3,1},{4,6},{5,7},{6,4},{7,5},{8,10},{9,11},{10,... | collective-permute-start | bytes 786440 | tf_op jit(solution)/shard_map/ppermute | solution.py:380
  12.7 4.5 %collective-permute-start = (bf16[1,8,32,128]{3,2,1,0:T(8,128)(2,1)S(1)}, bf16[1,8,32,128]{3,2,1,0:T(8,128)(2,1)S(1)}, u32[]{:S(2)}, u32[]{:S(2)}) collective-permute-start(bf16[1,8,32,128]{3,2,1,0:T(8,128)(2,1)S(1)} %copy-done.1), channel_id=1, source_target_pairs={{0,1},{1,0},{2,3},{3,2},{4,5},{5,4},{6,7},{7,6},{8,9},{9,8},{10,11... | collective-permute-start | bytes 196616 | tf_op jit(solution)/shard_map/ppermute | solution.py:380
  17.3 6.3 %collective-permute-start.8 = (f32[8,128]{1,0:T(8,128)S(1)}, f32[8,128]{1,0:T(8,128)S(1)}, u32[]{:S(2)}, u32[]{:S(2)}) collective-permute-start(f32[8,128]{1,0:T(8,128)S(1)} %get-tuple-element.16), channel_id=1, source_target_pairs={{0,24},{8,16},{16,8},{24,0},{1,25},{9,17},{17,9},{25,1},{2,26},{10... | collective-permute-start | bytes 12296 | tf_op jit(solution)/shard_map/ppermute | solution.py:377
  20.0 4.5 %collective-permute-start.9 = (f32[8,128]{1,0:T(8,128)S(1)}, f32[8,128]{1,0:T(8,128)S(1)}, u32[]{:S(2)}, u32[]{:S(2)}) collective-permute-start(f32[8,128]{1,0:T(8,128)S(1)} %get-tuple-element.17), channel_id=1, source_target_pairs={{0,16},{8,24},{16,0},{24,8},{1,17},{9,25},{17,1},{25,9},{2,18},{10... | collective-permute-start | bytes 12296 | tf_op jit(solution)/shard_map/ppermute | solution.py:377
  20.4 4.2 %collective-permute-start.10 = (f32[8,128]{1,0:T(8,128)S(1)}, f32[8,128]{1,0:T(8,128)S(1)}, u32[]{:S(2)}, u32[]{:S(2)}) collective-permute-start(f32[8,128]{1,0:T(8,128)S(1)} %get-tuple-element.18), channel_id=1, source_target_pairs={{0,8},{8,0},{16,24},{24,16},{1,9},{9,1},{17,25},{25,17},{2,10},{10... | collective-permute-start | bytes 12296 | tf_op jit(solution)/shard_map/ppermute | solution.py:377
  22.5 2.0 %collective-permute-start.7 = (f32[8,128]{1,0:T(8,128)S(1)}, f32[8,128]{1,0:T(8,128)S(1)}, u32[]{:S(2)}, u32[]{:S(2)}) collective-permute-start(f32[8,128]{1,0:T(8,128)S(1)} %score_batch.2), channel_id=1, source_target_pairs={{0,1},{1,0},{2,3},{3,2},{4,5},{5,4},{6,7},{7,6},{8,9},{9,8},{10,11... | collective-permute-start | bytes 12296 | tf_op jit(solution)/shard_map/ppermute | solution.py:380

commit v7 on v4

--- a/solution.py
+++ b/solution.py
@@ -104,10 +104,12 @@
 
 
 def memory_kernel(shards, slots, *refs):
-    packed_refs, passage_ref = refs[:shards], refs[shards].at[0]
-    out_refs = refs[shards + 1 : 2 * shards + 1]
-    query_ref, rank_ref, best_ref, list_ref, scalar_ref, list_sem = refs[2 * shards + 1 :]
-    q_count = out_refs[0].shape[0]
+    packed_refs, passage_ref = refs[shards - 1 :: -1], refs[shards].at[0]
+    pairs = shards // 2
+    pair_refs = refs[shards + pairs : shards : -1]
+    query_ref, rank_ref, best_ref, list_ref, scalar_ref, list_sem = refs[shards + 1 + pairs :]
+    out_refs = [pair_ref.at[index] for pair_ref in pair_refs for index in range(2)]
+    q_count = pair_refs[0].shape[1]
     p_count = passage_ref.shape[0]
     total, q_tokens, depth = query_ref.shape
     chunks = p_count // CHUNK
@@ -208,8 +210,8 @@
     return pl.pallas_call(
         functools.partial(memory_kernel, shards, slots),
         in_specs=[vmem] * (shards + 1),
-        out_specs=[vmem] * shards,
-        out_shape=[jax.ShapeDtypeStruct((q_count, p_count), jnp.float32)] * shards,
+        out_specs=[vmem] * (shards // 2),
+        out_shape=[jax.ShapeDtypeStruct((2, q_count, p_count), jnp.float32)] * (shards // 2),
         scratch_shapes=[
             pltpu.VMEM((total, q_tokens, depth), memory.dtype),
             pltpu.VMEM((total, p_count), jnp.float32),
@@ -260,8 +262,12 @@
 
 
 def loss_kernel(shards, own_batch, mate_batch, *refs):
-    memory_refs = refs[:shards]
+    pairs = shards // 2 - 1
+    far_refs, near_refs, hop_refs = refs[:pairs], refs[pairs : pairs + 2], refs[pairs + 2 : shards]
     candidate_ref, count_ref, batch_ref, memory_ref, loss_ref = refs[shards:]
+    memory_refs = [near_refs[0].at[0], near_refs[1].at[1]]
+    for far_ref, hop_ref in zip(far_refs, hop_refs):
+        memory_refs += [far_ref.at[0], hop_ref.at[1]]
     group, shard = lax.axis_index("group"), lax.axis_index("memory")
     chip, core = group // 2, group % 2
     _, q_count, slots = candidate_ref.shape
@@ -284,7 +290,7 @@
     holder, local = padded // p_count, padded % p_count
     picked = jnp.zeros((q_count, p_count), jnp.float32)
     for step in range(shards):
-        found = jnp.take_along_axis(memory_refs[-step][...], local, axis=1)
+        found = jnp.take_along_axis(memory_refs[step][...], local, axis=1)
         picked = jnp.where(holder == (shard ^ step), found, picked)
 
     valid = lax.broadcasted_iota(jnp.int32, (q_count, p_count), 1) < column_of(count_ref[...])
@@ -331,22 +337,23 @@
         return lax.ppermute(array, "group", [(i, i ^ step) for i in range(groups)])
 
     own = pack(queries, candidates, counts, memory.shape[1])
-    packed = [own] + [to_shard(own, step) for step in range(1, shards)]
+    packed = [to_shard(own, step) for step in range(shards - 1, 0, -1)] + [own]
     sent_positives, sent_queries, _ = lax.optimization_barrier((positives, queries, own))
     row = [positives] + [to_group(sent_positives, 2 * step) for step in range(1, chips)]
     mate_queries = to_group(sent_queries, 1)
 
-    scores = score_memory(packed, memory, q_count, slots)
-    returned = [to_shard(scores[step], step) for step in range(shards - 1, 0, -1)]
-    mate_queries, _ = lax.optimization_barrier((mate_queries, scores[0]))
+    near, *pairs = score_memory(packed, memory, q_count, slots)[::-1]
+    far = [to_shard(pair, 2 * index) for index, pair in enumerate(pairs, start=1)]
+    near = [near, to_shard(near, 1)]
+    hops = [to_shard(pair, 1) for pair in far]
+    mate_queries, _ = lax.optimization_barrier((mate_queries, far))
     mate_scores = score_batch(mate_queries, row)
     mate_batch = to_group(mate_scores, 1)
     own_queries, _ = lax.optimization_barrier((queries, mate_scores))
     own_batch = score_batch(own_queries, row)
     columns = groups * q_count
-    return finish(
-        own_batch, mate_batch, [scores[0]] + returned, candidates, counts, columns
-    )
+    parts = far + near + hops
+    return finish(own_batch, mate_batch, parts, candidates, counts, columns)
 
 
 def solution(mesh):

time: 25.2 us -> 26.3 us (1.044)
  starting transfers between devices: 14.1 us -> 16.4 us
  waiting for transfers between devices: 2.56 us -> 1.48 us
    ppermute x6, starting transfers between devices: 10.2 us -> 11.5 us  [to_shard(): return lax.ppermute(array, 'memory', [(i, i ^ step) for i in range(shards)])]
    ppermute x6, waiting for transfers between devices: 2.35 us -> 1.36 us  [to_shard(): return lax.ppermute(array, 'memory', [(i, i ^ step) for i in range(shards)])]
    ppermute x5, starting transfers between devices: 3.88 us -> 4.83 us  [to_group(): return lax.ppermute(array, 'group', [(i, i ^ step) for i in range(groups)])]
  transfers between devices with their start and end apart: 11 -> 11, of which waited for: 4 -> 4; matrix products, arithmetic and copies ran while one was open for 0% -> 0% of each run, Pallas kernels for 23% -> 22%
where the time goes in v7:
time: 26.3 us; the launch traced here: 26.2 us
  starting transfers between devices  16.4 us (62%)
  Pallas kernels  7.63 us (29%)
  waiting for transfers between devices  1.48 us (6%)
  between operations  0.71 us (3%)
    ppermute x6, starting transfers between devices, to_shard(): return lax.ppermute(array, 'memory', [(i, i ^ step) for i in range(shards)])  11.5 us
    ppermute x5, starting transfers between devices, to_group(): return lax.ppermute(array, 'group', [(i, i ^ step) for i in range(groups)])  4.83 us
    pallas_call x1, Pallas kernels, score_memory(): pl.pallas_call(functools.partial(memory_kernel, shards, slots), in_specs=...  4.13 us
    pallas_call x2, Pallas kernels, score_batch(): pl.pallas_call(batch_kernel, out_shape=jax.ShapeDtypeStruct((q_count, lan...  1.69 us
    ppermute x6, waiting for transfers between devices, to_shard(): return lax.ppermute(array, 'memory', [(i, i ^ step) for i in range(shards)])  1.36 us
    pallas_call x1, Pallas kernels, pack(): pl.pallas_call(functools.partial(pack_kernel, p_count), in_specs=[vmem, v...  1.02 us
    pallas_call x1, Pallas kernels, finish(): pl.pallas_call(functools.partial(loss_kernel, len(memory_parts)), out_sha...  0.8 us
  transfers between devices with their start and end apart: 11, of which 4 were waited for; matrix products, arithmetic and copies ran while one was open for 0% of the time, Pallas kernels for 22%

profile of v7, /device:TPU:0, one launch (start us, length us, event | category | flops | bytes accessed | tf_op | source)
XLA Modules:
  0.0 26.2 jit_solution(11081537106379342506)
XLA Ops:
  0.6 0.0 copy-start.1
  0.6 0.0 copy-start
  0.7 1.0 %pack.1.refs_3_ = bf16[272,128]{1,0:T(8,128)(2,1)S(1)} custom-call(bf16[1,8,32,128]{3,2,1,0:T(8,128)(2,1)} %query_ref.2, s32[1,8,64]{2,1,0:T(8,128)} %refs_4_.3, s32[1,8]{1,0:T(1,128)} %refs_5_.1), custom_call_target="tpu_custom_call" | custom-call | flops 10000000000 | bytes 16777216 | tf_op jit(solution)/shard_map/pack/pallas_call | solution.py:94
  1.7 0.0 copy-start.2
  1.7 0.0 copy-start.3
  1.7 5.1 %collective-permute-start.1 = (bf16[272,128]{1,0:T(8,128)(2,1)S(1)}, bf16[272,128]{1,0:T(8,128)(2,1)S(1)}, u32[]{:S(2)}, u32[]{:S(2)}) collective-permute-start(bf16[272,128]{1,0:T(8,128)(2,1)S(1)} %pack.1.refs_3_), channel_id=1, source_target_pairs={{0,24},{8,16},{16,8},{24,0},{1,25},{9,17},{17,9},{25,1},{2,26},{10... | collective-permute-start | bytes 208904 | tf_op jit(solution)/shard_map/ppermute | solution.py:334
  6.8 0.0 collective-permute-start.2
  6.8 0.6 %collective-permute-start.3 = (bf16[272,128]{1,0:T(8,128)(2,1)S(1)}, bf16[272,128]{1,0:T(8,128)(2,1)S(1)}, u32[]{:S(2)}, u32[]{:S(2)}) collective-permute-start(bf16[272,128]{1,0:T(8,128)(2,1)S(1)} %pack.1.refs_3_), channel_id=1, source_target_pairs={{0,8},{8,0},{16,24},{24,16},{1,9},{9,1},{17,25},{25,17},{2,10},{10... | collective-permute-start | bytes 208904 | tf_op jit(solution)/shard_map/ppermute | solution.py:334
  7.5 1.6 %collective-permute-start.5 = (bf16[1,8,128,128]{3,2,1,0:T(8,128)(2,1)S(1)}, bf16[1,8,128,128]{3,2,1,0:T(8,128)(2,1)S(1)}, u32[]{:S(2)}, u32[]{:S(2)}) collective-permute-start(bf16[1,8,128,128]{3,2,1,0:T(8,128)(2,1)S(1)} %copy-done), channel_id=1, source_target_pairs={{0,2},{1,3},{2,0},{3,1},{4,6},{5,7},{6,4},{7,5},{8,10},{9,11},{10,... | collective-permute-start | bytes 786440 | tf_op jit(solution)/shard_map/ppermute | solution.py:337
  9.1 1.5 %collective-permute-start.6 = (bf16[1,8,128,128]{3,2,1,0:T(8,128)(2,1)S(1)}, bf16[1,8,128,128]{3,2,1,0:T(8,128)(2,1)S(1)}, u32[]{:S(2)}, u32[]{:S(2)}) collective-permute-start(bf16[1,8,128,128]{3,2,1,0:T(8,128)(2,1)S(1)} %copy-done), channel_id=1, source_target_pairs={{0,4},{1,5},{2,6},{3,7},{4,0},{5,1},{6,2},{7,3},{8,12},{9,13},{10,... | collective-permute-start | bytes 786440 | tf_op jit(solution)/shard_map/ppermute | solution.py:337
  10.6 0.0 collective-permute-done.1.refs_0_
  10.6 1.7 %collective-permute-start.7 = (bf16[1,8,128,128]{3,2,1,0:T(8,128)(2,1)S(1)}, bf16[1,8,128,128]{3,2,1,0:T(8,128)(2,1)S(1)}, u32[]{:S(2)}, u32[]{:S(2)}) collective-permute-start(bf16[1,8,128,128]{3,2,1,0:T(8,128)(2,1)S(1)} %copy-done), channel_id=1, source_target_pairs={{0,6},{1,7},{2,4},{3,5},{4,2},{5,3},{6,0},{7,1},{8,14},{9,15},{10,... | collective-permute-start | bytes 786440 | tf_op jit(solution)/shard_map/ppermute | solution.py:337
  12.3 0.4 %collective-permute-done.2.refs_1_ = bf16[272,128]{1,0:T(8,128)(2,1)S(1)} collective-permute-done((bf16[272,128]{1,0:T(8,128)(2,1)S(1)}, bf16[272,128]{1,0:T(8,128)(2,1)S(1)}, u32[]{:S(2)}, u32[]{:S(2)}) %collective-permute-start.2) | collective-permute-done | bytes 69664 | tf_op jit(solution)/shard_map/ppermute | solution.py:334
  12.7 0.0 collective-permute-start
  12.7 0.0 collective-permute-done.3.refs_2_
  12.8 4.1 %score_memory.1 = (f32[2,8,128]{2,1,0:T(8,128)S(1)}, f32[2,8,128]{2,1,0:T(8,128)S(1)}) custom-call(bf16[272,128]{1,0:T(8,128)(2,1)S(1)} %collective-permute-done.1.refs_0_, bf16[272,128]{1,0:T(8,128)(2,1)S(1)} %collective-permute-done.2.refs_1_, bf16[272,128]{1,0:T(8,128)(2,1)S(1)} %collective-permute-done.3.refs_2_, bf16[272,128]{1,0:T(8,128)(2,1)S(1)} %pack.1.refs_3_, ...), custom_call_target="tpu_custom_call" | custom-call | flops 4294967296 | bytes 4194304 | tf_op jit(solution)/shard_map/score_memory/pallas_call | solution.py:210
  16.9 3.1 %collective-permute-start.4 = (f32[2,8,128]{2,1,0:T(8,128)S(1)}, f32[2,8,128]{2,1,0:T(8,128)S(1)}, u32[]{:S(2)}, u32[]{:S(2)}) collective-permute-start(f32[2,8,128]{2,1,0:T(8,128)S(1)} %get-tuple-element.10), channel_id=1, source_target_pairs={{0,16},{8,24},{16,0},{24,8},{1,17},{9,25},{17,1},{25,9},{2,18},{10... | collective-permute-start | bytes 24584 | tf_op jit(solution)/shard_map/ppermute | solution.py:334
  20.0 0.0 collective-permute-done.query_ref
  20.0 0.9 %collective-permute-start.9 = (f32[2,8,128]{2,1,0:T(8,128)S(1)}, f32[2,8,128]{2,1,0:T(8,128)S(1)}, u32[]{:S(2)}, u32[]{:S(2)}) collective-permute-start(f32[2,8,128]{2,1,0:T(8,128)S(1)} %get-tuple-element.14.refs_1_), channel_id=1, source_target_pairs={{0,8},{8,0},{16,24},{24,16},{1,9},{9,1},{17,25},{25,17},{2,10},{10... | collective-permute-start | bytes 24584 | tf_op jit(solution)/shard_map/ppermute | solution.py:334
  20.9 0.7 %collective-permute-done.4.refs_0_ = f32[2,8,128]{2,1,0:T(8,128)S(1)} collective-permute-done((f32[2,8,128]{2,1,0:T(8,128)S(1)}, f32[2,8,128]{2,1,0:T(8,128)S(1)}, u32[]{:S(2)}, u32[]{:S(2)}) %collective-permute-start.4) | collective-permute-done | bytes 8224 | tf_op jit(solution)/shard_map/ppermute | solution.py:334
  21.6 1.7 %collective-permute-start.10 = (f32[2,8,128]{2,1,0:T(8,128)S(1)}, f32[2,8,128]{2,1,0:T(8,128)S(1)}, u32[]{:S(2)}, u32[]{:S(2)}) collective-permute-start(f32[2,8,128]{2,1,0:T(8,128)S(1)} %collective-permute-done.4.refs_0_), channel_id=1, source_target_pairs={{0,8},{8,0},{16,24},{24,16},{1,9},{9,1},{17,25},{25,17},{2,10},{10... | collective-permute-start | bytes 24584 | tf_op jit(solution)/shard_map/ppermute | solution.py:334
  23.4 0.0 collective-permute-done.5.refs_1_
  23.4 0.0 collective-permute-done.6.refs_2_
  23.4 0.0 collective-permute-done.7.refs_3_
  23.4 0.8 %score_batch.2 = f32[8,128]{1,0:T(8,128)S(1)} custom-call(bf16[1,8,32,128]{3,2,1,0:T(8,128)(2,1)S(1)} %collective-permute-done.query_ref, bf16[1,8,128,128]{3,2,1,0:T(8,128)(2,1)S(1)} %copy-done, bf16[1,8,128,128]{3,2,1,0:T(8,128)(2,1)S(1)} %collective-permute-done.5.refs_1_, bf16[1,8,128,128]{3,2,1,0:T(8,128)(2,1)S(1)} %collective-permute-done.6.refs_2_, ...), custom_call_target="tpu_custom_call" | custom-call | flops 268435456 | bytes 1048576 | tf_op jit(solution)/shard_map/score_batch/pallas_call | solution.py:250
  24.2 0.0 collective-permute-start.8
  24.2 0.9 %score_batch.3.own_batch = f32[8,128]{1,0:T(8,128)S(1)} custom-call(bf16[1,8,32,128]{3,2,1,0:T(8,128)(2,1)S(1)} %copy-done.1, bf16[1,8,128,128]{3,2,1,0:T(8,128)(2,1)S(1)} %copy-done, bf16[1,8,128,128]{3,2,1,0:T(8,128)(2,1)S(1)} %collective-permute-done.5.refs_1_, bf16[1,8,128,128]{3,2,1,0:T(8,128)(2,1)S(1)} %collective-permute-done.6.refs_2_, ...), custom_call_target="tpu_custom_call" | custom-call | flops 268435456 | bytes 1048576 | tf_op jit(solution)/shard_map/score_batch/pallas_call | solution.py:250
  25.1 0.0 collective-permute-done.9.refs_2_
  25.1 0.2 collective-permute-done.10.refs_3_
  25.3 0.1 collective-permute-done.8.mate_batch
  25.4 0.0 copy-done.2
  25.4 0.8 %finish.1 = (f32[1,8,64]{2,1,0:T(8,128)}, f32[1,8,64]{2,1,0:T(8,128)}, f32[1,8]{1,0:T(1,128)}) custom-call(f32[8,128]{1,0:T(8,128)S(1)} %score_batch.3.own_batch, f32[8,128]{1,0:T(8,128)S(1)} %collective-permute-done.8.mate_batch, f32[2,8,128]{2,1,0:T(8,128)S(1)} %collective-permute-done.4.refs_0_, f32[2,8,128]{2,1,0:T(8,128)S(1)} %get-tuple-element.14.refs_1_, ...), custom_call_target="tpu_custom_call" | custom-call | tf_op jit(solution)/shard_map/finish/pallas_call | solution.py:314
  (5 shorter events, 0.0 us)
Async XLA Ops:
  0.6 12.1 %copy-start.1 = (bf16[1,8,32,128]{3,2,1,0:T(8,128)(2,1)S(1)}, bf16[1,8,32,128]{3,2,1,0:T(8,128)(2,1)}, u32[]{:S(2)}) copy-start(bf16[1,8,32,128]{3,2,1,0:T(8,128)(2,1)} %query_ref.2) | copy-start | bytes 196612
  0.6 6.8 %copy-start = (bf16[1,8,128,128]{3,2,1,0:T(8,128)(2,1)S(1)}, bf16[1,8,128,128]{3,2,1,0:T(8,128)(2,1)}, u32[]{:S(2)}) copy-start(bf16[1,8,128,128]{3,2,1,0:T(8,128)(2,1)} %refs_0_.3) | copy-start | bytes 786436
  0.7 12.1 %copy-start.4 = (bf16[1,128,128,128]{3,2,1,0:T(8,128)(2,1)S(1)}, bf16[1,128,128,128]{3,2,1,0:T(8,128)(2,1)}, u32[]{:S(2)}) copy-start(bf16[1,128,128,128]{3,2,1,0:T(8,128)(2,1)} %refs_4_.2) | copy-start | bytes 12582916
  1.7 23.7 %copy-start.2 = (s32[1,8,64]{2,1,0:T(8,128)S(1)}, s32[1,8,64]{2,1,0:T(8,128)}, u32[]{:S(2)}) copy-start(s32[1,8,64]{2,1,0:T(8,128)} %refs_4_.3) | copy-start | bytes 6148
  1.7 23.7 %copy-start.3 = (s32[1,8]{1,0:T(1,128)S(1)}, s32[1,8]{1,0:T(1,128)}, u32[]{:S(2)}) copy-start(s32[1,8]{1,0:T(1,128)} %refs_5_.1) | copy-start | bytes 100
  1.7 8.9 %collective-permute-start.1 = (bf16[272,128]{1,0:T(8,128)(2,1)S(1)}, bf16[272,128]{1,0:T(8,128)(2,1)S(1)}, u32[]{:S(2)}, u32[]{:S(2)}) collective-permute-start(bf16[272,128]{1,0:T(8,128)(2,1)S(1)} %pack.1.refs_3_), channel_id=1, source_target_pairs={{0,24},{8,16},{16,8},{24,0},{1,25},{9,17},{17,9},{25,1},{2,26},{10... | collective-permute-start | bytes 208904 | tf_op jit(solution)/shard_map/ppermute | solution.py:334
  6.8 5.9 %collective-permute-start.2 = (bf16[272,128]{1,0:T(8,128)(2,1)S(1)}, bf16[272,128]{1,0:T(8,128)(2,1)S(1)}, u32[]{:S(2)}, u32[]{:S(2)}) collective-permute-start(bf16[272,128]{1,0:T(8,128)(2,1)S(1)} %pack.1.refs_3_), channel_id=1, source_target_pairs={{0,16},{8,24},{16,0},{24,8},{1,17},{9,25},{17,1},{25,9},{2,18},{10... | collective-permute-start | bytes 208904 | tf_op jit(solution)/shard_map/ppermute | solution.py:334
  6.8 5.9 %collective-permute-start.3 = (bf16[272,128]{1,0:T(8,128)(2,1)S(1)}, bf16[272,128]{1,0:T(8,128)(2,1)S(1)}, u32[]{:S(2)}, u32[]{:S(2)}) collective-permute-start(bf16[272,128]{1,0:T(8,128)(2,1)S(1)} %pack.1.refs_3_), channel_id=1, source_target_pairs={{0,8},{8,0},{16,24},{24,16},{1,9},{9,1},{17,25},{25,17},{2,10},{10... | collective-permute-start | bytes 208904 | tf_op jit(solution)/shard_map/ppermute | solution.py:334
  7.5 15.9 %collective-permute-start.5 = (bf16[1,8,128,128]{3,2,1,0:T(8,128)(2,1)S(1)}, bf16[1,8,128,128]{3,2,1,0:T(8,128)(2,1)S(1)}, u32[]{:S(2)}, u32[]{:S(2)}) collective-permute-start(bf16[1,8,128,128]{3,2,1,0:T(8,128)(2,1)S(1)} %copy-done), channel_id=1, source_target_pairs={{0,2},{1,3},{2,0},{3,1},{4,6},{5,7},{6,4},{7,5},{8,10},{9,11},{10,... | collective-permute-start | bytes 786440 | tf_op jit(solution)/shard_map/ppermute | solution.py:337
  9.1 14.3 %collective-permute-start.6 = (bf16[1,8,128,128]{3,2,1,0:T(8,128)(2,1)S(1)}, bf16[1,8,128,128]{3,2,1,0:T(8,128)(2,1)S(1)}, u32[]{:S(2)}, u32[]{:S(2)}) collective-permute-start(bf16[1,8,128,128]{3,2,1,0:T(8,128)(2,1)S(1)} %copy-done), channel_id=1, source_target_pairs={{0,4},{1,5},{2,6},{3,7},{4,0},{5,1},{6,2},{7,3},{8,12},{9,13},{10,... | collective-permute-start | bytes 786440 | tf_op jit(solution)/shard_map/ppermute | solution.py:337
  10.6 12.7 %collective-permute-start.7 = (bf16[1,8,128,128]{3,2,1,0:T(8,128)(2,1)S(1)}, bf16[1,8,128,128]{3,2,1,0:T(8,128)(2,1)S(1)}, u32[]{:S(2)}, u32[]{:S(2)}) collective-permute-start(bf16[1,8,128,128]{3,2,1,0:T(8,128)(2,1)S(1)} %copy-done), channel_id=1, source_target_pairs={{0,6},{1,7},{2,4},{3,5},{4,2},{5,3},{6,0},{7,1},{8,14},{9,15},{10,... | collective-permute-start | bytes 786440 | tf_op jit(solution)/shard_map/ppermute | solution.py:337
  12.7 7.3 %collective-permute-start = (bf16[1,8,32,128]{3,2,1,0:T(8,128)(2,1)S(1)}, bf16[1,8,32,128]{3,2,1,0:T(8,128)(2,1)S(1)}, u32[]{:S(2)}, u32[]{:S(2)}) collective-permute-start(bf16[1,8,32,128]{3,2,1,0:T(8,128)(2,1)S(1)} %copy-done.1), channel_id=1, source_target_pairs={{0,1},{1,0},{2,3},{3,2},{4,5},{5,4},{6,7},{7,6},{8,9},{9,8},{10,11... | collective-permute-start | bytes 196616 | tf_op jit(solution)/shard_map/ppermute | solution.py:337
  16.9 4.7 %collective-permute-start.4 = (f32[2,8,128]{2,1,0:T(8,128)S(1)}, f32[2,8,128]{2,1,0:T(8,128)S(1)}, u32[]{:S(2)}, u32[]{:S(2)}) collective-permute-start(f32[2,8,128]{2,1,0:T(8,128)S(1)} %get-tuple-element.10), channel_id=1, source_target_pairs={{0,16},{8,24},{16,0},{24,8},{1,17},{9,25},{17,1},{25,9},{2,18},{10... | collective-permute-start | bytes 24584 | tf_op jit(solution)/shard_map/ppermute | solution.py:334
  20.0 5.1 %collective-permute-start.9 = (f32[2,8,128]{2,1,0:T(8,128)S(1)}, f32[2,8,128]{2,1,0:T(8,128)S(1)}, u32[]{:S(2)}, u32[]{:S(2)}) collective-permute-start(f32[2,8,128]{2,1,0:T(8,128)S(1)} %get-tuple-element.14.refs_1_), channel_id=1, source_target_pairs={{0,8},{8,0},{16,24},{24,16},{1,9},{9,1},{17,25},{25,17},{2,10},{10... | collective-permute-start | bytes 24584 | tf_op jit(solution)/shard_map/ppermute | solution.py:334
  21.6 3.7 %collective-permute-start.10 = (f32[2,8,128]{2,1,0:T(8,128)S(1)}, f32[2,8,128]{2,1,0:T(8,128)S(1)}, u32[]{:S(2)}, u32[]{:S(2)}) collective-permute-start(f32[2,8,128]{2,1,0:T(8,128)S(1)} %collective-permute-done.4.refs_0_), channel_id=1, source_target_pairs={{0,8},{8,0},{16,24},{24,16},{1,9},{9,1},{17,25},{25,17},{2,10},{10... | collective-permute-start | bytes 24584 | tf_op jit(solution)/shard_map/ppermute | solution.py:334
  24.2 1.2 %collective-permute-start.8 = (f32[8,128]{1,0:T(8,128)S(1)}, f32[8,128]{1,0:T(8,128)S(1)}, u32[]{:S(2)}, u32[]{:S(2)}) collective-permute-start(f32[8,128]{1,0:T(8,128)S(1)} %score_batch.2), channel_id=1, source_target_pairs={{0,1},{1,0},{2,3},{3,2},{4,5},{5,4},{6,7},{7,6},{8,9},{9,8},{10,11... | collective-permute-start | bytes 12296 | tf_op jit(solution)/shard_map/ppermute | solution.py:337

commit v8 on v4

--- a/solution.py
+++ b/solution.py
@@ -14,6 +14,10 @@
 PACK_FLOPS = 10**10
 PACK_BYTES = 2**24
 CHUNK = 32
+
+
+def send_order(count):
+    return [0, 1] + list(range(count - 1, 1, -1))
 
 
 def in_hbm(array):
@@ -104,7 +108,10 @@
 
 
 def memory_kernel(shards, slots, *refs):
-    packed_refs, passage_ref = refs[:shards], refs[shards].at[0]
+    passage_ref = refs[shards].at[0]
+    packed_refs = [None] * shards
+    for step, packed_ref in zip(send_order(shards), refs):
+        packed_refs[step] = packed_ref
     out_refs = refs[shards + 1 : 2 * shards + 1]
     query_ref, rank_ref, best_ref, list_ref, scalar_ref, list_sem = refs[2 * shards + 1 :]
     q_count = out_refs[0].shape[0]
@@ -233,7 +240,7 @@
     _, queries, q_tokens, depth = query_ref.shape
     count = passage_refs[0].shape[1]
     tokens = query_ref[0].reshape(queries * q_tokens, depth)
-    for chip, passage_ref in enumerate(passage_refs):
+    for chip, passage_ref in zip(send_order(len(passage_refs)), passage_refs):
         best_ref[chip * count : (chip + 1) * count, :] = token_max(passage_ref[0], tokens)
     sums = token_sum(best_ref[...], queries)
     empty = jnp.zeros((queries, out_ref.shape[1] - sums.shape[1]), jnp.float32)
@@ -331,9 +338,11 @@
         return lax.ppermute(array, "group", [(i, i ^ step) for i in range(groups)])
 
     own = pack(queries, candidates, counts, memory.shape[1])
-    packed = [own] + [to_shard(own, step) for step in range(1, shards)]
+    packed = [to_shard(own, step) if step else own for step in send_order(shards)]
     sent_positives, sent_queries, _ = lax.optimization_barrier((positives, queries, own))
-    row = [positives] + [to_group(sent_positives, 2 * step) for step in range(1, chips)]
+    row = [
+        to_group(sent_positives, 2 * step) if step else positives for step in send_order(chips)
+    ]
     mate_queries = to_group(sent_queries, 1)
 
     scores = score_memory(packed, memory, q_count, slots)

time: 25.2 us -> 26.1 us (1.036)
  starting transfers between devices: 14.1 us -> 16.1 us
  waiting for transfers between devices: 2.56 us -> 1.46 us
    ppermute x5, starting transfers between devices: 3.88 us -> 4.97 us  [to_group(): return lax.ppermute(array, 'group', [(i, i ^ step) for i in range(groups)])]
    ppermute x6, starting transfers between devices: 10.2 us -> 11.2 us  [to_shard(): return lax.ppermute(array, 'memory', [(i, i ^ step) for i in range(shards)])]
    ppermute x6, waiting for transfers between devices: 2.35 us -> 1.45 us  [to_shard(): return lax.ppermute(array, 'memory', [(i, i ^ step) for i in range(shards)])]
  transfers between devices with their start and end apart: 11 -> 11, of which waited for: 4 -> 1; matrix products, arithmetic and copies ran while one was open for 0% -> 0% of each run, Pallas kernels for 23% -> 22%
where the time goes in v8:
time: 26.1 us; the launch traced here: 26 us
  starting transfers between devices  16.1 us (62%)
  Pallas kernels  7.63 us (29%)
  waiting for transfers between devices  1.46 us (6%)
  between operations  0.74 us (3%)
    ppermute x6, starting transfers between devices, to_shard(): return lax.ppermute(array, 'memory', [(i, i ^ step) for i in range(shards)])  11.2 us
    ppermute x5, starting transfers between devices, to_group(): return lax.ppermute(array, 'group', [(i, i ^ step) for i in range(groups)])  4.97 us
    pallas_call x1, Pallas kernels, score_memory(): pl.pallas_call(functools.partial(memory_kernel, shards, slots), in_specs=...  4.13 us
    pallas_call x2, Pallas kernels, score_batch(): pl.pallas_call(batch_kernel, out_shape=jax.ShapeDtypeStruct((q_count, lan...  1.67 us
    ppermute x6, waiting for transfers between devices, to_shard(): return lax.ppermute(array, 'memory', [(i, i ^ step) for i in range(shards)])  1.45 us
    pallas_call x1, Pallas kernels, pack(): pl.pallas_call(functools.partial(pack_kernel, p_count), in_specs=[vmem, v...  1.02 us
    pallas_call x1, Pallas kernels, finish(): pl.pallas_call(functools.partial(loss_kernel, len(memory_parts)), out_sha...  0.8 us
  transfers between devices with their start and end apart: 11, of which 1 were waited for; matrix products, arithmetic and copies ran while one was open for 0% of the time, Pallas kernels for 22%

profile of v8, /device:TPU:0, one launch (start us, length us, event | category | flops | bytes accessed | tf_op | source)
XLA Modules:
  0.0 26.0 jit_solution(1605980514091231890)
XLA Ops:
  0.6 0.0 copy-start.1
  0.6 0.0 copy-start
  0.7 0.0 copy-start.4
  0.7 1.0 %pack.1.refs_0_ = bf16[272,128]{1,0:T(8,128)(2,1)S(1)} custom-call(bf16[1,8,32,128]{3,2,1,0:T(8,128)(2,1)} %query_ref.2, s32[1,8,64]{2,1,0:T(8,128)} %refs_4_.3, s32[1,8]{1,0:T(1,128)} %refs_5_.1), custom_call_target="tpu_custom_call" | custom-call | flops 10000000000 | bytes 16777216 | tf_op jit(solution)/shard_map/pack/pallas_call | solution.py:98
  1.7 0.0 copy-start.2
  1.7 0.0 copy-start.3
  1.7 4.1 %collective-permute-start.3 = (bf16[272,128]{1,0:T(8,128)(2,1)S(1)}, bf16[272,128]{1,0:T(8,128)(2,1)S(1)}, u32[]{:S(2)}, u32[]{:S(2)}) collective-permute-start(bf16[272,128]{1,0:T(8,128)(2,1)S(1)} %pack.1.refs_0_), channel_id=1, source_target_pairs={{0,16},{8,24},{16,0},{24,8},{1,17},{9,25},{17,1},{25,9},{2,18},{10... | collective-permute-start | bytes 208904 | tf_op jit(solution)/shard_map/ppermute | solution.py:335
  5.8 1.3 %collective-permute-start.2 = (bf16[272,128]{1,0:T(8,128)(2,1)S(1)}, bf16[272,128]{1,0:T(8,128)(2,1)S(1)}, u32[]{:S(2)}, u32[]{:S(2)}) collective-permute-start(bf16[272,128]{1,0:T(8,128)(2,1)S(1)} %pack.1.refs_0_), channel_id=1, source_target_pairs={{0,24},{8,16},{16,8},{24,0},{1,25},{9,17},{17,9},{25,1},{2,26},{10... | collective-permute-start | bytes 208904 | tf_op jit(solution)/shard_map/ppermute | solution.py:335
  7.2 0.2 collective-permute-start.1
  7.4 1.5 %collective-permute-start.6 = (bf16[1,8,128,128]{3,2,1,0:T(8,128)(2,1)S(1)}, bf16[1,8,128,128]{3,2,1,0:T(8,128)(2,1)S(1)}, u32[]{:S(2)}, u32[]{:S(2)}) collective-permute-start(bf16[1,8,128,128]{3,2,1,0:T(8,128)(2,1)S(1)} %copy-done), channel_id=1, source_target_pairs={{0,4},{1,5},{2,6},{3,7},{4,0},{5,1},{6,2},{7,3},{8,12},{9,13},{10,... | collective-permute-start | bytes 786440 | tf_op jit(solution)/shard_map/ppermute | solution.py:338
  8.9 1.4 %collective-permute-start.5 = (bf16[1,8,128,128]{3,2,1,0:T(8,128)(2,1)S(1)}, bf16[1,8,128,128]{3,2,1,0:T(8,128)(2,1)S(1)}, u32[]{:S(2)}, u32[]{:S(2)}) collective-permute-start(bf16[1,8,128,128]{3,2,1,0:T(8,128)(2,1)S(1)} %copy-done), channel_id=1, source_target_pairs={{0,6},{1,7},{2,4},{3,5},{4,2},{5,3},{6,0},{7,1},{8,14},{9,15},{10,... | collective-permute-start | bytes 786440 | tf_op jit(solution)/shard_map/ppermute | solution.py:338
  10.3 0.0 collective-permute-done.3.refs_3_
  10.4 2.0 %collective-permute-start.4 = (bf16[1,8,128,128]{3,2,1,0:T(8,128)(2,1)S(1)}, bf16[1,8,128,128]{3,2,1,0:T(8,128)(2,1)S(1)}, u32[]{:S(2)}, u32[]{:S(2)}) collective-permute-start(bf16[1,8,128,128]{3,2,1,0:T(8,128)(2,1)S(1)} %copy-done), channel_id=1, source_target_pairs={{0,2},{1,3},{2,0},{3,1},{4,6},{5,7},{6,4},{7,5},{8,10},{9,11},{10,... | collective-permute-start | bytes 786440 | tf_op jit(solution)/shard_map/ppermute | solution.py:338
  12.4 0.0 collective-permute-done.2.refs_2_
  12.4 0.0 collective-permute-start
  12.4 0.0 collective-permute-done.1.refs_1_
  12.4 4.1 %score_memory.1 = (f32[8,128]{1,0:T(8,128)S(1)}, f32[8,128]{1,0:T(8,128)S(1)}, f32[8,128]{1,0:T(8,128)S(1)}, f32[8,128]{1,0:T(8,128)S(1)}) custom-call(bf16[272,128]{1,0:T(8,128)(2,1)S(1)} %pack.1.refs_0_, bf16[272,128]{1,0:T(8,128)(2,1)S(1)} %collective-permute-done.1.refs_1_, bf16[272,128]{1,0:T(8,128)(2,1)S(1)} %collective-permute-done.2.refs_2_, ...), custom_call_target="tpu_custom_call" | custom-call | flops 4294967296 | bytes 4194304 | tf_op jit(solution)/shard_map/score_memory/pallas_call | solution.py:215
  16.5 0.0 collective-permute-done.query_ref
  16.5 4.1 %collective-permute-start.8 = (f32[8,128]{1,0:T(8,128)S(1)}, f32[8,128]{1,0:T(8,128)S(1)}, u32[]{:S(2)}, u32[]{:S(2)}) collective-permute-start(f32[8,128]{1,0:T(8,128)S(1)} %get-tuple-element.16), channel_id=1, source_target_pairs={{0,24},{8,16},{16,8},{24,0},{1,25},{9,17},{17,9},{25,1},{2,26},{10... | collective-permute-start | bytes 12296 | tf_op jit(solution)/shard_map/ppermute | solution.py:335
  20.6 0.0 collective-permute-start.9
  20.7 0.0 collective-permute-done.6.refs_3_
  20.7 1.4 %collective-permute-start.10 = (f32[8,128]{1,0:T(8,128)S(1)}, f32[8,128]{1,0:T(8,128)S(1)}, u32[]{:S(2)}, u32[]{:S(2)}) collective-permute-start(f32[8,128]{1,0:T(8,128)S(1)} %get-tuple-element.18), channel_id=1, source_target_pairs={{0,8},{8,0},{16,24},{24,16},{1,9},{9,1},{17,25},{25,17},{2,10},{10... | collective-permute-start | bytes 12296 | tf_op jit(solution)/shard_map/ppermute | solution.py:335
  22.0 0.0 collective-permute-done.5.refs_2_
  22.0 0.0 collective-permute-done.4.refs_1_
  22.0 0.8 %score_batch.2 = f32[8,128]{1,0:T(8,128)S(1)} custom-call(bf16[1,8,32,128]{3,2,1,0:T(8,128)(2,1)S(1)} %collective-permute-done.query_ref, bf16[1,8,128,128]{3,2,1,0:T(8,128)(2,1)S(1)} %copy-done, bf16[1,8,128,128]{3,2,1,0:T(8,128)(2,1)S(1)} %collective-permute-done.4.refs_1_, bf16[1,8,128,128]{3,2,1,0:T(8,128)(2,1)S(1)} %collective-permute-done.5.refs_2_, ...), custom_call_target="tpu_custom_call" | custom-call | flops 268435456 | bytes 1048576 | tf_op jit(solution)/shard_map/score_batch/pallas_call | solution.py:255
  22.9 0.0 collective-permute-start.7
  22.9 0.9 %score_batch.3.own_batch = f32[8,128]{1,0:T(8,128)S(1)} custom-call(bf16[1,8,32,128]{3,2,1,0:T(8,128)(2,1)S(1)} %copy-done.1, bf16[1,8,128,128]{3,2,1,0:T(8,128)(2,1)S(1)} %copy-done, bf16[1,8,128,128]{3,2,1,0:T(8,128)(2,1)S(1)} %collective-permute-done.4.refs_1_, bf16[1,8,128,128]{3,2,1,0:T(8,128)(2,1)S(1)} %collective-permute-done.5.refs_2_, ...), custom_call_target="tpu_custom_call" | custom-call | flops 268435456 | bytes 1048576 | tf_op jit(solution)/shard_map/score_batch/pallas_call | solution.py:255
  23.7 0.0 collective-permute-done.8.refs_1_
  23.7 1.4 %collective-permute-done.9.refs_2_ = f32[8,128]{1,0:T(8,128)S(1)} collective-permute-done((f32[8,128]{1,0:T(8,128)S(1)}, f32[8,128]{1,0:T(8,128)S(1)}, u32[]{:S(2)}, u32[]{:S(2)}) %collective-permute-start.9) | collective-permute-done | bytes 4128 | tf_op jit(solution)/shard_map/ppermute | solution.py:335
  25.2 0.0 collective-permute-done.10.refs_3_
  25.2 0.0 collective-permute-done.7.mate_batch
  25.2 0.8 %finish.1 = (f32[1,8,64]{2,1,0:T(8,128)}, f32[1,8,64]{2,1,0:T(8,128)}, f32[1,8]{1,0:T(1,128)}) custom-call(f32[8,128]{1,0:T(8,128)S(1)} %score_batch.3.own_batch, f32[8,128]{1,0:T(8,128)S(1)} %collective-permute-done.7.mate_batch, f32[8,128]{1,0:T(8,128)S(1)} %get-tuple-element.12.refs_0_, f32[8,128]{1,0:T(8,128)S(1)} %collective-permute-done.8.refs_1_, ...), custom_call_target="tpu_custom_call" | custom-call | tf_op jit(solution)/shard_map/finish/pallas_call | solution.py:315
  (5 shorter events, 0.0 us)
Async XLA Ops:
  0.6 11.7 %copy-start.1 = (bf16[1,8,32,128]{3,2,1,0:T(8,128)(2,1)S(1)}, bf16[1,8,32,128]{3,2,1,0:T(8,128)(2,1)}, u32[]{:S(2)}) copy-start(bf16[1,8,32,128]{3,2,1,0:T(8,128)(2,1)} %query_ref.2) | copy-start | bytes 196612
  0.6 6.8 %copy-start = (bf16[1,8,128,128]{3,2,1,0:T(8,128)(2,1)S(1)}, bf16[1,8,128,128]{3,2,1,0:T(8,128)(2,1)}, u32[]{:S(2)}) copy-start(bf16[1,8,128,128]{3,2,1,0:T(8,128)(2,1)} %refs_0_.3) | copy-start | bytes 786436
  0.7 11.7 %copy-start.4 = (bf16[1,128,128,128]{3,2,1,0:T(8,128)(2,1)S(1)}, bf16[1,128,128,128]{3,2,1,0:T(8,128)(2,1)}, u32[]{:S(2)}) copy-start(bf16[1,128,128,128]{3,2,1,0:T(8,128)(2,1)} %refs_4_.2) | copy-start | bytes 12582916
  1.7 23.5 %copy-start.2 = (s32[1,8,64]{2,1,0:T(8,128)S(1)}, s32[1,8,64]{2,1,0:T(8,128)}, u32[]{:S(2)}) copy-start(s32[1,8,64]{2,1,0:T(8,128)} %refs_4_.3) | copy-start | bytes 6148
  1.7 23.5 %copy-start.3 = (s32[1,8]{1,0:T(1,128)S(1)}, s32[1,8]{1,0:T(1,128)}, u32[]{:S(2)}) copy-start(s32[1,8]{1,0:T(1,128)} %refs_5_.1) | copy-start | bytes 100
  1.7 8.6 %collective-permute-start.3 = (bf16[272,128]{1,0:T(8,128)(2,1)S(1)}, bf16[272,128]{1,0:T(8,128)(2,1)S(1)}, u32[]{:S(2)}, u32[]{:S(2)}) collective-permute-start(bf16[272,128]{1,0:T(8,128)(2,1)S(1)} %pack.1.refs_0_), channel_id=1, source_target_pairs={{0,16},{8,24},{16,0},{24,8},{1,17},{9,25},{17,1},{25,9},{2,18},{10... | collective-permute-start | bytes 208904 | tf_op jit(solution)/shard_map/ppermute | solution.py:335
  5.8 6.6 %collective-permute-start.2 = (bf16[272,128]{1,0:T(8,128)(2,1)S(1)}, bf16[272,128]{1,0:T(8,128)(2,1)S(1)}, u32[]{:S(2)}, u32[]{:S(2)}) collective-permute-start(bf16[272,128]{1,0:T(8,128)(2,1)S(1)} %pack.1.refs_0_), channel_id=1, source_target_pairs={{0,24},{8,16},{16,8},{24,0},{1,25},{9,17},{17,9},{25,1},{2,26},{10... | collective-permute-start | bytes 208904 | tf_op jit(solution)/shard_map/ppermute | solution.py:335
  7.2 5.2 %collective-permute-start.1 = (bf16[272,128]{1,0:T(8,128)(2,1)S(1)}, bf16[272,128]{1,0:T(8,128)(2,1)S(1)}, u32[]{:S(2)}, u32[]{:S(2)}) collective-permute-start(bf16[272,128]{1,0:T(8,128)(2,1)S(1)} %pack.1.refs_0_), channel_id=1, source_target_pairs={{0,8},{8,0},{16,24},{24,16},{1,9},{9,1},{17,25},{25,17},{2,10},{10... | collective-permute-start | bytes 208904 | tf_op jit(solution)/shard_map/ppermute | solution.py:335
  7.4 13.3 %collective-permute-start.6 = (bf16[1,8,128,128]{3,2,1,0:T(8,128)(2,1)S(1)}, bf16[1,8,128,128]{3,2,1,0:T(8,128)(2,1)S(1)}, u32[]{:S(2)}, u32[]{:S(2)}) collective-permute-start(bf16[1,8,128,128]{3,2,1,0:T(8,128)(2,1)S(1)} %copy-done), channel_id=1, source_target_pairs={{0,4},{1,5},{2,6},{3,7},{4,0},{5,1},{6,2},{7,3},{8,12},{9,13},{10,... | collective-permute-start | bytes 786440 | tf_op jit(solution)/shard_map/ppermute | solution.py:338
  8.9 13.1 %collective-permute-start.5 = (bf16[1,8,128,128]{3,2,1,0:T(8,128)(2,1)S(1)}, bf16[1,8,128,128]{3,2,1,0:T(8,128)(2,1)S(1)}, u32[]{:S(2)}, u32[]{:S(2)}) collective-permute-start(bf16[1,8,128,128]{3,2,1,0:T(8,128)(2,1)S(1)} %copy-done), channel_id=1, source_target_pairs={{0,6},{1,7},{2,4},{3,5},{4,2},{5,3},{6,0},{7,1},{8,14},{9,15},{10,... | collective-permute-start | bytes 786440 | tf_op jit(solution)/shard_map/ppermute | solution.py:338
  10.4 11.7 %collective-permute-start.4 = (bf16[1,8,128,128]{3,2,1,0:T(8,128)(2,1)S(1)}, bf16[1,8,128,128]{3,2,1,0:T(8,128)(2,1)S(1)}, u32[]{:S(2)}, u32[]{:S(2)}) collective-permute-start(bf16[1,8,128,128]{3,2,1,0:T(8,128)(2,1)S(1)} %copy-done), channel_id=1, source_target_pairs={{0,2},{1,3},{2,0},{3,1},{4,6},{5,7},{6,4},{7,5},{8,10},{9,11},{10,... | collective-permute-start | bytes 786440 | tf_op jit(solution)/shard_map/ppermute | solution.py:338
  12.4 4.2 %collective-permute-start = (bf16[1,8,32,128]{3,2,1,0:T(8,128)(2,1)S(1)}, bf16[1,8,32,128]{3,2,1,0:T(8,128)(2,1)S(1)}, u32[]{:S(2)}, u32[]{:S(2)}) collective-permute-start(bf16[1,8,32,128]{3,2,1,0:T(8,128)(2,1)S(1)} %copy-done.1), channel_id=1, source_target_pairs={{0,1},{1,0},{2,3},{3,2},{4,5},{5,4},{6,7},{7,6},{8,9},{9,8},{10,11... | collective-permute-start | bytes 196616 | tf_op jit(solution)/shard_map/ppermute | solution.py:338
  16.5 7.2 %collective-permute-start.8 = (f32[8,128]{1,0:T(8,128)S(1)}, f32[8,128]{1,0:T(8,128)S(1)}, u32[]{:S(2)}, u32[]{:S(2)}) collective-permute-start(f32[8,128]{1,0:T(8,128)S(1)} %get-tuple-element.16), channel_id=1, source_target_pairs={{0,24},{8,16},{16,8},{24,0},{1,25},{9,17},{17,9},{25,1},{2,26},{10... | collective-permute-start | bytes 12296 | tf_op jit(solution)/shard_map/ppermute | solution.py:335
  20.6 4.5 %collective-permute-start.9 = (f32[8,128]{1,0:T(8,128)S(1)}, f32[8,128]{1,0:T(8,128)S(1)}, u32[]{:S(2)}, u32[]{:S(2)}) collective-permute-start(f32[8,128]{1,0:T(8,128)S(1)} %get-tuple-element.17), channel_id=1, source_target_pairs={{0,16},{8,24},{16,0},{24,8},{1,17},{9,25},{17,1},{25,9},{2,18},{10... | collective-permute-start | bytes 12296 | tf_op jit(solution)/shard_map/ppermute | solution.py:335
  20.7 4.5 %collective-permute-start.10 = (f32[8,128]{1,0:T(8,128)S(1)}, f32[8,128]{1,0:T(8,128)S(1)}, u32[]{:S(2)}, u32[]{:S(2)}) collective-permute-start(f32[8,128]{1,0:T(8,128)S(1)} %get-tuple-element.18), channel_id=1, source_target_pairs={{0,8},{8,0},{16,24},{24,16},{1,9},{9,1},{17,25},{25,17},{2,10},{10... | collective-permute-start | bytes 12296 | tf_op jit(solution)/shard_map/ppermute | solution.py:335
  22.9 2.3 %collective-permute-start.7 = (f32[8,128]{1,0:T(8,128)S(1)}, f32[8,128]{1,0:T(8,128)S(1)}, u32[]{:S(2)}, u32[]{:S(2)}) collective-permute-start(f32[8,128]{1,0:T(8,128)S(1)} %score_batch.2), channel_id=1, source_target_pairs={{0,1},{1,0},{2,3},{3,2},{4,5},{5,4},{6,7},{7,6},{8,9},{9,8},{10,11... | collective-permute-start | bytes 12296 | tf_op jit(solution)/shard_map/ppermute | solution.py:338

commit v9 on v4

--- a/solution.py
+++ b/solution.py
@@ -14,6 +14,10 @@
 PACK_FLOPS = 10**10
 PACK_BYTES = 2**24
 CHUNK = 32
+
+
+def return_order(shards):
+    return list(range(2, shards)) + [1]
 
 
 def in_hbm(array):
@@ -283,8 +287,8 @@
     padded = jnp.concatenate([ids, jnp.zeros((q_count, p_count - slots), jnp.int32)], axis=1)
     holder, local = padded // p_count, padded % p_count
     picked = jnp.zeros((q_count, p_count), jnp.float32)
-    for step in range(shards):
-        found = jnp.take_along_axis(memory_refs[-step][...], local, axis=1)
+    for step, part_ref in zip([0] + return_order(shards), memory_refs):
+        found = jnp.take_along_axis(part_ref[...], local, axis=1)
         picked = jnp.where(holder == (shard ^ step), found, picked)
 
     valid = lax.broadcasted_iota(jnp.int32, (q_count, p_count), 1) < column_of(count_ref[...])
@@ -337,7 +341,7 @@
     mate_queries = to_group(sent_queries, 1)
 
     scores = score_memory(packed, memory, q_count, slots)
-    returned = [to_shard(scores[step], step) for step in range(shards - 1, 0, -1)]
+    returned = [to_shard(scores[step], step) for step in return_order(shards)]
     mate_queries, _ = lax.optimization_barrier((mate_queries, scores[0]))
     mate_scores = score_batch(mate_queries, row)
     mate_batch = to_group(mate_scores, 1)

time: 25.2 us -> 25.4 us (level)
  waiting for transfers between devices: 2.56 us -> 3.72 us
  starting transfers between devices: 14.1 us -> 13.2 us
    ppermute x5, waiting for transfers between devices: 0.21 us -> 1.11 us  [to_group(): return lax.ppermute(array, 'group', [(i, i ^ step) for i in range(groups)])]
    ppermute x6, starting transfers between devices: 10.2 us -> 9.31 us  [to_shard(): return lax.ppermute(array, 'memory', [(i, i ^ step) for i in range(shards)])]
    ppermute x6, waiting for transfers between devices: 2.35 us -> 2.61 us  [to_shard(): return lax.ppermute(array, 'memory', [(i, i ^ step) for i in range(shards)])]
where the time goes in v9:
time: 25.4 us; the launch traced here: 25.3 us
  starting transfers between devices  13.2 us (52%)
  Pallas kernels  7.63 us (30%)
  waiting for transfers between devices  3.72 us (15%)
  between operations  0.73 us (3%)
    ppermute x6, starting transfers between devices, to_shard(): return lax.ppermute(array, 'memory', [(i, i ^ step) for i in range(shards)])  9.31 us
    pallas_call x1, Pallas kernels, score_memory(): pl.pallas_call(functools.partial(memory_kernel, shards, slots), in_specs=...  4.14 us
    ppermute x5, starting transfers between devices, to_group(): return lax.ppermute(array, 'group', [(i, i ^ step) for i in range(groups)])  3.88 us
    ppermute x6, waiting for transfers between devices, to_shard(): return lax.ppermute(array, 'memory', [(i, i ^ step) for i in range(shards)])  2.61 us
    pallas_call x2, Pallas kernels, score_batch(): pl.pallas_call(batch_kernel, out_shape=jax.ShapeDtypeStruct((q_count, lan...  1.67 us
    ppermute x5, waiting for transfers between devices, to_group(): return lax.ppermute(array, 'group', [(i, i ^ step) for i in range(groups)])  1.11 us
    pallas_call x1, Pallas kernels, pack(): pl.pallas_call(functools.partial(pack_kernel, p_count), in_specs=[vmem, v...  1.02 us
    pallas_call x1, Pallas kernels, finish(): pl.pallas_call(functools.partial(loss_kernel, len(memory_parts)), out_sha...  0.8 us
  transfers between devices with their start and end apart: 11, of which 4 were waited for; matrix products, arithmetic and copies ran while one was open for 0% of the time, Pallas kernels for 23%

profile of v9, /device:TPU:0, one launch (start us, length us, event | category | flops | bytes accessed | tf_op | source)
XLA Modules:
  0.0 25.3 jit_solution(304985343750407971)
XLA Ops:
  0.6 0.0 copy-start.1
  0.7 1.0 %pack.1.refs_0_ = bf16[272,128]{1,0:T(8,128)(2,1)S(1)} custom-call(bf16[1,8,32,128]{3,2,1,0:T(8,128)(2,1)} %query_ref.2, s32[1,8,64]{2,1,0:T(8,128)} %refs_4_.3, s32[1,8]{1,0:T(1,128)} %refs_5_.1), custom_call_target="tpu_custom_call" | custom-call | flops 10000000000 | bytes 16777216 | tf_op jit(solution)/shard_map/pack/pallas_call | solution.py:98
  1.7 0.0 copy-start.2
  1.7 0.0 copy-start.3
  1.7 5.1 %collective-permute-start.3 = (bf16[272,128]{1,0:T(8,128)(2,1)S(1)}, bf16[272,128]{1,0:T(8,128)(2,1)S(1)}, u32[]{:S(2)}, u32[]{:S(2)}) collective-permute-start(bf16[272,128]{1,0:T(8,128)(2,1)S(1)} %pack.1.refs_0_), channel_id=1, source_target_pairs={{0,24},{8,16},{16,8},{24,0},{1,25},{9,17},{17,9},{25,1},{2,26},{10... | collective-permute-start | bytes 208904 | tf_op jit(solution)/shard_map/ppermute | solution.py:332
  6.8 0.0 collective-permute-start.2
  6.8 0.6 %collective-permute-start.1 = (bf16[272,128]{1,0:T(8,128)(2,1)S(1)}, bf16[272,128]{1,0:T(8,128)(2,1)S(1)}, u32[]{:S(2)}, u32[]{:S(2)}) collective-permute-start(bf16[272,128]{1,0:T(8,128)(2,1)S(1)} %pack.1.refs_0_), channel_id=1, source_target_pairs={{0,8},{8,0},{16,24},{24,16},{1,9},{9,1},{17,25},{25,17},{2,10},{10... | collective-permute-start | bytes 208904 | tf_op jit(solution)/shard_map/ppermute | solution.py:332
  7.5 2.6 %collective-permute-start.6 = (bf16[1,8,128,128]{3,2,1,0:T(8,128)(2,1)S(1)}, bf16[1,8,128,128]{3,2,1,0:T(8,128)(2,1)S(1)}, u32[]{:S(2)}, u32[]{:S(2)}) collective-permute-start(bf16[1,8,128,128]{3,2,1,0:T(8,128)(2,1)S(1)} %copy-done), channel_id=1, source_target_pairs={{0,6},{1,7},{2,4},{3,5},{4,2},{5,3},{6,0},{7,1},{8,14},{9,15},{10,... | collective-permute-start | bytes 786440 | tf_op jit(solution)/shard_map/ppermute | solution.py:335
  10.1 0.5 %collective-permute-start.5 = (bf16[1,8,128,128]{3,2,1,0:T(8,128)(2,1)S(1)}, bf16[1,8,128,128]{3,2,1,0:T(8,128)(2,1)S(1)}, u32[]{:S(2)}, u32[]{:S(2)}) collective-permute-start(bf16[1,8,128,128]{3,2,1,0:T(8,128)(2,1)S(1)} %copy-done), channel_id=1, source_target_pairs={{0,4},{1,5},{2,6},{3,7},{4,0},{5,1},{6,2},{7,3},{8,12},{9,13},{10,... | collective-permute-start | bytes 786440 | tf_op jit(solution)/shard_map/ppermute | solution.py:335
  10.6 0.0 collective-permute-done.3.refs_3_
  10.6 0.8 %collective-permute-start.4 = (bf16[1,8,128,128]{3,2,1,0:T(8,128)(2,1)S(1)}, bf16[1,8,128,128]{3,2,1,0:T(8,128)(2,1)S(1)}, u32[]{:S(2)}, u32[]{:S(2)}) collective-permute-start(bf16[1,8,128,128]{3,2,1,0:T(8,128)(2,1)S(1)} %copy-done), channel_id=1, source_target_pairs={{0,2},{1,3},{2,0},{3,1},{4,6},{5,7},{6,4},{7,5},{8,10},{9,11},{10,... | collective-permute-start | bytes 786440 | tf_op jit(solution)/shard_map/ppermute | solution.py:335
  11.3 1.4 %collective-permute-done.2.refs_2_ = bf16[272,128]{1,0:T(8,128)(2,1)S(1)} collective-permute-done((bf16[272,128]{1,0:T(8,128)(2,1)S(1)}, bf16[272,128]{1,0:T(8,128)(2,1)S(1)}, u32[]{:S(2)}, u32[]{:S(2)}) %collective-permute-start.2) | collective-permute-done | bytes 69664 | tf_op jit(solution)/shard_map/ppermute | solution.py:332
  12.7 0.0 copy-done.1
  12.7 0.0 collective-permute-start
  12.7 0.0 collective-permute-done.1.refs_1_
  12.8 4.1 %score_memory.1 = (f32[8,128]{1,0:T(8,128)S(1)}, f32[8,128]{1,0:T(8,128)S(1)}, f32[8,128]{1,0:T(8,128)S(1)}, f32[8,128]{1,0:T(8,128)S(1)}) custom-call(bf16[272,128]{1,0:T(8,128)(2,1)S(1)} %pack.1.refs_0_, bf16[272,128]{1,0:T(8,128)(2,1)S(1)} %collective-permute-done.1.refs_1_, bf16[272,128]{1,0:T(8,128)(2,1)S(1)} %collective-permute-done.2.refs_2_, ...), custom_call_target="tpu_custom_call" | custom-call | flops 4294967296 | bytes 4194304 | tf_op jit(solution)/shard_map/score_memory/pallas_call | solution.py:212
  16.9 0.0 collective-permute-done.query_ref
  16.9 2.1 %collective-permute-start.8 = (f32[8,128]{1,0:T(8,128)S(1)}, f32[8,128]{1,0:T(8,128)S(1)}, u32[]{:S(2)}, u32[]{:S(2)}) collective-permute-start(f32[8,128]{1,0:T(8,128)S(1)} %get-tuple-element.16), channel_id=1, source_target_pairs={{0,16},{8,24},{16,0},{24,8},{1,17},{9,25},{17,1},{25,9},{2,18},{10... | collective-permute-start | bytes 12296 | tf_op jit(solution)/shard_map/ppermute | solution.py:332
  19.1 1.3 %collective-permute-start.9 = (f32[8,128]{1,0:T(8,128)S(1)}, f32[8,128]{1,0:T(8,128)S(1)}, u32[]{:S(2)}, u32[]{:S(2)}) collective-permute-start(f32[8,128]{1,0:T(8,128)S(1)} %get-tuple-element.17), channel_id=1, source_target_pairs={{0,24},{8,16},{16,8},{24,0},{1,25},{9,17},{17,9},{25,1},{2,26},{10... | collective-permute-start | bytes 12296 | tf_op jit(solution)/shard_map/ppermute | solution.py:332
  20.4 0.0 collective-permute-done.6.refs_3_
  20.4 0.1 collective-permute-start.10
  20.5 1.0 %collective-permute-done.5.refs_2_ = bf16[1,8,128,128]{3,2,1,0:T(8,128)(2,1)S(1)} collective-permute-done((bf16[1,8,128,128]{3,2,1,0:T(8,128)(2,1)S(1)}, bf16[1,8,128,128]{3,2,1,0:T(8,128)(2,1)S(1)}, u32[]{:S(2)}, u32[]{:S(2)}) %collective-permute-start.5) | collective-permute-done | bytes 262176 | tf_op jit(solution)/shard_map/ppermute | solution.py:335
  21.5 0.1 collective-permute-done.4.refs_1_
  21.6 0.8 %score_batch.2 = f32[8,128]{1,0:T(8,128)S(1)} custom-call(bf16[1,8,32,128]{3,2,1,0:T(8,128)(2,1)S(1)} %collective-permute-done.query_ref, bf16[1,8,128,128]{3,2,1,0:T(8,128)(2,1)S(1)} %copy-done, bf16[1,8,128,128]{3,2,1,0:T(8,128)(2,1)S(1)} %collective-permute-done.4.refs_1_, bf16[1,8,128,128]{3,2,1,0:T(8,128)(2,1)S(1)} %collective-permute-done.5.refs_2_, ...), custom_call_target="tpu_custom_call" | custom-call | flops 268435456 | bytes 1048576 | tf_op jit(solution)/shard_map/score_batch/pallas_call | solution.py:252
  22.4 0.0 collective-permute-start.7
  22.4 0.9 %score_batch.3.own_batch = f32[8,128]{1,0:T(8,128)S(1)} custom-call(bf16[1,8,32,128]{3,2,1,0:T(8,128)(2,1)S(1)} %copy-done.1, bf16[1,8,128,128]{3,2,1,0:T(8,128)(2,1)S(1)} %copy-done, bf16[1,8,128,128]{3,2,1,0:T(8,128)(2,1)S(1)} %collective-permute-done.4.refs_1_, bf16[1,8,128,128]{3,2,1,0:T(8,128)(2,1)S(1)} %collective-permute-done.5.refs_2_, ...), custom_call_target="tpu_custom_call" | custom-call | flops 268435456 | bytes 1048576 | tf_op jit(solution)/shard_map/score_batch/pallas_call | solution.py:252
  23.2 0.0 collective-permute-done.8.refs_1_
  23.3 1.2 %collective-permute-done.9.refs_2_ = f32[8,128]{1,0:T(8,128)S(1)} collective-permute-done((f32[8,128]{1,0:T(8,128)S(1)}, f32[8,128]{1,0:T(8,128)S(1)}, u32[]{:S(2)}, u32[]{:S(2)}) %collective-permute-start.9) | collective-permute-done | bytes 4128 | tf_op jit(solution)/shard_map/ppermute | solution.py:332
  24.5 0.0 collective-permute-done.10.refs_3_
  24.5 0.0 collective-permute-done.7.mate_batch
  24.5 0.0 copy-done.2
  24.5 0.8 %finish.1 = (f32[1,8,64]{2,1,0:T(8,128)}, f32[1,8,64]{2,1,0:T(8,128)}, f32[1,8]{1,0:T(1,128)}) custom-call(f32[8,128]{1,0:T(8,128)S(1)} %score_batch.3.own_batch, f32[8,128]{1,0:T(8,128)S(1)} %collective-permute-done.7.mate_batch, f32[8,128]{1,0:T(8,128)S(1)} %get-tuple-element.12.refs_0_, f32[8,128]{1,0:T(8,128)S(1)} %collective-permute-done.8.refs_1_, ...), custom_call_target="tpu_custom_call" | custom-call | tf_op jit(solution)/shard_map/finish/pallas_call | solution.py:312
  (5 shorter events, 0.0 us)
Async XLA Ops:
  0.6 12.1 %copy-start.1 = (bf16[1,8,32,128]{3,2,1,0:T(8,128)(2,1)S(1)}, bf16[1,8,32,128]{3,2,1,0:T(8,128)(2,1)}, u32[]{:S(2)}) copy-start(bf16[1,8,32,128]{3,2,1,0:T(8,128)(2,1)} %query_ref.2) | copy-start | bytes 196612
  0.6 6.8 %copy-start = (bf16[1,8,128,128]{3,2,1,0:T(8,128)(2,1)S(1)}, bf16[1,8,128,128]{3,2,1,0:T(8,128)(2,1)}, u32[]{:S(2)}) copy-start(bf16[1,8,128,128]{3,2,1,0:T(8,128)(2,1)} %refs_0_.3) | copy-start | bytes 786436
  0.7 12.1 %copy-start.4 = (bf16[1,128,128,128]{3,2,1,0:T(8,128)(2,1)S(1)}, bf16[1,128,128,128]{3,2,1,0:T(8,128)(2,1)}, u32[]{:S(2)}) copy-start(bf16[1,128,128,128]{3,2,1,0:T(8,128)(2,1)} %refs_4_.2) | copy-start | bytes 12582916
  1.7 22.8 %copy-start.2 = (s32[1,8,64]{2,1,0:T(8,128)S(1)}, s32[1,8,64]{2,1,0:T(8,128)}, u32[]{:S(2)}) copy-start(s32[1,8,64]{2,1,0:T(8,128)} %refs_4_.3) | copy-start | bytes 6148
  1.7 22.8 %copy-start.3 = (s32[1,8]{1,0:T(1,128)S(1)}, s32[1,8]{1,0:T(1,128)}, u32[]{:S(2)}) copy-start(s32[1,8]{1,0:T(1,128)} %refs_5_.1) | copy-start | bytes 100
  1.7 8.9 %collective-permute-start.3 = (bf16[272,128]{1,0:T(8,128)(2,1)S(1)}, bf16[272,128]{1,0:T(8,128)(2,1)S(1)}, u32[]{:S(2)}, u32[]{:S(2)}) collective-permute-start(bf16[272,128]{1,0:T(8,128)(2,1)S(1)} %pack.1.refs_0_), channel_id=1, source_target_pairs={{0,24},{8,16},{16,8},{24,0},{1,25},{9,17},{17,9},{25,1},{2,26},{10... | collective-permute-start | bytes 208904 | tf_op jit(solution)/shard_map/ppermute | solution.py:332
  6.8 5.9 %collective-permute-start.2 = (bf16[272,128]{1,0:T(8,128)(2,1)S(1)}, bf16[272,128]{1,0:T(8,128)(2,1)S(1)}, u32[]{:S(2)}, u32[]{:S(2)}) collective-permute-start(bf16[272,128]{1,0:T(8,128)(2,1)S(1)} %pack.1.refs_0_), channel_id=1, source_target_pairs={{0,16},{8,24},{16,0},{24,8},{1,17},{9,25},{17,1},{25,9},{2,18},{10... | collective-permute-start | bytes 208904 | tf_op jit(solution)/shard_map/ppermute | solution.py:332
  6.8 5.9 %collective-permute-start.1 = (bf16[272,128]{1,0:T(8,128)(2,1)S(1)}, bf16[272,128]{1,0:T(8,128)(2,1)S(1)}, u32[]{:S(2)}, u32[]{:S(2)}) collective-permute-start(bf16[272,128]{1,0:T(8,128)(2,1)S(1)} %pack.1.refs_0_), channel_id=1, source_target_pairs={{0,8},{8,0},{16,24},{24,16},{1,9},{9,1},{17,25},{25,17},{2,10},{10... | collective-permute-start | bytes 208904 | tf_op jit(solution)/shard_map/ppermute | solution.py:332
  7.5 12.9 %collective-permute-start.6 = (bf16[1,8,128,128]{3,2,1,0:T(8,128)(2,1)S(1)}, bf16[1,8,128,128]{3,2,1,0:T(8,128)(2,1)S(1)}, u32[]{:S(2)}, u32[]{:S(2)}) collective-permute-start(bf16[1,8,128,128]{3,2,1,0:T(8,128)(2,1)S(1)} %copy-done), channel_id=1, source_target_pairs={{0,6},{1,7},{2,4},{3,5},{4,2},{5,3},{6,0},{7,1},{8,14},{9,15},{10,... | collective-permute-start | bytes 786440 | tf_op jit(solution)/shard_map/ppermute | solution.py:335
  10.1 11.4 %collective-permute-start.5 = (bf16[1,8,128,128]{3,2,1,0:T(8,128)(2,1)S(1)}, bf16[1,8,128,128]{3,2,1,0:T(8,128)(2,1)S(1)}, u32[]{:S(2)}, u32[]{:S(2)}) collective-permute-start(bf16[1,8,128,128]{3,2,1,0:T(8,128)(2,1)S(1)} %copy-done), channel_id=1, source_target_pairs={{0,4},{1,5},{2,6},{3,7},{4,0},{5,1},{6,2},{7,3},{8,12},{9,13},{10,... | collective-permute-start | bytes 786440 | tf_op jit(solution)/shard_map/ppermute | solution.py:335
  10.6 11.0 %collective-permute-start.4 = (bf16[1,8,128,128]{3,2,1,0:T(8,128)(2,1)S(1)}, bf16[1,8,128,128]{3,2,1,0:T(8,128)(2,1)S(1)}, u32[]{:S(2)}, u32[]{:S(2)}) collective-permute-start(bf16[1,8,128,128]{3,2,1,0:T(8,128)(2,1)S(1)} %copy-done), channel_id=1, source_target_pairs={{0,2},{1,3},{2,0},{3,1},{4,6},{5,7},{6,4},{7,5},{8,10},{9,11},{10,... | collective-permute-start | bytes 786440 | tf_op jit(solution)/shard_map/ppermute | solution.py:335
  12.7 4.2 %collective-permute-start = (bf16[1,8,32,128]{3,2,1,0:T(8,128)(2,1)S(1)}, bf16[1,8,32,128]{3,2,1,0:T(8,128)(2,1)S(1)}, u32[]{:S(2)}, u32[]{:S(2)}) collective-permute-start(bf16[1,8,32,128]{3,2,1,0:T(8,128)(2,1)S(1)} %copy-done.1), channel_id=1, source_target_pairs={{0,1},{1,0},{2,3},{3,2},{4,5},{5,4},{6,7},{7,6},{8,9},{9,8},{10,11... | collective-permute-start | bytes 196616 | tf_op jit(solution)/shard_map/ppermute | solution.py:335
  16.9 6.3 %collective-permute-start.8 = (f32[8,128]{1,0:T(8,128)S(1)}, f32[8,128]{1,0:T(8,128)S(1)}, u32[]{:S(2)}, u32[]{:S(2)}) collective-permute-start(f32[8,128]{1,0:T(8,128)S(1)} %get-tuple-element.16), channel_id=1, source_target_pairs={{0,16},{8,24},{16,0},{24,8},{1,17},{9,25},{17,1},{25,9},{2,18},{10... | collective-permute-start | bytes 12296 | tf_op jit(solution)/shard_map/ppermute | solution.py:332
  19.1 5.4 %collective-permute-start.9 = (f32[8,128]{1,0:T(8,128)S(1)}, f32[8,128]{1,0:T(8,128)S(1)}, u32[]{:S(2)}, u32[]{:S(2)}) collective-permute-start(f32[8,128]{1,0:T(8,128)S(1)} %get-tuple-element.17), channel_id=1, source_target_pairs={{0,24},{8,16},{16,8},{24,0},{1,25},{9,17},{17,9},{25,1},{2,26},{10... | collective-permute-start | bytes 12296 | tf_op jit(solution)/shard_map/ppermute | solution.py:332
  20.4 4.1 %collective-permute-start.10 = (f32[8,128]{1,0:T(8,128)S(1)}, f32[8,128]{1,0:T(8,128)S(1)}, u32[]{:S(2)}, u32[]{:S(2)}) collective-permute-start(f32[8,128]{1,0:T(8,128)S(1)} %get-tuple-element.18), channel_id=1, source_target_pairs={{0,8},{8,0},{16,24},{24,16},{1,9},{9,1},{17,25},{25,17},{2,10},{10... | collective-permute-start | bytes 12296 | tf_op jit(solution)/shard_map/ppermute | solution.py:332
  22.4 2.1 %collective-permute-start.7 = (f32[8,128]{1,0:T(8,128)S(1)}, f32[8,128]{1,0:T(8,128)S(1)}, u32[]{:S(2)}, u32[]{:S(2)}) collective-permute-start(f32[8,128]{1,0:T(8,128)S(1)} %score_batch.2), channel_id=1, source_target_pairs={{0,1},{1,0},{2,3},{3,2},{4,5},{5,4},{6,7},{7,6},{8,9},{9,8},{10,11... | collective-permute-start | bytes 12296 | tf_op jit(solution)/shard_map/ppermute | solution.py:335

commit v10 on v4

--- a/solution.py
+++ b/solution.py
@@ -13,7 +13,6 @@
 LOW = 256
 PACK_FLOPS = 10**10
 PACK_BYTES = 2**24
-CHUNK = 32
 
 
 def in_hbm(array):
@@ -106,11 +105,11 @@
 def memory_kernel(shards, slots, *refs):
     packed_refs, passage_ref = refs[:shards], refs[shards].at[0]
     out_refs = refs[shards + 1 : 2 * shards + 1]
-    query_ref, rank_ref, best_ref, list_ref, scalar_ref, list_sem = refs[2 * shards + 1 :]
+    query_ref, rank_ref, best_ref, list_ref, scalar_ref, *refs = refs[2 * shards + 1 :]
+    most_ref, rounds_ref, list_sems = refs
     q_count = out_refs[0].shape[0]
     p_count = passage_ref.shape[0]
     total, q_tokens, depth = query_ref.shape
-    chunks = p_count // CHUNK
 
     me = lax.axis_index("memory").astype(jnp.float32)
     keys = []
@@ -130,11 +129,12 @@
     earlier = lax.broadcasted_iota(jnp.int32, square, 1) < lax.broadcasted_iota(
         jnp.int32, square, 0
     )
-    before = jnp.dot(earlier.astype(jnp.float32), named, preferred_element_type=jnp.float32)
+    before = jnp.dot(
+        earlier.astype(jnp.bfloat16),
+        named.astype(jnp.bfloat16),
+        preferred_element_type=jnp.float32,
+    )
     rank_ref[...] = jnp.where(named > 0.0, before, -1.0)
-    counts = jnp.sum(named, axis=0, keepdims=True)
-    most = jnp.broadcast_to(jnp.max(counts, axis=1, keepdims=True), counts.shape)
-
     def left_over(first):
         left = jnp.where(rank_ref[...] == first, 1.0, 0.0)
         left = jnp.sum(left, axis=0, keepdims=True)
@@ -157,9 +157,9 @@
         for slot, above in enumerate(extra):
             rows[slot] = rows[slot] + LOW * above
         list_ref[...] = jnp.concatenate(rows, axis=0).astype(jnp.int32)
-        copy = pltpu.make_async_copy(list_ref, scalar_ref, list_sem)
+        copy = pltpu.make_async_copy(list_ref, scalar_ref, list_sems.at[0])
         copy.start()
-        copy.wait()
+        return copy
 
     def unit(index):
         tokens = [query_ref[scalar_ref[slot, index] & (LOW - 1)] for slot in range(SLOTS)]
@@ -174,22 +174,26 @@
                 total_scores = jnp.where(rank == float(slot), sums[slot : slot + 1], total_scores)
             out_ref[...] = total_scores
 
-    write_list(0.0, [most])
-    rounds = (scalar_ref[0, 0] // LOW + SLOTS - 1) // SLOTS
-
-    @pl.loop(0, chunks)
-    def _(chunk):
-        for start in range(0, CHUNK, 8):
-            first = pl.multiple_of(chunk * CHUNK + start, 8)
-            rows = [unit(first + offset) for offset in range(8)]
-            best_ref[pl.ds(first, 8), :] = jnp.concatenate(rows, axis=0)
-
+    list_copy = write_list(0.0, [])
+    counts = jnp.sum(named, axis=0, keepdims=True)
+    most = jnp.broadcast_to(jnp.max(counts, axis=1, keepdims=True), most_ref.shape)
+    most_ref[...] = most.astype(jnp.int32)
+    most_copy = pltpu.make_async_copy(most_ref, rounds_ref, list_sems.at[1])
+    most_copy.start()
+    list_copy.wait()
+
+    for first in range(0, p_count, 8):
+        rows = [unit(first + offset) for offset in range(8)]
+        best_ref[first : first + 8, :] = jnp.concatenate(rows, axis=0)
+
+    most_copy.wait()
+    rounds = (rounds_ref[0, 0] + SLOTS - 1) // SLOTS
     add_scores(0.0, [jnp.zeros((q_count, p_count), jnp.float32)] * shards)
 
     @pl.loop(1, rounds)
     def _(turn):
         done = (turn * SLOTS).astype(jnp.float32)
-        write_list(done, left_over(done))
+        write_list(done, left_over(done)).wait()
 
         @pl.loop(0, scalar_ref[1, 0] // LOW)
         def _(place):
@@ -216,7 +220,9 @@
             pltpu.VMEM((p_count, SLOTS * q_tokens), jnp.float32),
             pltpu.VMEM((SLOTS, p_count), jnp.int32),
             pltpu.SMEM((SLOTS, p_count), jnp.int32),
-            pltpu.SemaphoreType.DMA,
+            pltpu.VMEM((8, LANES), jnp.int32),
+            pltpu.SMEM((8, LANES), jnp.int32),
+            pltpu.SemaphoreType.DMA((2,)),
         ],
         compiler_params=pltpu.CompilerParams(vmem_limit_bytes=16 * MIB),
         cost_estimate=pl.CostEstimate(

time: 25.2 us -> 24.6 us (0.976)
  Pallas kernels: 7.63 us -> 7.09 us
    ppermute x5, waiting for transfers between devices: 0.21 us -> 0.75 us  [to_group(): return lax.ppermute(array, 'group', [(i, i ^ step) for i in range(groups)])]
    pallas_call x1, Pallas kernels: 4.14 us -> 3.59 us  [score_memory(): pl.pallas_call(functools.partial(memory_kernel, shards, slots), in_specs=...]
    ppermute x6, waiting for transfers between devices: 2.35 us -> 1.81 us  [to_shard(): return lax.ppermute(array, 'memory', [(i, i ^ step) for i in range(shards)])]
  transfers between devices with their start and end apart: 11 -> 11, of which waited for: 4 -> 4; matrix products, arithmetic and copies ran while one was open for 0% -> 0% of each run, Pallas kernels for 23% -> 21%
where the time goes in v10:
time: 24.6 us; the launch traced here: 24.5 us
  starting transfers between devices  14.1 us (57%)
  Pallas kernels  7.09 us (29%)
  waiting for transfers between devices  2.56 us (10%)
  between operations  0.73 us (3%)
    ppermute x6, starting transfers between devices, to_shard(): return lax.ppermute(array, 'memory', [(i, i ^ step) for i in range(shards)])  10.2 us
    ppermute x5, starting transfers between devices, to_group(): return lax.ppermute(array, 'group', [(i, i ^ step) for i in range(groups)])  3.88 us
    pallas_call x1, Pallas kernels, score_memory(): pl.pallas_call(functools.partial(memory_kernel, shards, slots), in_specs=...  3.59 us
    ppermute x6, waiting for transfers between devices, to_shard(): return lax.ppermute(array, 'memory', [(i, i ^ step) for i in range(shards)])  1.81 us
    pallas_call x2, Pallas kernels, score_batch(): pl.pallas_call(batch_kernel, out_shape=jax.ShapeDtypeStruct((q_count, lan...  1.67 us
    pallas_call x1, Pallas kernels, pack(): pl.pallas_call(functools.partial(pack_kernel, p_count), in_specs=[vmem, v...  1.02 us
    pallas_call x1, Pallas kernels, finish(): pl.pallas_call(functools.partial(loss_kernel, len(memory_parts)), out_sha...  0.8 us
    ppermute x5, waiting for transfers between devices, to_group(): return lax.ppermute(array, 'group', [(i, i ^ step) for i in range(groups)])  0.75 us
  transfers between devices with their start and end apart: 11, of which 4 were waited for; matrix products, arithmetic and copies ran while one was open for 0% of the time, Pallas kernels for 21%

profile of v10, /device:TPU:0, one launch (start us, length us, event | category | flops | bytes accessed | tf_op | source)
XLA Modules:
  0.0 24.5 jit_solution(17568263986457652755)
XLA Ops:
  0.6 0.0 copy-start.1
  0.7 1.0 %pack.1.refs_0_ = bf16[272,128]{1,0:T(8,128)(2,1)S(1)} custom-call(bf16[1,8,32,128]{3,2,1,0:T(8,128)(2,1)} %query_ref.2, s32[1,8,64]{2,1,0:T(8,128)} %refs_4_.3, s32[1,8]{1,0:T(1,128)} %refs_5_.1), custom_call_target="tpu_custom_call" | custom-call | flops 10000000000 | bytes 16777216 | tf_op jit(solution)/shard_map/pack/pallas_call | solution.py:93
  1.7 0.0 copy-start.2
  1.7 0.0 copy-start.3
  1.7 5.1 %collective-permute-start.3 = (bf16[272,128]{1,0:T(8,128)(2,1)S(1)}, bf16[272,128]{1,0:T(8,128)(2,1)S(1)}, u32[]{:S(2)}, u32[]{:S(2)}) collective-permute-start(bf16[272,128]{1,0:T(8,128)(2,1)S(1)} %pack.1.refs_0_), channel_id=1, source_target_pairs={{0,24},{8,16},{16,8},{24,0},{1,25},{9,17},{17,9},{25,1},{2,26},{10... | collective-permute-start | bytes 208904 | tf_op jit(solution)/shard_map/ppermute | solution.py:334
  6.8 0.0 collective-permute-start.2
  6.8 0.6 %collective-permute-start.1 = (bf16[272,128]{1,0:T(8,128)(2,1)S(1)}, bf16[272,128]{1,0:T(8,128)(2,1)S(1)}, u32[]{:S(2)}, u32[]{:S(2)}) collective-permute-start(bf16[272,128]{1,0:T(8,128)(2,1)S(1)} %pack.1.refs_0_), channel_id=1, source_target_pairs={{0,8},{8,0},{16,24},{24,16},{1,9},{9,1},{17,25},{25,17},{2,10},{10... | collective-permute-start | bytes 208904 | tf_op jit(solution)/shard_map/ppermute | solution.py:334
  7.5 0.0 copy-done
  7.5 2.6 %collective-permute-start.6 = (bf16[1,8,128,128]{3,2,1,0:T(8,128)(2,1)S(1)}, bf16[1,8,128,128]{3,2,1,0:T(8,128)(2,1)S(1)}, u32[]{:S(2)}, u32[]{:S(2)}) collective-permute-start(bf16[1,8,128,128]{3,2,1,0:T(8,128)(2,1)S(1)} %copy-done), channel_id=1, source_target_pairs={{0,6},{1,7},{2,4},{3,5},{4,2},{5,3},{6,0},{7,1},{8,14},{9,15},{10,... | collective-permute-start | bytes 786440 | tf_op jit(solution)/shard_map/ppermute | solution.py:337
  10.1 0.5 %collective-permute-start.5 = (bf16[1,8,128,128]{3,2,1,0:T(8,128)(2,1)S(1)}, bf16[1,8,128,128]{3,2,1,0:T(8,128)(2,1)S(1)}, u32[]{:S(2)}, u32[]{:S(2)}) collective-permute-start(bf16[1,8,128,128]{3,2,1,0:T(8,128)(2,1)S(1)} %copy-done), channel_id=1, source_target_pairs={{0,4},{1,5},{2,6},{3,7},{4,0},{5,1},{6,2},{7,3},{8,12},{9,13},{10,... | collective-permute-start | bytes 786440 | tf_op jit(solution)/shard_map/ppermute | solution.py:337
  10.6 0.0 collective-permute-done.3.refs_3_
  10.6 0.8 %collective-permute-start.4 = (bf16[1,8,128,128]{3,2,1,0:T(8,128)(2,1)S(1)}, bf16[1,8,128,128]{3,2,1,0:T(8,128)(2,1)S(1)}, u32[]{:S(2)}, u32[]{:S(2)}) collective-permute-start(bf16[1,8,128,128]{3,2,1,0:T(8,128)(2,1)S(1)} %copy-done), channel_id=1, source_target_pairs={{0,2},{1,3},{2,0},{3,1},{4,6},{5,7},{6,4},{7,5},{8,10},{9,11},{10,... | collective-permute-start | bytes 786440 | tf_op jit(solution)/shard_map/ppermute | solution.py:337
  11.3 1.4 %collective-permute-done.2.refs_2_ = bf16[272,128]{1,0:T(8,128)(2,1)S(1)} collective-permute-done((bf16[272,128]{1,0:T(8,128)(2,1)S(1)}, bf16[272,128]{1,0:T(8,128)(2,1)S(1)}, u32[]{:S(2)}, u32[]{:S(2)}) %collective-permute-start.2) | collective-permute-done | bytes 69664 | tf_op jit(solution)/shard_map/ppermute | solution.py:334
  12.7 0.0 collective-permute-start
  12.7 0.0 collective-permute-done.1.refs_1_
  12.7 0.0 copy-done.4
  12.8 3.6 %score_memory.1 = (f32[8,128]{1,0:T(8,128)S(1)}, f32[8,128]{1,0:T(8,128)S(1)}, f32[8,128]{1,0:T(8,128)S(1)}, f32[8,128]{1,0:T(8,128)S(1)}) custom-call(bf16[272,128]{1,0:T(8,128)(2,1)S(1)} %pack.1.refs_0_, bf16[272,128]{1,0:T(8,128)(2,1)S(1)} %collective-permute-done.1.refs_1_, bf16[272,128]{1,0:T(8,128)(2,1)S(1)} %collective-permute-done.2.refs_2_, ...), custom_call_target="tpu_custom_call" | custom-call | flops 4294967296 | bytes 4194304 | tf_op jit(solution)/shard_map/score_memory/pallas_call | solution.py:212
  16.4 0.0 collective-permute-done.query_ref
  16.4 2.8 %collective-permute-start.8 = (f32[8,128]{1,0:T(8,128)S(1)}, f32[8,128]{1,0:T(8,128)S(1)}, u32[]{:S(2)}, u32[]{:S(2)}) collective-permute-start(f32[8,128]{1,0:T(8,128)S(1)} %get-tuple-element.16), channel_id=1, source_target_pairs={{0,24},{8,16},{16,8},{24,0},{1,25},{9,17},{17,9},{25,1},{2,26},{10... | collective-permute-start | bytes 12296 | tf_op jit(solution)/shard_map/ppermute | solution.py:334
  19.2 0.0 collective-permute-start.9
  19.2 0.0 collective-permute-done.6.refs_3_
  19.2 1.7 %collective-permute-start.10 = (f32[8,128]{1,0:T(8,128)S(1)}, f32[8,128]{1,0:T(8,128)S(1)}, u32[]{:S(2)}, u32[]{:S(2)}) collective-permute-start(f32[8,128]{1,0:T(8,128)S(1)} %get-tuple-element.18), channel_id=1, source_target_pairs={{0,8},{8,0},{16,24},{24,16},{1,9},{9,1},{17,25},{25,17},{2,10},{10... | collective-permute-start | bytes 12296 | tf_op jit(solution)/shard_map/ppermute | solution.py:334
  20.8 0.6 %collective-permute-done.5.refs_2_ = bf16[1,8,128,128]{3,2,1,0:T(8,128)(2,1)S(1)} collective-permute-done((bf16[1,8,128,128]{3,2,1,0:T(8,128)(2,1)S(1)}, bf16[1,8,128,128]{3,2,1,0:T(8,128)(2,1)S(1)}, u32[]{:S(2)}, u32[]{:S(2)}) %collective-permute-start.5) | collective-permute-done | bytes 262176 | tf_op jit(solution)/shard_map/ppermute | solution.py:337
  21.5 0.1 collective-permute-done.4.refs_1_
  21.6 0.8 %score_batch.2 = f32[8,128]{1,0:T(8,128)S(1)} custom-call(bf16[1,8,32,128]{3,2,1,0:T(8,128)(2,1)S(1)} %collective-permute-done.query_ref, bf16[1,8,128,128]{3,2,1,0:T(8,128)(2,1)S(1)} %copy-done, bf16[1,8,128,128]{3,2,1,0:T(8,128)(2,1)S(1)} %collective-permute-done.4.refs_1_, bf16[1,8,128,128]{3,2,1,0:T(8,128)(2,1)S(1)} %collective-permute-done.5.refs_2_, ...), custom_call_target="tpu_custom_call" | custom-call | flops 268435456 | bytes 1048576 | tf_op jit(solution)/shard_map/score_batch/pallas_call | solution.py:254
  22.4 0.0 collective-permute-start.7
  22.4 0.9 %score_batch.3.own_batch = f32[8,128]{1,0:T(8,128)S(1)} custom-call(bf16[1,8,32,128]{3,2,1,0:T(8,128)(2,1)S(1)} %copy-done.1, bf16[1,8,128,128]{3,2,1,0:T(8,128)(2,1)S(1)} %copy-done, bf16[1,8,128,128]{3,2,1,0:T(8,128)(2,1)S(1)} %collective-permute-done.4.refs_1_, bf16[1,8,128,128]{3,2,1,0:T(8,128)(2,1)S(1)} %collective-permute-done.5.refs_2_, ...), custom_call_target="tpu_custom_call" | custom-call | flops 268435456 | bytes 1048576 | tf_op jit(solution)/shard_map/score_batch/pallas_call | solution.py:254
  23.2 0.0 collective-permute-done.8.refs_1_
  23.3 0.4 %collective-permute-done.9.refs_2_ = f32[8,128]{1,0:T(8,128)S(1)} collective-permute-done((f32[8,128]{1,0:T(8,128)S(1)}, f32[8,128]{1,0:T(8,128)S(1)}, u32[]{:S(2)}, u32[]{:S(2)}) %collective-permute-start.9) | collective-permute-done | bytes 4128 | tf_op jit(solution)/shard_map/ppermute | solution.py:334
  23.7 0.0 collective-permute-done.10.refs_3_
  23.7 0.0 collective-permute-done.7.mate_batch
  23.7 0.8 %finish.1 = (f32[1,8,64]{2,1,0:T(8,128)}, f32[1,8,64]{2,1,0:T(8,128)}, f32[1,8]{1,0:T(1,128)}) custom-call(f32[8,128]{1,0:T(8,128)S(1)} %score_batch.3.own_batch, f32[8,128]{1,0:T(8,128)S(1)} %collective-permute-done.7.mate_batch, f32[8,128]{1,0:T(8,128)S(1)} %get-tuple-element.12.refs_0_, f32[8,128]{1,0:T(8,128)S(1)} %collective-permute-done.8.refs_1_, ...), custom_call_target="tpu_custom_call" | custom-call | tf_op jit(solution)/shard_map/finish/pallas_call | solution.py:314
  (5 shorter events, 0.0 us)
Async XLA Ops:
  0.6 12.1 %copy-start.1 = (bf16[1,8,32,128]{3,2,1,0:T(8,128)(2,1)S(1)}, bf16[1,8,32,128]{3,2,1,0:T(8,128)(2,1)}, u32[]{:S(2)}) copy-start(bf16[1,8,32,128]{3,2,1,0:T(8,128)(2,1)} %query_ref.2) | copy-start | bytes 196612
  0.6 6.8 %copy-start = (bf16[1,8,128,128]{3,2,1,0:T(8,128)(2,1)S(1)}, bf16[1,8,128,128]{3,2,1,0:T(8,128)(2,1)}, u32[]{:S(2)}) copy-start(bf16[1,8,128,128]{3,2,1,0:T(8,128)(2,1)} %refs_0_.3) | copy-start | bytes 786436
  0.7 12.1 %copy-start.4 = (bf16[1,128,128,128]{3,2,1,0:T(8,128)(2,1)S(1)}, bf16[1,128,128,128]{3,2,1,0:T(8,128)(2,1)}, u32[]{:S(2)}) copy-start(bf16[1,128,128,128]{3,2,1,0:T(8,128)(2,1)} %refs_4_.2) | copy-start | bytes 12582916
  1.7 22.0 %copy-start.2 = (s32[1,8,64]{2,1,0:T(8,128)S(1)}, s32[1,8,64]{2,1,0:T(8,128)}, u32[]{:S(2)}) copy-start(s32[1,8,64]{2,1,0:T(8,128)} %refs_4_.3) | copy-start | bytes 6148
  1.7 22.0 %copy-start.3 = (s32[1,8]{1,0:T(1,128)S(1)}, s32[1,8]{1,0:T(1,128)}, u32[]{:S(2)}) copy-start(s32[1,8]{1,0:T(1,128)} %refs_5_.1) | copy-start | bytes 100
  1.7 8.9 %collective-permute-start.3 = (bf16[272,128]{1,0:T(8,128)(2,1)S(1)}, bf16[272,128]{1,0:T(8,128)(2,1)S(1)}, u32[]{:S(2)}, u32[]{:S(2)}) collective-permute-start(bf16[272,128]{1,0:T(8,128)(2,1)S(1)} %pack.1.refs_0_), channel_id=1, source_target_pairs={{0,24},{8,16},{16,8},{24,0},{1,25},{9,17},{17,9},{25,1},{2,26},{10... | collective-permute-start | bytes 208904 | tf_op jit(solution)/shard_map/ppermute | solution.py:334
  6.8 5.9 %collective-permute-start.2 = (bf16[272,128]{1,0:T(8,128)(2,1)S(1)}, bf16[272,128]{1,0:T(8,128)(2,1)S(1)}, u32[]{:S(2)}, u32[]{:S(2)}) collective-permute-start(bf16[272,128]{1,0:T(8,128)(2,1)S(1)} %pack.1.refs_0_), channel_id=1, source_target_pairs={{0,16},{8,24},{16,0},{24,8},{1,17},{9,25},{17,1},{25,9},{2,18},{10... | collective-permute-start | bytes 208904 | tf_op jit(solution)/shard_map/ppermute | solution.py:334
  6.8 5.9 %collective-permute-start.1 = (bf16[272,128]{1,0:T(8,128)(2,1)S(1)}, bf16[272,128]{1,0:T(8,128)(2,1)S(1)}, u32[]{:S(2)}, u32[]{:S(2)}) collective-permute-start(bf16[272,128]{1,0:T(8,128)(2,1)S(1)} %pack.1.refs_0_), channel_id=1, source_target_pairs={{0,8},{8,0},{16,24},{24,16},{1,9},{9,1},{17,25},{25,17},{2,10},{10... | collective-permute-start | bytes 208904 | tf_op jit(solution)/shard_map/ppermute | solution.py:334
  7.5 11.7 %collective-permute-start.6 = (bf16[1,8,128,128]{3,2,1,0:T(8,128)(2,1)S(1)}, bf16[1,8,128,128]{3,2,1,0:T(8,128)(2,1)S(1)}, u32[]{:S(2)}, u32[]{:S(2)}) collective-permute-start(bf16[1,8,128,128]{3,2,1,0:T(8,128)(2,1)S(1)} %copy-done), channel_id=1, source_target_pairs={{0,6},{1,7},{2,4},{3,5},{4,2},{5,3},{6,0},{7,1},{8,14},{9,15},{10,... | collective-permute-start | bytes 786440 | tf_op jit(solution)/shard_map/ppermute | solution.py:337
  10.1 11.4 %collective-permute-start.5 = (bf16[1,8,128,128]{3,2,1,0:T(8,128)(2,1)S(1)}, bf16[1,8,128,128]{3,2,1,0:T(8,128)(2,1)S(1)}, u32[]{:S(2)}, u32[]{:S(2)}) collective-permute-start(bf16[1,8,128,128]{3,2,1,0:T(8,128)(2,1)S(1)} %copy-done), channel_id=1, source_target_pairs={{0,4},{1,5},{2,6},{3,7},{4,0},{5,1},{6,2},{7,3},{8,12},{9,13},{10,... | collective-permute-start | bytes 786440 | tf_op jit(solution)/shard_map/ppermute | solution.py:337
  10.6 11.0 %collective-permute-start.4 = (bf16[1,8,128,128]{3,2,1,0:T(8,128)(2,1)S(1)}, bf16[1,8,128,128]{3,2,1,0:T(8,128)(2,1)S(1)}, u32[]{:S(2)}, u32[]{:S(2)}) collective-permute-start(bf16[1,8,128,128]{3,2,1,0:T(8,128)(2,1)S(1)} %copy-done), channel_id=1, source_target_pairs={{0,2},{1,3},{2,0},{3,1},{4,6},{5,7},{6,4},{7,5},{8,10},{9,11},{10,... | collective-permute-start | bytes 786440 | tf_op jit(solution)/shard_map/ppermute | solution.py:337
  12.7 3.6 %collective-permute-start = (bf16[1,8,32,128]{3,2,1,0:T(8,128)(2,1)S(1)}, bf16[1,8,32,128]{3,2,1,0:T(8,128)(2,1)S(1)}, u32[]{:S(2)}, u32[]{:S(2)}) collective-permute-start(bf16[1,8,32,128]{3,2,1,0:T(8,128)(2,1)S(1)} %copy-done.1), channel_id=1, source_target_pairs={{0,1},{1,0},{2,3},{3,2},{4,5},{5,4},{6,7},{7,6},{8,9},{9,8},{10,11... | collective-permute-start | bytes 196616 | tf_op jit(solution)/shard_map/ppermute | solution.py:337
  16.4 6.9 %collective-permute-start.8 = (f32[8,128]{1,0:T(8,128)S(1)}, f32[8,128]{1,0:T(8,128)S(1)}, u32[]{:S(2)}, u32[]{:S(2)}) collective-permute-start(f32[8,128]{1,0:T(8,128)S(1)} %get-tuple-element.16), channel_id=1, source_target_pairs={{0,24},{8,16},{16,8},{24,0},{1,25},{9,17},{17,9},{25,1},{2,26},{10... | collective-permute-start | bytes 12296 | tf_op jit(solution)/shard_map/ppermute | solution.py:334
  19.2 4.5 %collective-permute-start.9 = (f32[8,128]{1,0:T(8,128)S(1)}, f32[8,128]{1,0:T(8,128)S(1)}, u32[]{:S(2)}, u32[]{:S(2)}) collective-permute-start(f32[8,128]{1,0:T(8,128)S(1)} %get-tuple-element.17), channel_id=1, source_target_pairs={{0,16},{8,24},{16,0},{24,8},{1,17},{9,25},{17,1},{25,9},{2,18},{10... | collective-permute-start | bytes 12296 | tf_op jit(solution)/shard_map/ppermute | solution.py:334
  19.2 4.5 %collective-permute-start.10 = (f32[8,128]{1,0:T(8,128)S(1)}, f32[8,128]{1,0:T(8,128)S(1)}, u32[]{:S(2)}, u32[]{:S(2)}) collective-permute-start(f32[8,128]{1,0:T(8,128)S(1)} %get-tuple-element.18), channel_id=1, source_target_pairs={{0,8},{8,0},{16,24},{24,16},{1,9},{9,1},{17,25},{25,17},{2,10},{10... | collective-permute-start | bytes 12296 | tf_op jit(solution)/shard_map/ppermute | solution.py:334
  22.4 1.3 %collective-permute-start.7 = (f32[8,128]{1,0:T(8,128)S(1)}, f32[8,128]{1,0:T(8,128)S(1)}, u32[]{:S(2)}, u32[]{:S(2)}) collective-permute-start(f32[8,128]{1,0:T(8,128)S(1)} %score_batch.2), channel_id=1, source_target_pairs={{0,1},{1,0},{2,3},{3,2},{4,5},{5,4},{6,7},{7,6},{8,9},{9,8},{10,11... | collective-permute-start | bytes 12296 | tf_op jit(solution)/shard_map/ppermute | solution.py:337

commit v11 on v10

--- a/solution.py
+++ b/solution.py
@@ -11,6 +11,7 @@
 MIB = 1024 * 1024
 SLOTS = 8
 LOW = 256
+HALF = 64
 PACK_FLOPS = 10**10
 PACK_BYTES = 2**24
 
@@ -165,8 +166,7 @@
         tokens = [query_ref[scalar_ref[slot, index] & (LOW - 1)] for slot in range(SLOTS)]
         return token_max(passage_ref[pl.ds(index, 1)], jnp.concatenate(tokens, axis=0))
 
-    def add_scores(first, scores):
-        sums = token_sum(best_ref[...], SLOTS)
+    def add_scores(first, scores, sums):
         for index, out_ref in enumerate(out_refs):
             rank = rank_ref[index * q_count : (index + 1) * q_count] - first
             total_scores = scores[index]
@@ -182,13 +182,15 @@
     most_copy.start()
     list_copy.wait()
 
-    for first in range(0, p_count, 8):
-        rows = [unit(first + offset) for offset in range(8)]
-        best_ref[first : first + 8, :] = jnp.concatenate(rows, axis=0)
+    sums = []
+    for first in range(0, p_count, HALF):
+        rows = [unit(index) for index in range(first, first + HALF)]
+        sums.append(token_sum(jnp.concatenate(rows, axis=0), SLOTS))
 
     most_copy.wait()
     rounds = (rounds_ref[0, 0] + SLOTS - 1) // SLOTS
-    add_scores(0.0, [jnp.zeros((q_count, p_count), jnp.float32)] * shards)
+    nothing = [jnp.zeros((q_count, p_count), jnp.float32)] * shards
+    add_scores(0.0, nothing, jnp.concatenate(sums, axis=1))
 
     @pl.loop(1, rounds)
     def _(turn):
@@ -200,7 +202,8 @@
             index = scalar_ref[0, place] // LOW
             best_ref[pl.ds(index, 1), :] = unit(index)
 
-        add_scores(done, [out_ref[...] for out_ref in out_refs])
+        scores = [out_ref[...] for out_ref in out_refs]
+        add_scores(done, scores, token_sum(best_ref[...], SLOTS))
 
 
 def score_memory(packed, memory, q_count, slots):

time: 24.6 us -> 24.7 us (level)
  transfers between devices with their start and end apart: 11 -> 11, of which waited for: 4 -> 4; matrix products, arithmetic and copies ran while one was open for 0% -> 0% of each run, Pallas kernels for 21% -> 22%
where the time goes in v11:
time: 24.7 us; the launch traced here: 24.6 us
  starting transfers between devices  14.1 us (57%)
  Pallas kernels  7.2 us (29%)
  waiting for transfers between devices  2.56 us (10%)
  between operations  0.73 us (3%)
    ppermute x6, starting transfers between devices, to_shard(): return lax.ppermute(array, 'memory', [(i, i ^ step) for i in range(shards)])  10.2 us
    ppermute x5, starting transfers between devices, to_group(): return lax.ppermute(array, 'group', [(i, i ^ step) for i in range(groups)])  3.88 us
    pallas_call x1, Pallas kernels, score_memory(): pl.pallas_call(functools.partial(memory_kernel, shards, slots), in_specs=...  3.71 us
    ppermute x6, waiting for transfers between devices, to_shard(): return lax.ppermute(array, 'memory', [(i, i ^ step) for i in range(shards)])  1.92 us
    pallas_call x2, Pallas kernels, score_batch(): pl.pallas_call(batch_kernel, out_shape=jax.ShapeDtypeStruct((q_count, lan...  1.67 us
    pallas_call x1, Pallas kernels, pack(): pl.pallas_call(functools.partial(pack_kernel, p_count), in_specs=[vmem, v...  1.02 us
    pallas_call x1, Pallas kernels, finish(): pl.pallas_call(functools.partial(loss_kernel, len(memory_parts)), out_sha...  0.8 us
    ppermute x5, waiting for transfers between devices, to_group(): return lax.ppermute(array, 'group', [(i, i ^ step) for i in range(groups)])  0.64 us
  transfers between devices with their start and end apart: 11, of which 4 were waited for; matrix products, arithmetic and copies ran while one was open for 0% of the time, Pallas kernels for 22%

profile of v11, /device:TPU:0, one launch (start us, length us, event | category | flops | bytes accessed | tf_op | source)
XLA Modules:
  0.0 24.6 jit_solution(4104504840767584858)
XLA Ops:
  0.6 0.0 copy-start.1
  0.7 1.0 %pack.1.refs_0_ = bf16[272,128]{1,0:T(8,128)(2,1)S(1)} custom-call(bf16[1,8,32,128]{3,2,1,0:T(8,128)(2,1)} %query_ref.2, s32[1,8,64]{2,1,0:T(8,128)} %refs_4_.3, s32[1,8]{1,0:T(1,128)} %refs_5_.1), custom_call_target="tpu_custom_call" | custom-call | flops 10000000000 | bytes 16777216 | tf_op jit(solution)/shard_map/pack/pallas_call | solution.py:94
  1.7 0.0 copy-start.2
  1.7 0.0 copy-start.3
  1.7 5.1 %collective-permute-start.3 = (bf16[272,128]{1,0:T(8,128)(2,1)S(1)}, bf16[272,128]{1,0:T(8,128)(2,1)S(1)}, u32[]{:S(2)}, u32[]{:S(2)}) collective-permute-start(bf16[272,128]{1,0:T(8,128)(2,1)S(1)} %pack.1.refs_0_), channel_id=1, source_target_pairs={{0,24},{8,16},{16,8},{24,0},{1,25},{9,17},{17,9},{25,1},{2,26},{10... | collective-permute-start | bytes 208904 | tf_op jit(solution)/shard_map/ppermute | solution.py:337
  6.8 0.0 collective-permute-start.2
  6.8 0.6 %collective-permute-start.1 = (bf16[272,128]{1,0:T(8,128)(2,1)S(1)}, bf16[272,128]{1,0:T(8,128)(2,1)S(1)}, u32[]{:S(2)}, u32[]{:S(2)}) collective-permute-start(bf16[272,128]{1,0:T(8,128)(2,1)S(1)} %pack.1.refs_0_), channel_id=1, source_target_pairs={{0,8},{8,0},{16,24},{24,16},{1,9},{9,1},{17,25},{25,17},{2,10},{10... | collective-permute-start | bytes 208904 | tf_op jit(solution)/shard_map/ppermute | solution.py:337
  7.5 0.0 copy-done
  7.5 2.6 %collective-permute-start.6 = (bf16[1,8,128,128]{3,2,1,0:T(8,128)(2,1)S(1)}, bf16[1,8,128,128]{3,2,1,0:T(8,128)(2,1)S(1)}, u32[]{:S(2)}, u32[]{:S(2)}) collective-permute-start(bf16[1,8,128,128]{3,2,1,0:T(8,128)(2,1)S(1)} %copy-done), channel_id=1, source_target_pairs={{0,6},{1,7},{2,4},{3,5},{4,2},{5,3},{6,0},{7,1},{8,14},{9,15},{10,... | collective-permute-start | bytes 786440 | tf_op jit(solution)/shard_map/ppermute | solution.py:340
  10.1 0.5 %collective-permute-start.5 = (bf16[1,8,128,128]{3,2,1,0:T(8,128)(2,1)S(1)}, bf16[1,8,128,128]{3,2,1,0:T(8,128)(2,1)S(1)}, u32[]{:S(2)}, u32[]{:S(2)}) collective-permute-start(bf16[1,8,128,128]{3,2,1,0:T(8,128)(2,1)S(1)} %copy-done), channel_id=1, source_target_pairs={{0,4},{1,5},{2,6},{3,7},{4,0},{5,1},{6,2},{7,3},{8,12},{9,13},{10,... | collective-permute-start | bytes 786440 | tf_op jit(solution)/shard_map/ppermute | solution.py:340
  10.6 0.0 collective-permute-done.3.refs_3_
  10.6 0.8 %collective-permute-start.4 = (bf16[1,8,128,128]{3,2,1,0:T(8,128)(2,1)S(1)}, bf16[1,8,128,128]{3,2,1,0:T(8,128)(2,1)S(1)}, u32[]{:S(2)}, u32[]{:S(2)}) collective-permute-start(bf16[1,8,128,128]{3,2,1,0:T(8,128)(2,1)S(1)} %copy-done), channel_id=1, source_target_pairs={{0,2},{1,3},{2,0},{3,1},{4,6},{5,7},{6,4},{7,5},{8,10},{9,11},{10,... | collective-permute-start | bytes 786440 | tf_op jit(solution)/shard_map/ppermute | solution.py:340
  11.3 1.4 %collective-permute-done.2.refs_2_ = bf16[272,128]{1,0:T(8,128)(2,1)S(1)} collective-permute-done((bf16[272,128]{1,0:T(8,128)(2,1)S(1)}, bf16[272,128]{1,0:T(8,128)(2,1)S(1)}, u32[]{:S(2)}, u32[]{:S(2)}) %collective-permute-start.2) | collective-permute-done | bytes 69664 | tf_op jit(solution)/shard_map/ppermute | solution.py:337
  12.7 0.0 collective-permute-start
  12.7 0.0 collective-permute-done.1.refs_1_
  12.7 0.0 copy-done.4
  12.8 3.7 %score_memory.1 = (f32[8,128]{1,0:T(8,128)S(1)}, f32[8,128]{1,0:T(8,128)S(1)}, f32[8,128]{1,0:T(8,128)S(1)}, f32[8,128]{1,0:T(8,128)S(1)}) custom-call(bf16[272,128]{1,0:T(8,128)(2,1)S(1)} %pack.1.refs_0_, bf16[272,128]{1,0:T(8,128)(2,1)S(1)} %collective-permute-done.1.refs_1_, bf16[272,128]{1,0:T(8,128)(2,1)S(1)} %collective-permute-done.2.refs_2_, ...), custom_call_target="tpu_custom_call" | custom-call | flops 4294967296 | bytes 4194304 | tf_op jit(solution)/shard_map/score_memory/pallas_call | solution.py:215
  16.5 0.0 collective-permute-done.query_ref
  16.5 2.8 %collective-permute-start.8 = (f32[8,128]{1,0:T(8,128)S(1)}, f32[8,128]{1,0:T(8,128)S(1)}, u32[]{:S(2)}, u32[]{:S(2)}) collective-permute-start(f32[8,128]{1,0:T(8,128)S(1)} %get-tuple-element.16), channel_id=1, source_target_pairs={{0,24},{8,16},{16,8},{24,0},{1,25},{9,17},{17,9},{25,1},{2,26},{10... | collective-permute-start | bytes 12296 | tf_op jit(solution)/shard_map/ppermute | solution.py:337
  19.3 0.0 collective-permute-start.9
  19.3 0.0 collective-permute-done.6.refs_3_
  19.3 1.7 %collective-permute-start.10 = (f32[8,128]{1,0:T(8,128)S(1)}, f32[8,128]{1,0:T(8,128)S(1)}, u32[]{:S(2)}, u32[]{:S(2)}) collective-permute-start(f32[8,128]{1,0:T(8,128)S(1)} %get-tuple-element.18), channel_id=1, source_target_pairs={{0,8},{8,0},{16,24},{24,16},{1,9},{9,1},{17,25},{25,17},{2,10},{10... | collective-permute-start | bytes 12296 | tf_op jit(solution)/shard_map/ppermute | solution.py:337
  20.9 0.5 %collective-permute-done.5.refs_2_ = bf16[1,8,128,128]{3,2,1,0:T(8,128)(2,1)S(1)} collective-permute-done((bf16[1,8,128,128]{3,2,1,0:T(8,128)(2,1)S(1)}, bf16[1,8,128,128]{3,2,1,0:T(8,128)(2,1)S(1)}, u32[]{:S(2)}, u32[]{:S(2)}) %collective-permute-start.5) | collective-permute-done | bytes 262176 | tf_op jit(solution)/shard_map/ppermute | solution.py:340
  21.5 0.1 collective-permute-done.4.refs_1_
  21.6 0.8 %score_batch.2 = f32[8,128]{1,0:T(8,128)S(1)} custom-call(bf16[1,8,32,128]{3,2,1,0:T(8,128)(2,1)S(1)} %collective-permute-done.query_ref, bf16[1,8,128,128]{3,2,1,0:T(8,128)(2,1)S(1)} %copy-done, bf16[1,8,128,128]{3,2,1,0:T(8,128)(2,1)S(1)} %collective-permute-done.4.refs_1_, bf16[1,8,128,128]{3,2,1,0:T(8,128)(2,1)S(1)} %collective-permute-done.5.refs_2_, ...), custom_call_target="tpu_custom_call" | custom-call | flops 268435456 | bytes 1048576 | tf_op jit(solution)/shard_map/score_batch/pallas_call | solution.py:257
  22.4 0.0 collective-permute-start.7
  22.4 0.9 %score_batch.3.own_batch = f32[8,128]{1,0:T(8,128)S(1)} custom-call(bf16[1,8,32,128]{3,2,1,0:T(8,128)(2,1)S(1)} %copy-done.1, bf16[1,8,128,128]{3,2,1,0:T(8,128)(2,1)S(1)} %copy-done, bf16[1,8,128,128]{3,2,1,0:T(8,128)(2,1)S(1)} %collective-permute-done.4.refs_1_, bf16[1,8,128,128]{3,2,1,0:T(8,128)(2,1)S(1)} %collective-permute-done.5.refs_2_, ...), custom_call_target="tpu_custom_call" | custom-call | flops 268435456 | bytes 1048576 | tf_op jit(solution)/shard_map/score_batch/pallas_call | solution.py:257
  23.2 0.0 collective-permute-done.8.refs_1_
  23.3 0.5 %collective-permute-done.9.refs_2_ = f32[8,128]{1,0:T(8,128)S(1)} collective-permute-done((f32[8,128]{1,0:T(8,128)S(1)}, f32[8,128]{1,0:T(8,128)S(1)}, u32[]{:S(2)}, u32[]{:S(2)}) %collective-permute-start.9) | collective-permute-done | bytes 4128 | tf_op jit(solution)/shard_map/ppermute | solution.py:337
  23.8 0.0 collective-permute-done.10.refs_3_
  23.8 0.0 collective-permute-done.7.mate_batch
  23.8 0.8 %finish.1 = (f32[1,8,64]{2,1,0:T(8,128)}, f32[1,8,64]{2,1,0:T(8,128)}, f32[1,8]{1,0:T(1,128)}) custom-call(f32[8,128]{1,0:T(8,128)S(1)} %score_batch.3.own_batch, f32[8,128]{1,0:T(8,128)S(1)} %collective-permute-done.7.mate_batch, f32[8,128]{1,0:T(8,128)S(1)} %get-tuple-element.12.refs_0_, f32[8,128]{1,0:T(8,128)S(1)} %collective-permute-done.8.refs_1_, ...), custom_call_target="tpu_custom_call" | custom-call | tf_op jit(solution)/shard_map/finish/pallas_call | solution.py:317
  (5 shorter events, 0.0 us)
Async XLA Ops:
  0.6 12.1 %copy-start.1 = (bf16[1,8,32,128]{3,2,1,0:T(8,128)(2,1)S(1)}, bf16[1,8,32,128]{3,2,1,0:T(8,128)(2,1)}, u32[]{:S(2)}) copy-start(bf16[1,8,32,128]{3,2,1,0:T(8,128)(2,1)} %query_ref.2) | copy-start | bytes 196612
  0.6 6.8 %copy-start = (bf16[1,8,128,128]{3,2,1,0:T(8,128)(2,1)S(1)}, bf16[1,8,128,128]{3,2,1,0:T(8,128)(2,1)}, u32[]{:S(2)}) copy-start(bf16[1,8,128,128]{3,2,1,0:T(8,128)(2,1)} %refs_0_.3) | copy-start | bytes 786436
  0.7 12.1 %copy-start.4 = (bf16[1,128,128,128]{3,2,1,0:T(8,128)(2,1)S(1)}, bf16[1,128,128,128]{3,2,1,0:T(8,128)(2,1)}, u32[]{:S(2)}) copy-start(bf16[1,128,128,128]{3,2,1,0:T(8,128)(2,1)} %refs_4_.2) | copy-start | bytes 12582916
  1.7 22.1 %copy-start.2 = (s32[1,8,64]{2,1,0:T(8,128)S(1)}, s32[1,8,64]{2,1,0:T(8,128)}, u32[]{:S(2)}) copy-start(s32[1,8,64]{2,1,0:T(8,128)} %refs_4_.3) | copy-start | bytes 6148
  1.7 22.1 %copy-start.3 = (s32[1,8]{1,0:T(1,128)S(1)}, s32[1,8]{1,0:T(1,128)}, u32[]{:S(2)}) copy-start(s32[1,8]{1,0:T(1,128)} %refs_5_.1) | copy-start | bytes 100
  1.7 8.9 %collective-permute-start.3 = (bf16[272,128]{1,0:T(8,128)(2,1)S(1)}, bf16[272,128]{1,0:T(8,128)(2,1)S(1)}, u32[]{:S(2)}, u32[]{:S(2)}) collective-permute-start(bf16[272,128]{1,0:T(8,128)(2,1)S(1)} %pack.1.refs_0_), channel_id=1, source_target_pairs={{0,24},{8,16},{16,8},{24,0},{1,25},{9,17},{17,9},{25,1},{2,26},{10... | collective-permute-start | bytes 208904 | tf_op jit(solution)/shard_map/ppermute | solution.py:337
  6.8 5.9 %collective-permute-start.2 = (bf16[272,128]{1,0:T(8,128)(2,1)S(1)}, bf16[272,128]{1,0:T(8,128)(2,1)S(1)}, u32[]{:S(2)}, u32[]{:S(2)}) collective-permute-start(bf16[272,128]{1,0:T(8,128)(2,1)S(1)} %pack.1.refs_0_), channel_id=1, source_target_pairs={{0,16},{8,24},{16,0},{24,8},{1,17},{9,25},{17,1},{25,9},{2,18},{10... | collective-permute-start | bytes 208904 | tf_op jit(solution)/shard_map/ppermute | solution.py:337
  6.8 5.9 %collective-permute-start.1 = (bf16[272,128]{1,0:T(8,128)(2,1)S(1)}, bf16[272,128]{1,0:T(8,128)(2,1)S(1)}, u32[]{:S(2)}, u32[]{:S(2)}) collective-permute-start(bf16[272,128]{1,0:T(8,128)(2,1)S(1)} %pack.1.refs_0_), channel_id=1, source_target_pairs={{0,8},{8,0},{16,24},{24,16},{1,9},{9,1},{17,25},{25,17},{2,10},{10... | collective-permute-start | bytes 208904 | tf_op jit(solution)/shard_map/ppermute | solution.py:337
  7.5 11.8 %collective-permute-start.6 = (bf16[1,8,128,128]{3,2,1,0:T(8,128)(2,1)S(1)}, bf16[1,8,128,128]{3,2,1,0:T(8,128)(2,1)S(1)}, u32[]{:S(2)}, u32[]{:S(2)}) collective-permute-start(bf16[1,8,128,128]{3,2,1,0:T(8,128)(2,1)S(1)} %copy-done), channel_id=1, source_target_pairs={{0,6},{1,7},{2,4},{3,5},{4,2},{5,3},{6,0},{7,1},{8,14},{9,15},{10,... | collective-permute-start | bytes 786440 | tf_op jit(solution)/shard_map/ppermute | solution.py:340
  10.1 11.4 %collective-permute-start.5 = (bf16[1,8,128,128]{3,2,1,0:T(8,128)(2,1)S(1)}, bf16[1,8,128,128]{3,2,1,0:T(8,128)(2,1)S(1)}, u32[]{:S(2)}, u32[]{:S(2)}) collective-permute-start(bf16[1,8,128,128]{3,2,1,0:T(8,128)(2,1)S(1)} %copy-done), channel_id=1, source_target_pairs={{0,4},{1,5},{2,6},{3,7},{4,0},{5,1},{6,2},{7,3},{8,12},{9,13},{10,... | collective-permute-start | bytes 786440 | tf_op jit(solution)/shard_map/ppermute | solution.py:340
  10.6 11.0 %collective-permute-start.4 = (bf16[1,8,128,128]{3,2,1,0:T(8,128)(2,1)S(1)}, bf16[1,8,128,128]{3,2,1,0:T(8,128)(2,1)S(1)}, u32[]{:S(2)}, u32[]{:S(2)}) collective-permute-start(bf16[1,8,128,128]{3,2,1,0:T(8,128)(2,1)S(1)} %copy-done), channel_id=1, source_target_pairs={{0,2},{1,3},{2,0},{3,1},{4,6},{5,7},{6,4},{7,5},{8,10},{9,11},{10,... | collective-permute-start | bytes 786440 | tf_op jit(solution)/shard_map/ppermute | solution.py:340
  12.7 3.7 %collective-permute-start = (bf16[1,8,32,128]{3,2,1,0:T(8,128)(2,1)S(1)}, bf16[1,8,32,128]{3,2,1,0:T(8,128)(2,1)S(1)}, u32[]{:S(2)}, u32[]{:S(2)}) collective-permute-start(bf16[1,8,32,128]{3,2,1,0:T(8,128)(2,1)S(1)} %copy-done.1), channel_id=1, source_target_pairs={{0,1},{1,0},{2,3},{3,2},{4,5},{5,4},{6,7},{7,6},{8,9},{9,8},{10,11... | collective-permute-start | bytes 196616 | tf_op jit(solution)/shard_map/ppermute | solution.py:340
  16.5 6.8 %collective-permute-start.8 = (f32[8,128]{1,0:T(8,128)S(1)}, f32[8,128]{1,0:T(8,128)S(1)}, u32[]{:S(2)}, u32[]{:S(2)}) collective-permute-start(f32[8,128]{1,0:T(8,128)S(1)} %get-tuple-element.16), channel_id=1, source_target_pairs={{0,24},{8,16},{16,8},{24,0},{1,25},{9,17},{17,9},{25,1},{2,26},{10... | collective-permute-start | bytes 12296 | tf_op jit(solution)/shard_map/ppermute | solution.py:337
  19.3 4.5 %collective-permute-start.9 = (f32[8,128]{1,0:T(8,128)S(1)}, f32[8,128]{1,0:T(8,128)S(1)}, u32[]{:S(2)}, u32[]{:S(2)}) collective-permute-start(f32[8,128]{1,0:T(8,128)S(1)} %get-tuple-element.17), channel_id=1, source_target_pairs={{0,16},{8,24},{16,0},{24,8},{1,17},{9,25},{17,1},{25,9},{2,18},{10... | collective-permute-start | bytes 12296 | tf_op jit(solution)/shard_map/ppermute | solution.py:337
  19.3 4.5 %collective-permute-start.10 = (f32[8,128]{1,0:T(8,128)S(1)}, f32[8,128]{1,0:T(8,128)S(1)}, u32[]{:S(2)}, u32[]{:S(2)}) collective-permute-start(f32[8,128]{1,0:T(8,128)S(1)} %get-tuple-element.18), channel_id=1, source_target_pairs={{0,8},{8,0},{16,24},{24,16},{1,9},{9,1},{17,25},{25,17},{2,10},{10... | collective-permute-start | bytes 12296 | tf_op jit(solution)/shard_map/ppermute | solution.py:337
  22.4 1.4 %collective-permute-start.7 = (f32[8,128]{1,0:T(8,128)S(1)}, f32[8,128]{1,0:T(8,128)S(1)}, u32[]{:S(2)}, u32[]{:S(2)}) collective-permute-start(f32[8,128]{1,0:T(8,128)S(1)} %score_batch.2), channel_id=1, source_target_pairs={{0,1},{1,0},{2,3},{3,2},{4,5},{5,4},{6,7},{7,6},{8,9},{9,8},{10,11... | collective-permute-start | bytes 12296 | tf_op jit(solution)/shard_map/ppermute | solution.py:340

commit v12 on v10

--- a/solution.py
+++ b/solution.py
@@ -113,9 +113,7 @@
 
     me = lax.axis_index("memory").astype(jnp.float32)
     keys = []
-    for index, packed_ref in enumerate(packed_refs):
-        tokens = packed_ref[: q_count * q_tokens].reshape(q_count, q_tokens, depth)
-        query_ref[index * q_count : (index + 1) * q_count] = tokens
+    for packed_ref in packed_refs:
         planes = packed_ref[q_count * q_tokens :].astype(jnp.float32)
         local, holder = planes[:q_count], planes[q_count:]
         keys.append(jnp.where(holder == me, local, -1.0))
@@ -175,6 +173,9 @@
             out_ref[...] = total_scores
 
     list_copy = write_list(0.0, [])
+    for index, packed_ref in enumerate(packed_refs):
+        tokens = packed_ref[: q_count * q_tokens].reshape(q_count, q_tokens, depth)
+        query_ref[index * q_count : (index + 1) * q_count] = tokens
     counts = jnp.sum(named, axis=0, keepdims=True)
     most = jnp.broadcast_to(jnp.max(counts, axis=1, keepdims=True), most_ref.shape)
     most_ref[...] = most.astype(jnp.int32)
@@ -240,7 +241,8 @@
     count = passage_refs[0].shape[1]
     tokens = query_ref[0].reshape(queries * q_tokens, depth)
     for chip, passage_ref in enumerate(passage_refs):
-        best_ref[chip * count : (chip + 1) * count, :] = token_max(passage_ref[0], tokens)
+        rows = [token_max(passage_ref[0, index : index + 1], tokens) for index in range(count)]
+        best_ref[chip * count : (chip + 1) * count, :] = jnp.concatenate(rows, axis=0)
     sums = token_sum(best_ref[...], queries)
     empty = jnp.zeros((queries, out_ref.shape[1] - sums.shape[1]), jnp.float32)
     out_ref[...] = jnp.concatenate([sums, empty], axis=1) if empty.size else sums

time: 24.6 us -> 24.6 us (level)
  transfers between devices with their start and end apart: 11 -> 11, of which waited for: 4 -> 4; matrix products, arithmetic and copies ran while one was open for 0% -> 0% of each run, Pallas kernels for 21% -> 22%
where the time goes in v12:
time: 24.6 us; the launch traced here: 24.5 us
  starting transfers between devices  14.1 us (57%)
  Pallas kernels  7.1 us (29%)
  waiting for transfers between devices  2.55 us (10%)
  between operations  0.73 us (3%)
    ppermute x6, starting transfers between devices, to_shard(): return lax.ppermute(array, 'memory', [(i, i ^ step) for i in range(shards)])  10.2 us
    ppermute x5, starting transfers between devices, to_group(): return lax.ppermute(array, 'group', [(i, i ^ step) for i in range(groups)])  3.88 us
    pallas_call x1, Pallas kernels, score_memory(): pl.pallas_call(functools.partial(memory_kernel, shards, slots), in_specs=...  3.59 us
    ppermute x6, waiting for transfers between devices, to_shard(): return lax.ppermute(array, 'memory', [(i, i ^ step) for i in range(shards)])  1.8 us
    pallas_call x2, Pallas kernels, score_batch(): pl.pallas_call(batch_kernel, out_shape=jax.ShapeDtypeStruct((q_count, lan...  1.68 us
    pallas_call x1, Pallas kernels, pack(): pl.pallas_call(functools.partial(pack_kernel, p_count), in_specs=[vmem, v...  1.02 us
    pallas_call x1, Pallas kernels, finish(): pl.pallas_call(functools.partial(loss_kernel, len(memory_parts)), out_sha...  0.8 us
    ppermute x5, waiting for transfers between devices, to_group(): return lax.ppermute(array, 'group', [(i, i ^ step) for i in range(groups)])  0.75 us
  transfers between devices with their start and end apart: 11, of which 4 were waited for; matrix products, arithmetic and copies ran while one was open for 0% of the time, Pallas kernels for 22%

profile of v12, /device:TPU:0, one launch (start us, length us, event | category | flops | bytes accessed | tf_op | source)
XLA Modules:
  0.0 24.5 jit_solution(8954655422595852269)
XLA Ops:
  0.6 0.0 copy-start.1
  0.6 0.0 copy-start
  0.7 1.0 %pack.1.refs_0_ = bf16[272,128]{1,0:T(8,128)(2,1)S(1)} custom-call(bf16[1,8,32,128]{3,2,1,0:T(8,128)(2,1)} %query_ref.2, s32[1,8,64]{2,1,0:T(8,128)} %refs_4_.3, s32[1,8]{1,0:T(1,128)} %refs_5_.1), custom_call_target="tpu_custom_call" | custom-call | flops 10000000000 | bytes 16777216 | tf_op jit(solution)/shard_map/pack/pallas_call | solution.py:93
  1.7 0.0 copy-start.2
  1.7 0.0 copy-start.3
  1.7 5.1 %collective-permute-start.3 = (bf16[272,128]{1,0:T(8,128)(2,1)S(1)}, bf16[272,128]{1,0:T(8,128)(2,1)S(1)}, u32[]{:S(2)}, u32[]{:S(2)}) collective-permute-start(bf16[272,128]{1,0:T(8,128)(2,1)S(1)} %pack.1.refs_0_), channel_id=1, source_target_pairs={{0,24},{8,16},{16,8},{24,0},{1,25},{9,17},{17,9},{25,1},{2,26},{10... | collective-permute-start | bytes 208904 | tf_op jit(solution)/shard_map/ppermute | solution.py:336
  6.8 0.0 collective-permute-start.2
  6.8 0.6 %collective-permute-start.1 = (bf16[272,128]{1,0:T(8,128)(2,1)S(1)}, bf16[272,128]{1,0:T(8,128)(2,1)S(1)}, u32[]{:S(2)}, u32[]{:S(2)}) collective-permute-start(bf16[272,128]{1,0:T(8,128)(2,1)S(1)} %pack.1.refs_0_), channel_id=1, source_target_pairs={{0,8},{8,0},{16,24},{24,16},{1,9},{9,1},{17,25},{25,17},{2,10},{10... | collective-permute-start | bytes 208904 | tf_op jit(solution)/shard_map/ppermute | solution.py:336
  7.5 2.6 %collective-permute-start.6 = (bf16[1,8,128,128]{3,2,1,0:T(8,128)(2,1)S(1)}, bf16[1,8,128,128]{3,2,1,0:T(8,128)(2,1)S(1)}, u32[]{:S(2)}, u32[]{:S(2)}) collective-permute-start(bf16[1,8,128,128]{3,2,1,0:T(8,128)(2,1)S(1)} %copy-done), channel_id=1, source_target_pairs={{0,6},{1,7},{2,4},{3,5},{4,2},{5,3},{6,0},{7,1},{8,14},{9,15},{10,... | collective-permute-start | bytes 786440 | tf_op jit(solution)/shard_map/ppermute | solution.py:339
  10.1 0.5 %collective-permute-start.5 = (bf16[1,8,128,128]{3,2,1,0:T(8,128)(2,1)S(1)}, bf16[1,8,128,128]{3,2,1,0:T(8,128)(2,1)S(1)}, u32[]{:S(2)}, u32[]{:S(2)}) collective-permute-start(bf16[1,8,128,128]{3,2,1,0:T(8,128)(2,1)S(1)} %copy-done), channel_id=1, source_target_pairs={{0,4},{1,5},{2,6},{3,7},{4,0},{5,1},{6,2},{7,3},{8,12},{9,13},{10,... | collective-permute-start | bytes 786440 | tf_op jit(solution)/shard_map/ppermute | solution.py:339
  10.6 0.0 collective-permute-done.3.refs_3_
  10.6 0.8 %collective-permute-start.4 = (bf16[1,8,128,128]{3,2,1,0:T(8,128)(2,1)S(1)}, bf16[1,8,128,128]{3,2,1,0:T(8,128)(2,1)S(1)}, u32[]{:S(2)}, u32[]{:S(2)}) collective-permute-start(bf16[1,8,128,128]{3,2,1,0:T(8,128)(2,1)S(1)} %copy-done), channel_id=1, source_target_pairs={{0,2},{1,3},{2,0},{3,1},{4,6},{5,7},{6,4},{7,5},{8,10},{9,11},{10,... | collective-permute-start | bytes 786440 | tf_op jit(solution)/shard_map/ppermute | solution.py:339
  11.3 1.4 %collective-permute-done.2.refs_2_ = bf16[272,128]{1,0:T(8,128)(2,1)S(1)} collective-permute-done((bf16[272,128]{1,0:T(8,128)(2,1)S(1)}, bf16[272,128]{1,0:T(8,128)(2,1)S(1)}, u32[]{:S(2)}, u32[]{:S(2)}) %collective-permute-start.2) | collective-permute-done | bytes 69664 | tf_op jit(solution)/shard_map/ppermute | solution.py:336
  12.7 0.0 collective-permute-start
  12.7 0.0 collective-permute-done.1.refs_1_
  12.8 3.6 %score_memory.1 = (f32[8,128]{1,0:T(8,128)S(1)}, f32[8,128]{1,0:T(8,128)S(1)}, f32[8,128]{1,0:T(8,128)S(1)}, f32[8,128]{1,0:T(8,128)S(1)}) custom-call(bf16[272,128]{1,0:T(8,128)(2,1)S(1)} %pack.1.refs_0_, bf16[272,128]{1,0:T(8,128)(2,1)S(1)} %collective-permute-done.1.refs_1_, bf16[272,128]{1,0:T(8,128)(2,1)S(1)} %collective-permute-done.2.refs_2_, ...), custom_call_target="tpu_custom_call" | custom-call | flops 4294967296 | bytes 4194304 | tf_op jit(solution)/shard_map/score_memory/pallas_call | solution.py:213
  16.4 0.0 collective-permute-done.query_ref
  16.4 2.8 %collective-permute-start.8 = (f32[8,128]{1,0:T(8,128)S(1)}, f32[8,128]{1,0:T(8,128)S(1)}, u32[]{:S(2)}, u32[]{:S(2)}) collective-permute-start(f32[8,128]{1,0:T(8,128)S(1)} %get-tuple-element.16), channel_id=1, source_target_pairs={{0,24},{8,16},{16,8},{24,0},{1,25},{9,17},{17,9},{25,1},{2,26},{10... | collective-permute-start | bytes 12296 | tf_op jit(solution)/shard_map/ppermute | solution.py:336
  19.2 0.0 collective-permute-start.9
  19.2 0.0 collective-permute-done.6.refs_3_
  19.2 1.7 %collective-permute-start.10 = (f32[8,128]{1,0:T(8,128)S(1)}, f32[8,128]{1,0:T(8,128)S(1)}, u32[]{:S(2)}, u32[]{:S(2)}) collective-permute-start(f32[8,128]{1,0:T(8,128)S(1)} %get-tuple-element.18), channel_id=1, source_target_pairs={{0,8},{8,0},{16,24},{24,16},{1,9},{9,1},{17,25},{25,17},{2,10},{10... | collective-permute-start | bytes 12296 | tf_op jit(solution)/shard_map/ppermute | solution.py:336
  20.8 0.6 %collective-permute-done.5.refs_2_ = bf16[1,8,128,128]{3,2,1,0:T(8,128)(2,1)S(1)} collective-permute-done((bf16[1,8,128,128]{3,2,1,0:T(8,128)(2,1)S(1)}, bf16[1,8,128,128]{3,2,1,0:T(8,128)(2,1)S(1)}, u32[]{:S(2)}, u32[]{:S(2)}) %collective-permute-start.5) | collective-permute-done | bytes 262176 | tf_op jit(solution)/shard_map/ppermute | solution.py:339
  21.5 0.1 collective-permute-done.4.refs_1_
  21.6 0.8 %score_batch.2 = f32[8,128]{1,0:T(8,128)S(1)} custom-call(bf16[1,8,32,128]{3,2,1,0:T(8,128)(2,1)S(1)} %collective-permute-done.query_ref, bf16[1,8,128,128]{3,2,1,0:T(8,128)(2,1)S(1)} %copy-done, bf16[1,8,128,128]{3,2,1,0:T(8,128)(2,1)S(1)} %collective-permute-done.4.refs_1_, bf16[1,8,128,128]{3,2,1,0:T(8,128)(2,1)S(1)} %collective-permute-done.5.refs_2_, ...), custom_call_target="tpu_custom_call" | custom-call | flops 268435456 | bytes 1048576 | tf_op jit(solution)/shard_map/score_batch/pallas_call | solution.py:256
  22.4 0.0 collective-permute-start.7
  22.4 0.9 %score_batch.3.own_batch = f32[8,128]{1,0:T(8,128)S(1)} custom-call(bf16[1,8,32,128]{3,2,1,0:T(8,128)(2,1)S(1)} %copy-done.1, bf16[1,8,128,128]{3,2,1,0:T(8,128)(2,1)S(1)} %copy-done, bf16[1,8,128,128]{3,2,1,0:T(8,128)(2,1)S(1)} %collective-permute-done.4.refs_1_, bf16[1,8,128,128]{3,2,1,0:T(8,128)(2,1)S(1)} %collective-permute-done.5.refs_2_, ...), custom_call_target="tpu_custom_call" | custom-call | flops 268435456 | bytes 1048576 | tf_op jit(solution)/shard_map/score_batch/pallas_call | solution.py:256
  23.3 0.0 collective-permute-done.8.refs_1_
  23.3 0.4 %collective-permute-done.9.refs_2_ = f32[8,128]{1,0:T(8,128)S(1)} collective-permute-done((f32[8,128]{1,0:T(8,128)S(1)}, f32[8,128]{1,0:T(8,128)S(1)}, u32[]{:S(2)}, u32[]{:S(2)}) %collective-permute-start.9) | collective-permute-done | bytes 4128 | tf_op jit(solution)/shard_map/ppermute | solution.py:336
  23.7 0.0 collective-permute-done.10.refs_3_
  23.7 0.0 collective-permute-done.7.mate_batch
  23.7 0.0 copy-done.2
  23.7 0.8 %finish.1 = (f32[1,8,64]{2,1,0:T(8,128)}, f32[1,8,64]{2,1,0:T(8,128)}, f32[1,8]{1,0:T(1,128)}) custom-call(f32[8,128]{1,0:T(8,128)S(1)} %score_batch.3.own_batch, f32[8,128]{1,0:T(8,128)S(1)} %collective-permute-done.7.mate_batch, f32[8,128]{1,0:T(8,128)S(1)} %get-tuple-element.12.refs_0_, f32[8,128]{1,0:T(8,128)S(1)} %collective-permute-done.8.refs_1_, ...), custom_call_target="tpu_custom_call" | custom-call | tf_op jit(solution)/shard_map/finish/pallas_call | solution.py:316
  (5 shorter events, 0.0 us)
Async XLA Ops:
  0.6 12.1 %copy-start.1 = (bf16[1,8,32,128]{3,2,1,0:T(8,128)(2,1)S(1)}, bf16[1,8,32,128]{3,2,1,0:T(8,128)(2,1)}, u32[]{:S(2)}) copy-start(bf16[1,8,32,128]{3,2,1,0:T(8,128)(2,1)} %query_ref.2) | copy-start | bytes 196612
  0.6 6.8 %copy-start = (bf16[1,8,128,128]{3,2,1,0:T(8,128)(2,1)S(1)}, bf16[1,8,128,128]{3,2,1,0:T(8,128)(2,1)}, u32[]{:S(2)}) copy-start(bf16[1,8,128,128]{3,2,1,0:T(8,128)(2,1)} %refs_0_.3) | copy-start | bytes 786436
  0.7 12.1 %copy-start.4 = (bf16[1,128,128,128]{3,2,1,0:T(8,128)(2,1)S(1)}, bf16[1,128,128,128]{3,2,1,0:T(8,128)(2,1)}, u32[]{:S(2)}) copy-start(bf16[1,128,128,128]{3,2,1,0:T(8,128)(2,1)} %refs_4_.2) | copy-start | bytes 12582916
  1.7 22.0 %copy-start.2 = (s32[1,8,64]{2,1,0:T(8,128)S(1)}, s32[1,8,64]{2,1,0:T(8,128)}, u32[]{:S(2)}) copy-start(s32[1,8,64]{2,1,0:T(8,128)} %refs_4_.3) | copy-start | bytes 6148
  1.7 22.0 %copy-start.3 = (s32[1,8]{1,0:T(1,128)S(1)}, s32[1,8]{1,0:T(1,128)}, u32[]{:S(2)}) copy-start(s32[1,8]{1,0:T(1,128)} %refs_5_.1) | copy-start | bytes 100
  1.7 8.9 %collective-permute-start.3 = (bf16[272,128]{1,0:T(8,128)(2,1)S(1)}, bf16[272,128]{1,0:T(8,128)(2,1)S(1)}, u32[]{:S(2)}, u32[]{:S(2)}) collective-permute-start(bf16[272,128]{1,0:T(8,128)(2,1)S(1)} %pack.1.refs_0_), channel_id=1, source_target_pairs={{0,24},{8,16},{16,8},{24,0},{1,25},{9,17},{17,9},{25,1},{2,26},{10... | collective-permute-start | bytes 208904 | tf_op jit(solution)/shard_map/ppermute | solution.py:336
  6.8 5.9 %collective-permute-start.2 = (bf16[272,128]{1,0:T(8,128)(2,1)S(1)}, bf16[272,128]{1,0:T(8,128)(2,1)S(1)}, u32[]{:S(2)}, u32[]{:S(2)}) collective-permute-start(bf16[272,128]{1,0:T(8,128)(2,1)S(1)} %pack.1.refs_0_), channel_id=1, source_target_pairs={{0,16},{8,24},{16,0},{24,8},{1,17},{9,25},{17,1},{25,9},{2,18},{10... | collective-permute-start | bytes 208904 | tf_op jit(solution)/shard_map/ppermute | solution.py:336
  6.8 5.9 %collective-permute-start.1 = (bf16[272,128]{1,0:T(8,128)(2,1)S(1)}, bf16[272,128]{1,0:T(8,128)(2,1)S(1)}, u32[]{:S(2)}, u32[]{:S(2)}) collective-permute-start(bf16[272,128]{1,0:T(8,128)(2,1)S(1)} %pack.1.refs_0_), channel_id=1, source_target_pairs={{0,8},{8,0},{16,24},{24,16},{1,9},{9,1},{17,25},{25,17},{2,10},{10... | collective-permute-start | bytes 208904 | tf_op jit(solution)/shard_map/ppermute | solution.py:336
  7.5 11.7 %collective-permute-start.6 = (bf16[1,8,128,128]{3,2,1,0:T(8,128)(2,1)S(1)}, bf16[1,8,128,128]{3,2,1,0:T(8,128)(2,1)S(1)}, u32[]{:S(2)}, u32[]{:S(2)}) collective-permute-start(bf16[1,8,128,128]{3,2,1,0:T(8,128)(2,1)S(1)} %copy-done), channel_id=1, source_target_pairs={{0,6},{1,7},{2,4},{3,5},{4,2},{5,3},{6,0},{7,1},{8,14},{9,15},{10,... | collective-permute-start | bytes 786440 | tf_op jit(solution)/shard_map/ppermute | solution.py:339
  10.1 11.4 %collective-permute-start.5 = (bf16[1,8,128,128]{3,2,1,0:T(8,128)(2,1)S(1)}, bf16[1,8,128,128]{3,2,1,0:T(8,128)(2,1)S(1)}, u32[]{:S(2)}, u32[]{:S(2)}) collective-permute-start(bf16[1,8,128,128]{3,2,1,0:T(8,128)(2,1)S(1)} %copy-done), channel_id=1, source_target_pairs={{0,4},{1,5},{2,6},{3,7},{4,0},{5,1},{6,2},{7,3},{8,12},{9,13},{10,... | collective-permute-start | bytes 786440 | tf_op jit(solution)/shard_map/ppermute | solution.py:339
  10.6 11.0 %collective-permute-start.4 = (bf16[1,8,128,128]{3,2,1,0:T(8,128)(2,1)S(1)}, bf16[1,8,128,128]{3,2,1,0:T(8,128)(2,1)S(1)}, u32[]{:S(2)}, u32[]{:S(2)}) collective-permute-start(bf16[1,8,128,128]{3,2,1,0:T(8,128)(2,1)S(1)} %copy-done), channel_id=1, source_target_pairs={{0,2},{1,3},{2,0},{3,1},{4,6},{5,7},{6,4},{7,5},{8,10},{9,11},{10,... | collective-permute-start | bytes 786440 | tf_op jit(solution)/shard_map/ppermute | solution.py:339
  12.7 3.6 %collective-permute-start = (bf16[1,8,32,128]{3,2,1,0:T(8,128)(2,1)S(1)}, bf16[1,8,32,128]{3,2,1,0:T(8,128)(2,1)S(1)}, u32[]{:S(2)}, u32[]{:S(2)}) collective-permute-start(bf16[1,8,32,128]{3,2,1,0:T(8,128)(2,1)S(1)} %copy-done.1), channel_id=1, source_target_pairs={{0,1},{1,0},{2,3},{3,2},{4,5},{5,4},{6,7},{7,6},{8,9},{9,8},{10,11... | collective-permute-start | bytes 196616 | tf_op jit(solution)/shard_map/ppermute | solution.py:339
  16.4 6.9 %collective-permute-start.8 = (f32[8,128]{1,0:T(8,128)S(1)}, f32[8,128]{1,0:T(8,128)S(1)}, u32[]{:S(2)}, u32[]{:S(2)}) collective-permute-start(f32[8,128]{1,0:T(8,128)S(1)} %get-tuple-element.16), channel_id=1, source_target_pairs={{0,24},{8,16},{16,8},{24,0},{1,25},{9,17},{17,9},{25,1},{2,26},{10... | collective-permute-start | bytes 12296 | tf_op jit(solution)/shard_map/ppermute | solution.py:336
  19.2 4.5 %collective-permute-start.9 = (f32[8,128]{1,0:T(8,128)S(1)}, f32[8,128]{1,0:T(8,128)S(1)}, u32[]{:S(2)}, u32[]{:S(2)}) collective-permute-start(f32[8,128]{1,0:T(8,128)S(1)} %get-tuple-element.17), channel_id=1, source_target_pairs={{0,16},{8,24},{16,0},{24,8},{1,17},{9,25},{17,1},{25,9},{2,18},{10... | collective-permute-start | bytes 12296 | tf_op jit(solution)/shard_map/ppermute | solution.py:336
  19.2 4.5 %collective-permute-start.10 = (f32[8,128]{1,0:T(8,128)S(1)}, f32[8,128]{1,0:T(8,128)S(1)}, u32[]{:S(2)}, u32[]{:S(2)}) collective-permute-start(f32[8,128]{1,0:T(8,128)S(1)} %get-tuple-element.18), channel_id=1, source_target_pairs={{0,8},{8,0},{16,24},{24,16},{1,9},{9,1},{17,25},{25,17},{2,10},{10... | collective-permute-start | bytes 12296 | tf_op jit(solution)/shard_map/ppermute | solution.py:336
  22.4 1.3 %collective-permute-start.7 = (f32[8,128]{1,0:T(8,128)S(1)}, f32[8,128]{1,0:T(8,128)S(1)}, u32[]{:S(2)}, u32[]{:S(2)}) collective-permute-start(f32[8,128]{1,0:T(8,128)S(1)} %score_batch.2), channel_id=1, source_target_pairs={{0,1},{1,0},{2,3},{3,2},{4,5},{5,4},{6,7},{7,6},{8,9},{9,8},{10,11... | collective-permute-start | bytes 12296 | tf_op jit(solution)/shard_map/ppermute | solution.py:339

commit v13 on v12

--- a/solution.py
+++ b/solution.py
@@ -159,8 +159,11 @@
         copy.start()
         return copy
 
-    def unit(index):
-        tokens = [query_ref[scalar_ref[slot, index] & (LOW - 1)] for slot in range(SLOTS)]
+    def unit(index, mask):
+        numbers = [scalar_ref[slot, index] for slot in range(SLOTS)]
+        if mask:
+            numbers = [number & (LOW - 1) for number in numbers]
+        tokens = [query_ref[number] for number in numbers]
         return token_max(passage_ref[pl.ds(index, 1)], jnp.concatenate(tokens, axis=0))
 
     def add_scores(first, scores):
@@ -184,7 +187,7 @@
     list_copy.wait()
 
     for first in range(0, p_count, 8):
-        rows = [unit(first + offset) for offset in range(8)]
+        rows = [unit(first + offset, False) for offset in range(8)]
         best_ref[first : first + 8, :] = jnp.concatenate(rows, axis=0)
 
     most_copy.wait()
@@ -199,7 +202,7 @@
         @pl.loop(0, scalar_ref[1, 0] // LOW)
         def _(place):
             index = scalar_ref[0, place] // LOW
-            best_ref[pl.ds(index, 1), :] = unit(index)
+            best_ref[pl.ds(index, 1), :] = unit(index, True)
 
         add_scores(done, [out_ref[...] for out_ref in out_refs])
 

time: 24.6 us -> 24.6 us (level)
  no operation moved by 1% of the time
where the time goes in v13:
time: 24.6 us; the launch traced here: 24.5 us
  starting transfers between devices  14.1 us (57%)
  Pallas kernels  7.09 us (29%)
  waiting for transfers between devices  2.54 us (10%)
  between operations  0.73 us (3%)
    ppermute x6, starting transfers between devices, to_shard(): return lax.ppermute(array, 'memory', [(i, i ^ step) for i in range(shards)])  10.2 us
    ppermute x5, starting transfers between devices, to_group(): return lax.ppermute(array, 'group', [(i, i ^ step) for i in range(groups)])  3.88 us
    pallas_call x1, Pallas kernels, score_memory(): pl.pallas_call(functools.partial(memory_kernel, shards, slots), in_specs=...  3.59 us
    ppermute x6, waiting for transfers between devices, to_shard(): return lax.ppermute(array, 'memory', [(i, i ^ step) for i in range(shards)])  1.78 us
    pallas_call x2, Pallas kernels, score_batch(): pl.pallas_call(batch_kernel, out_shape=jax.ShapeDtypeStruct((q_count, lan...  1.68 us
    pallas_call x1, Pallas kernels, pack(): pl.pallas_call(functools.partial(pack_kernel, p_count), in_specs=[vmem, v...  1.02 us
    pallas_call x1, Pallas kernels, finish(): pl.pallas_call(functools.partial(loss_kernel, len(memory_parts)), out_sha...  0.8 us
    ppermute x5, waiting for transfers between devices, to_group(): return lax.ppermute(array, 'group', [(i, i ^ step) for i in range(groups)])  0.76 us
  transfers between devices with their start and end apart: 11, of which 4 were waited for; matrix products, arithmetic and copies ran while one was open for 0% of the time, Pallas kernels for 22%

profile of v13, /device:TPU:0, one launch (start us, length us, event | category | flops | bytes accessed | tf_op | source)
XLA Modules:
  0.0 24.5 jit_solution(17438042489796028209)
XLA Ops:
  0.6 0.0 copy-start.1
  0.7 1.0 %pack.1.refs_0_ = bf16[272,128]{1,0:T(8,128)(2,1)S(1)} custom-call(bf16[1,8,32,128]{3,2,1,0:T(8,128)(2,1)} %query_ref.2, s32[1,8,64]{2,1,0:T(8,128)} %refs_4_.3, s32[1,8]{1,0:T(1,128)} %refs_5_.1), custom_call_target="tpu_custom_call" | custom-call | flops 10000000000 | bytes 16777216 | tf_op jit(solution)/shard_map/pack/pallas_call | solution.py:93
  1.7 0.0 copy-start.2
  1.7 0.0 copy-start.3
  1.7 5.1 %collective-permute-start.3 = (bf16[272,128]{1,0:T(8,128)(2,1)S(1)}, bf16[272,128]{1,0:T(8,128)(2,1)S(1)}, u32[]{:S(2)}, u32[]{:S(2)}) collective-permute-start(bf16[272,128]{1,0:T(8,128)(2,1)S(1)} %pack.1.refs_0_), channel_id=1, source_target_pairs={{0,24},{8,16},{16,8},{24,0},{1,25},{9,17},{17,9},{25,1},{2,26},{10... | collective-permute-start | bytes 208904 | tf_op jit(solution)/shard_map/ppermute | solution.py:339
  6.8 0.0 collective-permute-start.2
  6.8 0.6 %collective-permute-start.1 = (bf16[272,128]{1,0:T(8,128)(2,1)S(1)}, bf16[272,128]{1,0:T(8,128)(2,1)S(1)}, u32[]{:S(2)}, u32[]{:S(2)}) collective-permute-start(bf16[272,128]{1,0:T(8,128)(2,1)S(1)} %pack.1.refs_0_), channel_id=1, source_target_pairs={{0,8},{8,0},{16,24},{24,16},{1,9},{9,1},{17,25},{25,17},{2,10},{10... | collective-permute-start | bytes 208904 | tf_op jit(solution)/shard_map/ppermute | solution.py:339
  7.5 2.6 %collective-permute-start.6 = (bf16[1,8,128,128]{3,2,1,0:T(8,128)(2,1)S(1)}, bf16[1,8,128,128]{3,2,1,0:T(8,128)(2,1)S(1)}, u32[]{:S(2)}, u32[]{:S(2)}) collective-permute-start(bf16[1,8,128,128]{3,2,1,0:T(8,128)(2,1)S(1)} %copy-done), channel_id=1, source_target_pairs={{0,6},{1,7},{2,4},{3,5},{4,2},{5,3},{6,0},{7,1},{8,14},{9,15},{10,... | collective-permute-start | bytes 786440 | tf_op jit(solution)/shard_map/ppermute | solution.py:342
  10.1 0.5 %collective-permute-start.5 = (bf16[1,8,128,128]{3,2,1,0:T(8,128)(2,1)S(1)}, bf16[1,8,128,128]{3,2,1,0:T(8,128)(2,1)S(1)}, u32[]{:S(2)}, u32[]{:S(2)}) collective-permute-start(bf16[1,8,128,128]{3,2,1,0:T(8,128)(2,1)S(1)} %copy-done), channel_id=1, source_target_pairs={{0,4},{1,5},{2,6},{3,7},{4,0},{5,1},{6,2},{7,3},{8,12},{9,13},{10,... | collective-permute-start | bytes 786440 | tf_op jit(solution)/shard_map/ppermute | solution.py:342
  10.6 0.0 collective-permute-done.3.refs_3_
  10.6 0.8 %collective-permute-start.4 = (bf16[1,8,128,128]{3,2,1,0:T(8,128)(2,1)S(1)}, bf16[1,8,128,128]{3,2,1,0:T(8,128)(2,1)S(1)}, u32[]{:S(2)}, u32[]{:S(2)}) collective-permute-start(bf16[1,8,128,128]{3,2,1,0:T(8,128)(2,1)S(1)} %copy-done), channel_id=1, source_target_pairs={{0,2},{1,3},{2,0},{3,1},{4,6},{5,7},{6,4},{7,5},{8,10},{9,11},{10,... | collective-permute-start | bytes 786440 | tf_op jit(solution)/shard_map/ppermute | solution.py:342
  11.3 1.4 %collective-permute-done.2.refs_2_ = bf16[272,128]{1,0:T(8,128)(2,1)S(1)} collective-permute-done((bf16[272,128]{1,0:T(8,128)(2,1)S(1)}, bf16[272,128]{1,0:T(8,128)(2,1)S(1)}, u32[]{:S(2)}, u32[]{:S(2)}) %collective-permute-start.2) | collective-permute-done | bytes 69664 | tf_op jit(solution)/shard_map/ppermute | solution.py:339
  12.7 0.0 copy-done.1
  12.7 0.0 collective-permute-start
  12.7 0.0 collective-permute-done.1.refs_1_
  12.8 3.6 %score_memory.1 = (f32[8,128]{1,0:T(8,128)S(1)}, f32[8,128]{1,0:T(8,128)S(1)}, f32[8,128]{1,0:T(8,128)S(1)}, f32[8,128]{1,0:T(8,128)S(1)}) custom-call(bf16[272,128]{1,0:T(8,128)(2,1)S(1)} %pack.1.refs_0_, bf16[272,128]{1,0:T(8,128)(2,1)S(1)} %collective-permute-done.1.refs_1_, bf16[272,128]{1,0:T(8,128)(2,1)S(1)} %collective-permute-done.2.refs_2_, ...), custom_call_target="tpu_custom_call" | custom-call | flops 4294967296 | bytes 4194304 | tf_op jit(solution)/shard_map/score_memory/pallas_call | solution.py:216
  16.4 0.0 collective-permute-done.query_ref
  16.4 2.8 %collective-permute-start.8 = (f32[8,128]{1,0:T(8,128)S(1)}, f32[8,128]{1,0:T(8,128)S(1)}, u32[]{:S(2)}, u32[]{:S(2)}) collective-permute-start(f32[8,128]{1,0:T(8,128)S(1)} %get-tuple-element.16), channel_id=1, source_target_pairs={{0,24},{8,16},{16,8},{24,0},{1,25},{9,17},{17,9},{25,1},{2,26},{10... | collective-permute-start | bytes 12296 | tf_op jit(solution)/shard_map/ppermute | solution.py:339
  19.1 0.0 collective-permute-start.9
  19.1 0.0 collective-permute-done.6.refs_3_
  19.1 1.7 %collective-permute-start.10 = (f32[8,128]{1,0:T(8,128)S(1)}, f32[8,128]{1,0:T(8,128)S(1)}, u32[]{:S(2)}, u32[]{:S(2)}) collective-permute-start(f32[8,128]{1,0:T(8,128)S(1)} %get-tuple-element.18), channel_id=1, source_target_pairs={{0,8},{8,0},{16,24},{24,16},{1,9},{9,1},{17,25},{25,17},{2,10},{10... | collective-permute-start | bytes 12296 | tf_op jit(solution)/shard_map/ppermute | solution.py:339
  20.8 0.7 %collective-permute-done.5.refs_2_ = bf16[1,8,128,128]{3,2,1,0:T(8,128)(2,1)S(1)} collective-permute-done((bf16[1,8,128,128]{3,2,1,0:T(8,128)(2,1)S(1)}, bf16[1,8,128,128]{3,2,1,0:T(8,128)(2,1)S(1)}, u32[]{:S(2)}, u32[]{:S(2)}) %collective-permute-start.5) | collective-permute-done | bytes 262176 | tf_op jit(solution)/shard_map/ppermute | solution.py:342
  21.5 0.1 collective-permute-done.4.refs_1_
  21.6 0.8 %score_batch.2 = f32[8,128]{1,0:T(8,128)S(1)} custom-call(bf16[1,8,32,128]{3,2,1,0:T(8,128)(2,1)S(1)} %collective-permute-done.query_ref, bf16[1,8,128,128]{3,2,1,0:T(8,128)(2,1)S(1)} %copy-done, bf16[1,8,128,128]{3,2,1,0:T(8,128)(2,1)S(1)} %collective-permute-done.4.refs_1_, bf16[1,8,128,128]{3,2,1,0:T(8,128)(2,1)S(1)} %collective-permute-done.5.refs_2_, ...), custom_call_target="tpu_custom_call" | custom-call | flops 268435456 | bytes 1048576 | tf_op jit(solution)/shard_map/score_batch/pallas_call | solution.py:259
  22.4 0.0 collective-permute-start.7
  22.4 0.9 %score_batch.3.own_batch = f32[8,128]{1,0:T(8,128)S(1)} custom-call(bf16[1,8,32,128]{3,2,1,0:T(8,128)(2,1)S(1)} %copy-done.1, bf16[1,8,128,128]{3,2,1,0:T(8,128)(2,1)S(1)} %copy-done, bf16[1,8,128,128]{3,2,1,0:T(8,128)(2,1)S(1)} %collective-permute-done.4.refs_1_, bf16[1,8,128,128]{3,2,1,0:T(8,128)(2,1)S(1)} %collective-permute-done.5.refs_2_, ...), custom_call_target="tpu_custom_call" | custom-call | flops 268435456 | bytes 1048576 | tf_op jit(solution)/shard_map/score_batch/pallas_call | solution.py:259
  23.3 0.0 collective-permute-done.8.refs_1_
  23.3 0.4 %collective-permute-done.9.refs_2_ = f32[8,128]{1,0:T(8,128)S(1)} collective-permute-done((f32[8,128]{1,0:T(8,128)S(1)}, f32[8,128]{1,0:T(8,128)S(1)}, u32[]{:S(2)}, u32[]{:S(2)}) %collective-permute-start.9) | collective-permute-done | bytes 4128 | tf_op jit(solution)/shard_map/ppermute | solution.py:339
  23.6 0.0 collective-permute-done.10.refs_3_
  23.6 0.0 collective-permute-done.7.mate_batch
  23.7 0.0 copy-done.3
  23.7 0.8 %finish.1 = (f32[1,8,64]{2,1,0:T(8,128)}, f32[1,8,64]{2,1,0:T(8,128)}, f32[1,8]{1,0:T(1,128)}) custom-call(f32[8,128]{1,0:T(8,128)S(1)} %score_batch.3.own_batch, f32[8,128]{1,0:T(8,128)S(1)} %collective-permute-done.7.mate_batch, f32[8,128]{1,0:T(8,128)S(1)} %get-tuple-element.12.refs_0_, f32[8,128]{1,0:T(8,128)S(1)} %collective-permute-done.8.refs_1_, ...), custom_call_target="tpu_custom_call" | custom-call | tf_op jit(solution)/shard_map/finish/pallas_call | solution.py:319
  (5 shorter events, 0.0 us)
Async XLA Ops:
  0.6 12.1 %copy-start.1 = (bf16[1,8,32,128]{3,2,1,0:T(8,128)(2,1)S(1)}, bf16[1,8,32,128]{3,2,1,0:T(8,128)(2,1)}, u32[]{:S(2)}) copy-start(bf16[1,8,32,128]{3,2,1,0:T(8,128)(2,1)} %query_ref.2) | copy-start | bytes 196612
  0.6 6.8 %copy-start = (bf16[1,8,128,128]{3,2,1,0:T(8,128)(2,1)S(1)}, bf16[1,8,128,128]{3,2,1,0:T(8,128)(2,1)}, u32[]{:S(2)}) copy-start(bf16[1,8,128,128]{3,2,1,0:T(8,128)(2,1)} %refs_0_.3) | copy-start | bytes 786436
  0.7 12.1 %copy-start.4 = (bf16[1,128,128,128]{3,2,1,0:T(8,128)(2,1)S(1)}, bf16[1,128,128,128]{3,2,1,0:T(8,128)(2,1)}, u32[]{:S(2)}) copy-start(bf16[1,128,128,128]{3,2,1,0:T(8,128)(2,1)} %refs_4_.2) | copy-start | bytes 12582916
  1.7 22.0 %copy-start.2 = (s32[1,8,64]{2,1,0:T(8,128)S(1)}, s32[1,8,64]{2,1,0:T(8,128)}, u32[]{:S(2)}) copy-start(s32[1,8,64]{2,1,0:T(8,128)} %refs_4_.3) | copy-start | bytes 6148
  1.7 22.0 %copy-start.3 = (s32[1,8]{1,0:T(1,128)S(1)}, s32[1,8]{1,0:T(1,128)}, u32[]{:S(2)}) copy-start(s32[1,8]{1,0:T(1,128)} %refs_5_.1) | copy-start | bytes 100
  1.7 8.9 %collective-permute-start.3 = (bf16[272,128]{1,0:T(8,128)(2,1)S(1)}, bf16[272,128]{1,0:T(8,128)(2,1)S(1)}, u32[]{:S(2)}, u32[]{:S(2)}) collective-permute-start(bf16[272,128]{1,0:T(8,128)(2,1)S(1)} %pack.1.refs_0_), channel_id=1, source_target_pairs={{0,24},{8,16},{16,8},{24,0},{1,25},{9,17},{17,9},{25,1},{2,26},{10... | collective-permute-start | bytes 208904 | tf_op jit(solution)/shard_map/ppermute | solution.py:339
  6.8 5.9 %collective-permute-start.2 = (bf16[272,128]{1,0:T(8,128)(2,1)S(1)}, bf16[272,128]{1,0:T(8,128)(2,1)S(1)}, u32[]{:S(2)}, u32[]{:S(2)}) collective-permute-start(bf16[272,128]{1,0:T(8,128)(2,1)S(1)} %pack.1.refs_0_), channel_id=1, source_target_pairs={{0,16},{8,24},{16,0},{24,8},{1,17},{9,25},{17,1},{25,9},{2,18},{10... | collective-permute-start | bytes 208904 | tf_op jit(solution)/shard_map/ppermute | solution.py:339
  6.8 5.9 %collective-permute-start.1 = (bf16[272,128]{1,0:T(8,128)(2,1)S(1)}, bf16[272,128]{1,0:T(8,128)(2,1)S(1)}, u32[]{:S(2)}, u32[]{:S(2)}) collective-permute-start(bf16[272,128]{1,0:T(8,128)(2,1)S(1)} %pack.1.refs_0_), channel_id=1, source_target_pairs={{0,8},{8,0},{16,24},{24,16},{1,9},{9,1},{17,25},{25,17},{2,10},{10... | collective-permute-start | bytes 208904 | tf_op jit(solution)/shard_map/ppermute | solution.py:339
  7.5 11.7 %collective-permute-start.6 = (bf16[1,8,128,128]{3,2,1,0:T(8,128)(2,1)S(1)}, bf16[1,8,128,128]{3,2,1,0:T(8,128)(2,1)S(1)}, u32[]{:S(2)}, u32[]{:S(2)}) collective-permute-start(bf16[1,8,128,128]{3,2,1,0:T(8,128)(2,1)S(1)} %copy-done), channel_id=1, source_target_pairs={{0,6},{1,7},{2,4},{3,5},{4,2},{5,3},{6,0},{7,1},{8,14},{9,15},{10,... | collective-permute-start | bytes 786440 | tf_op jit(solution)/shard_map/ppermute | solution.py:342
  10.1 11.4 %collective-permute-start.5 = (bf16[1,8,128,128]{3,2,1,0:T(8,128)(2,1)S(1)}, bf16[1,8,128,128]{3,2,1,0:T(8,128)(2,1)S(1)}, u32[]{:S(2)}, u32[]{:S(2)}) collective-permute-start(bf16[1,8,128,128]{3,2,1,0:T(8,128)(2,1)S(1)} %copy-done), channel_id=1, source_target_pairs={{0,4},{1,5},{2,6},{3,7},{4,0},{5,1},{6,2},{7,3},{8,12},{9,13},{10,... | collective-permute-start | bytes 786440 | tf_op jit(solution)/shard_map/ppermute | solution.py:342
  10.6 11.0 %collective-permute-start.4 = (bf16[1,8,128,128]{3,2,1,0:T(8,128)(2,1)S(1)}, bf16[1,8,128,128]{3,2,1,0:T(8,128)(2,1)S(1)}, u32[]{:S(2)}, u32[]{:S(2)}) collective-permute-start(bf16[1,8,128,128]{3,2,1,0:T(8,128)(2,1)S(1)} %copy-done), channel_id=1, source_target_pairs={{0,2},{1,3},{2,0},{3,1},{4,6},{5,7},{6,4},{7,5},{8,10},{9,11},{10,... | collective-permute-start | bytes 786440 | tf_op jit(solution)/shard_map/ppermute | solution.py:342
  12.7 3.6 %collective-permute-start = (bf16[1,8,32,128]{3,2,1,0:T(8,128)(2,1)S(1)}, bf16[1,8,32,128]{3,2,1,0:T(8,128)(2,1)S(1)}, u32[]{:S(2)}, u32[]{:S(2)}) collective-permute-start(bf16[1,8,32,128]{3,2,1,0:T(8,128)(2,1)S(1)} %copy-done.1), channel_id=1, source_target_pairs={{0,1},{1,0},{2,3},{3,2},{4,5},{5,4},{6,7},{7,6},{8,9},{9,8},{10,11... | collective-permute-start | bytes 196616 | tf_op jit(solution)/shard_map/ppermute | solution.py:342
  16.4 6.9 %collective-permute-start.8 = (f32[8,128]{1,0:T(8,128)S(1)}, f32[8,128]{1,0:T(8,128)S(1)}, u32[]{:S(2)}, u32[]{:S(2)}) collective-permute-start(f32[8,128]{1,0:T(8,128)S(1)} %get-tuple-element.16), channel_id=1, source_target_pairs={{0,24},{8,16},{16,8},{24,0},{1,25},{9,17},{17,9},{25,1},{2,26},{10... | collective-permute-start | bytes 12296 | tf_op jit(solution)/shard_map/ppermute | solution.py:339
  19.1 4.5 %collective-permute-start.9 = (f32[8,128]{1,0:T(8,128)S(1)}, f32[8,128]{1,0:T(8,128)S(1)}, u32[]{:S(2)}, u32[]{:S(2)}) collective-permute-start(f32[8,128]{1,0:T(8,128)S(1)} %get-tuple-element.17), channel_id=1, source_target_pairs={{0,16},{8,24},{16,0},{24,8},{1,17},{9,25},{17,1},{25,9},{2,18},{10... | collective-permute-start | bytes 12296 | tf_op jit(solution)/shard_map/ppermute | solution.py:339
  19.1 4.5 %collective-permute-start.10 = (f32[8,128]{1,0:T(8,128)S(1)}, f32[8,128]{1,0:T(8,128)S(1)}, u32[]{:S(2)}, u32[]{:S(2)}) collective-permute-start(f32[8,128]{1,0:T(8,128)S(1)} %get-tuple-element.18), channel_id=1, source_target_pairs={{0,8},{8,0},{16,24},{24,16},{1,9},{9,1},{17,25},{25,17},{2,10},{10... | collective-permute-start | bytes 12296 | tf_op jit(solution)/shard_map/ppermute | solution.py:339
  22.4 1.2 %collective-permute-start.7 = (f32[8,128]{1,0:T(8,128)S(1)}, f32[8,128]{1,0:T(8,128)S(1)}, u32[]{:S(2)}, u32[]{:S(2)}) collective-permute-start(f32[8,128]{1,0:T(8,128)S(1)} %score_batch.2), channel_id=1, source_target_pairs={{0,1},{1,0},{2,3},{3,2},{4,5},{5,4},{6,7},{7,6},{8,9},{9,8},{10,11... | collective-permute-start | bytes 12296 | tf_op jit(solution)/shard_map/ppermute | solution.py:342

commit v14 on v12

--- a/solution.py
+++ b/solution.py
@@ -77,14 +77,25 @@
     return (ids % p_count).astype(jnp.float32), holder.astype(jnp.float32)
 
 
-def pack_kernel(p_count, query_ref, candidate_ref, count_ref, out_ref):
+def pack_kernel(p_count, query_ref, candidate_ref, count_ref, out_ref, sems):
     _, q_count, slots = candidate_ref.shape
     _, _, q_tokens, depth = query_ref.shape
     tokens = q_count * q_tokens
-    out_ref[:tokens] = query_ref[0].reshape(tokens, depth)
+    copies = [
+        pltpu.make_async_copy(
+            query_ref.at[0, index],
+            out_ref.at[pl.ds(index * q_tokens, q_tokens)],
+            sems.at[index],
+        )
+        for index in range(q_count)
+    ]
+    for copy in copies:
+        copy.start()
     planes = jnp.concatenate(split_ids(p_count, candidate_ref, count_ref), axis=0)
     empty = jnp.zeros((2 * q_count, depth - slots), jnp.float32)
     out_ref[tokens:] = jnp.concatenate([planes, empty], axis=1).astype(out_ref.dtype)
+    for copy in copies:
+        copy.wait()
 
 
 def pack(queries, candidates, counts, p_count):
@@ -92,7 +103,12 @@
     vmem = pl.BlockSpec(memory_space=pltpu.VMEM)
     return pl.pallas_call(
         functools.partial(pack_kernel, p_count),
-        in_specs=[vmem, vmem, pl.BlockSpec(memory_space=pltpu.SMEM)],
+        in_specs=[
+            pl.BlockSpec(memory_space=pltpu.HBM),
+            vmem,
+            pl.BlockSpec(memory_space=pltpu.SMEM),
+        ],
+        scratch_shapes=[pltpu.SemaphoreType.DMA((q_count,))],
         out_shape=jax.ShapeDtypeStruct((q_count * (q_tokens + 2), depth), queries.dtype),
         compiler_params=pltpu.CompilerParams(vmem_limit_bytes=4 * MIB),
         cost_estimate=pl.CostEstimate(

time: 24.6 us -> 25.8 us (1.049)
  Pallas kernels: 7.1 us -> 8.08 us
    pallas_call x1, Pallas kernels: 1.02 us -> 2 us  [pack(): pl.pallas_call(functools.partial(pack_kernel, p_count), in_specs=[pl.Bloc...]
  transfers between devices with their start and end apart: 11 -> 11, of which waited for: 4 -> 4; matrix products, arithmetic and copies ran while one was open for 0% -> 0% of each run, Pallas kernels for 22% -> 21%
where the time goes in v14:
time: 25.8 us; the launch traced here: 25.5 us
  starting transfers between devices  14.1 us (55%)
  Pallas kernels  8.08 us (31%)
  waiting for transfers between devices  2.55 us (10%)
  between operations  0.73 us (3%)
    ppermute x6, starting transfers between devices, to_shard(): return lax.ppermute(array, 'memory', [(i, i ^ step) for i in range(shards)])  10.2 us
    ppermute x5, starting transfers between devices, to_group(): return lax.ppermute(array, 'group', [(i, i ^ step) for i in range(groups)])  3.88 us
    pallas_call x1, Pallas kernels, score_memory(): pl.pallas_call(functools.partial(memory_kernel, shards, slots), in_specs=...  3.59 us
    pallas_call x1, Pallas kernels, pack(): pl.pallas_call(functools.partial(pack_kernel, p_count), in_specs=[pl.Bloc...  2 us
    ppermute x6, waiting for transfers between devices, to_shard(): return lax.ppermute(array, 'memory', [(i, i ^ step) for i in range(shards)])  1.79 us
    pallas_call x2, Pallas kernels, score_batch(): pl.pallas_call(batch_kernel, out_shape=jax.ShapeDtypeStruct((q_count, lan...  1.68 us
    pallas_call x1, Pallas kernels, finish(): pl.pallas_call(functools.partial(loss_kernel, len(memory_parts)), out_sha...  0.8 us
    ppermute x5, waiting for transfers between devices, to_group(): return lax.ppermute(array, 'group', [(i, i ^ step) for i in range(groups)])  0.76 us
  transfers between devices with their start and end apart: 11, of which 4 were waited for; matrix products, arithmetic and copies ran while one was open for 0% of the time, Pallas kernels for 21%

profile of v14, /device:TPU:0, one launch (start us, length us, event | category | flops | bytes accessed | tf_op | source)
XLA Modules:
  0.0 25.5 jit_solution(9558935972133667371)
XLA Ops:
  0.7 2.0 %pack.1.refs_0_ = bf16[272,128]{1,0:T(8,128)(2,1)S(1)} custom-call(bf16[1,8,32,128]{3,2,1,0:T(8,128)(2,1)} %query_ref.2, s32[1,8,64]{2,1,0:T(8,128)} %refs_4_.3, s32[1,8]{1,0:T(1,128)} %refs_5_.1), custom_call_target="tpu_custom_call" | custom-call | flops 10000000000 | bytes 16777216 | tf_op jit(solution)/shard_map/pack/pallas_call | solution.py:104
  2.7 0.0 copy-start.2
  2.7 0.0 copy-start.3
  2.7 5.1 %collective-permute-start.3 = (bf16[272,128]{1,0:T(8,128)(2,1)S(1)}, bf16[272,128]{1,0:T(8,128)(2,1)S(1)}, u32[]{:S(2)}, u32[]{:S(2)}) collective-permute-start(bf16[272,128]{1,0:T(8,128)(2,1)S(1)} %pack.1.refs_0_), channel_id=1, source_target_pairs={{0,24},{8,16},{16,8},{24,0},{1,25},{9,17},{17,9},{25,1},{2,26},{10... | collective-permute-start | bytes 208904 | tf_op jit(solution)/shard_map/ppermute | solution.py:352
  7.8 0.0 collective-permute-start.2
  7.8 0.6 %collective-permute-start.1 = (bf16[272,128]{1,0:T(8,128)(2,1)S(1)}, bf16[272,128]{1,0:T(8,128)(2,1)S(1)}, u32[]{:S(2)}, u32[]{:S(2)}) collective-permute-start(bf16[272,128]{1,0:T(8,128)(2,1)S(1)} %pack.1.refs_0_), channel_id=1, source_target_pairs={{0,8},{8,0},{16,24},{24,16},{1,9},{9,1},{17,25},{25,17},{2,10},{10... | collective-permute-start | bytes 208904 | tf_op jit(solution)/shard_map/ppermute | solution.py:352
  8.4 0.0 copy-done
  8.5 2.6 %collective-permute-start.6 = (bf16[1,8,128,128]{3,2,1,0:T(8,128)(2,1)S(1)}, bf16[1,8,128,128]{3,2,1,0:T(8,128)(2,1)S(1)}, u32[]{:S(2)}, u32[]{:S(2)}) collective-permute-start(bf16[1,8,128,128]{3,2,1,0:T(8,128)(2,1)S(1)} %copy-done), channel_id=1, source_target_pairs={{0,6},{1,7},{2,4},{3,5},{4,2},{5,3},{6,0},{7,1},{8,14},{9,15},{10,... | collective-permute-start | bytes 786440 | tf_op jit(solution)/shard_map/ppermute | solution.py:355
  11.0 0.5 %collective-permute-start.5 = (bf16[1,8,128,128]{3,2,1,0:T(8,128)(2,1)S(1)}, bf16[1,8,128,128]{3,2,1,0:T(8,128)(2,1)S(1)}, u32[]{:S(2)}, u32[]{:S(2)}) collective-permute-start(bf16[1,8,128,128]{3,2,1,0:T(8,128)(2,1)S(1)} %copy-done), channel_id=1, source_target_pairs={{0,4},{1,5},{2,6},{3,7},{4,0},{5,1},{6,2},{7,3},{8,12},{9,13},{10,... | collective-permute-start | bytes 786440 | tf_op jit(solution)/shard_map/ppermute | solution.py:355
  11.6 0.0 collective-permute-done.3.refs_3_
  11.6 0.8 %collective-permute-start.4 = (bf16[1,8,128,128]{3,2,1,0:T(8,128)(2,1)S(1)}, bf16[1,8,128,128]{3,2,1,0:T(8,128)(2,1)S(1)}, u32[]{:S(2)}, u32[]{:S(2)}) collective-permute-start(bf16[1,8,128,128]{3,2,1,0:T(8,128)(2,1)S(1)} %copy-done), channel_id=1, source_target_pairs={{0,2},{1,3},{2,0},{3,1},{4,6},{5,7},{6,4},{7,5},{8,10},{9,11},{10,... | collective-permute-start | bytes 786440 | tf_op jit(solution)/shard_map/ppermute | solution.py:355
  12.3 1.4 %collective-permute-done.2.refs_2_ = bf16[272,128]{1,0:T(8,128)(2,1)S(1)} collective-permute-done((bf16[272,128]{1,0:T(8,128)(2,1)S(1)}, bf16[272,128]{1,0:T(8,128)(2,1)S(1)}, u32[]{:S(2)}, u32[]{:S(2)}) %collective-permute-start.2) | collective-permute-done | bytes 69664 | tf_op jit(solution)/shard_map/ppermute | solution.py:352
  13.7 0.0 collective-permute-start
  13.7 0.0 collective-permute-done.1.refs_1_
  13.7 0.0 copy-done.4
  13.7 3.6 %score_memory.1 = (f32[8,128]{1,0:T(8,128)S(1)}, f32[8,128]{1,0:T(8,128)S(1)}, f32[8,128]{1,0:T(8,128)S(1)}, f32[8,128]{1,0:T(8,128)S(1)}) custom-call(bf16[272,128]{1,0:T(8,128)(2,1)S(1)} %pack.1.refs_0_, bf16[272,128]{1,0:T(8,128)(2,1)S(1)} %collective-permute-done.1.refs_1_, bf16[272,128]{1,0:T(8,128)(2,1)S(1)} %collective-permute-done.2.refs_2_, ...), custom_call_target="tpu_custom_call" | custom-call | flops 4294967296 | bytes 4194304 | tf_op jit(solution)/shard_map/score_memory/pallas_call | solution.py:229
  17.3 0.0 collective-permute-done.query_ref
  17.3 2.8 %collective-permute-start.8 = (f32[8,128]{1,0:T(8,128)S(1)}, f32[8,128]{1,0:T(8,128)S(1)}, u32[]{:S(2)}, u32[]{:S(2)}) collective-permute-start(f32[8,128]{1,0:T(8,128)S(1)} %get-tuple-element.16), channel_id=1, source_target_pairs={{0,24},{8,16},{16,8},{24,0},{1,25},{9,17},{17,9},{25,1},{2,26},{10... | collective-permute-start | bytes 12296 | tf_op jit(solution)/shard_map/ppermute | solution.py:352
  20.1 0.0 collective-permute-start.9
  20.1 0.0 collective-permute-done.6.refs_3_
  20.1 1.7 %collective-permute-start.10 = (f32[8,128]{1,0:T(8,128)S(1)}, f32[8,128]{1,0:T(8,128)S(1)}, u32[]{:S(2)}, u32[]{:S(2)}) collective-permute-start(f32[8,128]{1,0:T(8,128)S(1)} %get-tuple-element.18), channel_id=1, source_target_pairs={{0,8},{8,0},{16,24},{24,16},{1,9},{9,1},{17,25},{25,17},{2,10},{10... | collective-permute-start | bytes 12296 | tf_op jit(solution)/shard_map/ppermute | solution.py:352
  21.8 0.7 %collective-permute-done.5.refs_2_ = bf16[1,8,128,128]{3,2,1,0:T(8,128)(2,1)S(1)} collective-permute-done((bf16[1,8,128,128]{3,2,1,0:T(8,128)(2,1)S(1)}, bf16[1,8,128,128]{3,2,1,0:T(8,128)(2,1)S(1)}, u32[]{:S(2)}, u32[]{:S(2)}) %collective-permute-start.5) | collective-permute-done | bytes 262176 | tf_op jit(solution)/shard_map/ppermute | solution.py:355
  22.5 0.1 collective-permute-done.4.refs_1_
  22.6 0.8 %score_batch.2 = f32[8,128]{1,0:T(8,128)S(1)} custom-call(bf16[1,8,32,128]{3,2,1,0:T(8,128)(2,1)S(1)} %collective-permute-done.query_ref, bf16[1,8,128,128]{3,2,1,0:T(8,128)(2,1)S(1)} %copy-done, bf16[1,8,128,128]{3,2,1,0:T(8,128)(2,1)S(1)} %collective-permute-done.4.refs_1_, bf16[1,8,128,128]{3,2,1,0:T(8,128)(2,1)S(1)} %collective-permute-done.5.refs_2_, ...), custom_call_target="tpu_custom_call" | custom-call | flops 268435456 | bytes 1048576 | tf_op jit(solution)/shard_map/score_batch/pallas_call | solution.py:272
  23.4 0.0 collective-permute-start.7
  23.4 0.9 %score_batch.3.own_batch = f32[8,128]{1,0:T(8,128)S(1)} custom-call(bf16[1,8,32,128]{3,2,1,0:T(8,128)(2,1)S(1)} %copy-done.1, bf16[1,8,128,128]{3,2,1,0:T(8,128)(2,1)S(1)} %copy-done, bf16[1,8,128,128]{3,2,1,0:T(8,128)(2,1)S(1)} %collective-permute-done.4.refs_1_, bf16[1,8,128,128]{3,2,1,0:T(8,128)(2,1)S(1)} %collective-permute-done.5.refs_2_, ...), custom_call_target="tpu_custom_call" | custom-call | flops 268435456 | bytes 1048576 | tf_op jit(solution)/shard_map/score_batch/pallas_call | solution.py:272
  24.2 0.0 collective-permute-done.8.refs_1_
  24.2 0.4 %collective-permute-done.9.refs_2_ = f32[8,128]{1,0:T(8,128)S(1)} collective-permute-done((f32[8,128]{1,0:T(8,128)S(1)}, f32[8,128]{1,0:T(8,128)S(1)}, u32[]{:S(2)}, u32[]{:S(2)}) %collective-permute-start.9) | collective-permute-done | bytes 4128 | tf_op jit(solution)/shard_map/ppermute | solution.py:352
  24.6 0.0 collective-permute-done.10.refs_3_
  24.6 0.0 collective-permute-done.7.mate_batch
  24.7 0.0 copy-done.3
  24.7 0.8 %finish.1 = (f32[1,8,64]{2,1,0:T(8,128)}, f32[1,8,64]{2,1,0:T(8,128)}, f32[1,8]{1,0:T(1,128)}) custom-call(f32[8,128]{1,0:T(8,128)S(1)} %score_batch.3.own_batch, f32[8,128]{1,0:T(8,128)S(1)} %collective-permute-done.7.mate_batch, f32[8,128]{1,0:T(8,128)S(1)} %get-tuple-element.12.refs_0_, f32[8,128]{1,0:T(8,128)S(1)} %collective-permute-done.8.refs_1_, ...), custom_call_target="tpu_custom_call" | custom-call | tf_op jit(solution)/shard_map/finish/pallas_call | solution.py:332
  (5 shorter events, 0.0 us)
Async XLA Ops:
  0.6 13.1 %copy-start.1 = (bf16[1,8,32,128]{3,2,1,0:T(8,128)(2,1)S(1)}, bf16[1,8,32,128]{3,2,1,0:T(8,128)(2,1)}, u32[]{:S(2)}) copy-start(bf16[1,8,32,128]{3,2,1,0:T(8,128)(2,1)} %query_ref.2) | copy-start | bytes 196612
  0.6 7.8 %copy-start = (bf16[1,8,128,128]{3,2,1,0:T(8,128)(2,1)S(1)}, bf16[1,8,128,128]{3,2,1,0:T(8,128)(2,1)}, u32[]{:S(2)}) copy-start(bf16[1,8,128,128]{3,2,1,0:T(8,128)(2,1)} %refs_0_.3) | copy-start | bytes 786436
  0.7 13.1 %copy-start.4 = (bf16[1,128,128,128]{3,2,1,0:T(8,128)(2,1)S(1)}, bf16[1,128,128,128]{3,2,1,0:T(8,128)(2,1)}, u32[]{:S(2)}) copy-start(bf16[1,128,128,128]{3,2,1,0:T(8,128)(2,1)} %refs_4_.2) | copy-start | bytes 12582916
  2.7 22.0 %copy-start.2 = (s32[1,8,64]{2,1,0:T(8,128)S(1)}, s32[1,8,64]{2,1,0:T(8,128)}, u32[]{:S(2)}) copy-start(s32[1,8,64]{2,1,0:T(8,128)} %refs_4_.3) | copy-start | bytes 6148
  2.7 22.0 %copy-start.3 = (s32[1,8]{1,0:T(1,128)S(1)}, s32[1,8]{1,0:T(1,128)}, u32[]{:S(2)}) copy-start(s32[1,8]{1,0:T(1,128)} %refs_5_.1) | copy-start | bytes 100
  2.7 8.9 %collective-permute-start.3 = (bf16[272,128]{1,0:T(8,128)(2,1)S(1)}, bf16[272,128]{1,0:T(8,128)(2,1)S(1)}, u32[]{:S(2)}, u32[]{:S(2)}) collective-permute-start(bf16[272,128]{1,0:T(8,128)(2,1)S(1)} %pack.1.refs_0_), channel_id=1, source_target_pairs={{0,24},{8,16},{16,8},{24,0},{1,25},{9,17},{17,9},{25,1},{2,26},{10... | collective-permute-start | bytes 208904 | tf_op jit(solution)/shard_map/ppermute | solution.py:352
  7.8 5.9 %collective-permute-start.2 = (bf16[272,128]{1,0:T(8,128)(2,1)S(1)}, bf16[272,128]{1,0:T(8,128)(2,1)S(1)}, u32[]{:S(2)}, u32[]{:S(2)}) collective-permute-start(bf16[272,128]{1,0:T(8,128)(2,1)S(1)} %pack.1.refs_0_), channel_id=1, source_target_pairs={{0,16},{8,24},{16,0},{24,8},{1,17},{9,25},{17,1},{25,9},{2,18},{10... | collective-permute-start | bytes 208904 | tf_op jit(solution)/shard_map/ppermute | solution.py:352
  7.8 5.9 %collective-permute-start.1 = (bf16[272,128]{1,0:T(8,128)(2,1)S(1)}, bf16[272,128]{1,0:T(8,128)(2,1)S(1)}, u32[]{:S(2)}, u32[]{:S(2)}) collective-permute-start(bf16[272,128]{1,0:T(8,128)(2,1)S(1)} %pack.1.refs_0_), channel_id=1, source_target_pairs={{0,8},{8,0},{16,24},{24,16},{1,9},{9,1},{17,25},{25,17},{2,10},{10... | collective-permute-start | bytes 208904 | tf_op jit(solution)/shard_map/ppermute | solution.py:352
  8.5 11.7 %collective-permute-start.6 = (bf16[1,8,128,128]{3,2,1,0:T(8,128)(2,1)S(1)}, bf16[1,8,128,128]{3,2,1,0:T(8,128)(2,1)S(1)}, u32[]{:S(2)}, u32[]{:S(2)}) collective-permute-start(bf16[1,8,128,128]{3,2,1,0:T(8,128)(2,1)S(1)} %copy-done), channel_id=1, source_target_pairs={{0,6},{1,7},{2,4},{3,5},{4,2},{5,3},{6,0},{7,1},{8,14},{9,15},{10,... | collective-permute-start | bytes 786440 | tf_op jit(solution)/shard_map/ppermute | solution.py:355
  11.0 11.4 %collective-permute-start.5 = (bf16[1,8,128,128]{3,2,1,0:T(8,128)(2,1)S(1)}, bf16[1,8,128,128]{3,2,1,0:T(8,128)(2,1)S(1)}, u32[]{:S(2)}, u32[]{:S(2)}) collective-permute-start(bf16[1,8,128,128]{3,2,1,0:T(8,128)(2,1)S(1)} %copy-done), channel_id=1, source_target_pairs={{0,4},{1,5},{2,6},{3,7},{4,0},{5,1},{6,2},{7,3},{8,12},{9,13},{10,... | collective-permute-start | bytes 786440 | tf_op jit(solution)/shard_map/ppermute | solution.py:355
  11.6 11.0 %collective-permute-start.4 = (bf16[1,8,128,128]{3,2,1,0:T(8,128)(2,1)S(1)}, bf16[1,8,128,128]{3,2,1,0:T(8,128)(2,1)S(1)}, u32[]{:S(2)}, u32[]{:S(2)}) collective-permute-start(bf16[1,8,128,128]{3,2,1,0:T(8,128)(2,1)S(1)} %copy-done), channel_id=1, source_target_pairs={{0,2},{1,3},{2,0},{3,1},{4,6},{5,7},{6,4},{7,5},{8,10},{9,11},{10,... | collective-permute-start | bytes 786440 | tf_op jit(solution)/shard_map/ppermute | solution.py:355
  13.7 3.6 %collective-permute-start = (bf16[1,8,32,128]{3,2,1,0:T(8,128)(2,1)S(1)}, bf16[1,8,32,128]{3,2,1,0:T(8,128)(2,1)S(1)}, u32[]{:S(2)}, u32[]{:S(2)}) collective-permute-start(bf16[1,8,32,128]{3,2,1,0:T(8,128)(2,1)S(1)} %copy-done.1), channel_id=1, source_target_pairs={{0,1},{1,0},{2,3},{3,2},{4,5},{5,4},{6,7},{7,6},{8,9},{9,8},{10,11... | collective-permute-start | bytes 196616 | tf_op jit(solution)/shard_map/ppermute | solution.py:355
  17.3 6.9 %collective-permute-start.8 = (f32[8,128]{1,0:T(8,128)S(1)}, f32[8,128]{1,0:T(8,128)S(1)}, u32[]{:S(2)}, u32[]{:S(2)}) collective-permute-start(f32[8,128]{1,0:T(8,128)S(1)} %get-tuple-element.16), channel_id=1, source_target_pairs={{0,24},{8,16},{16,8},{24,0},{1,25},{9,17},{17,9},{25,1},{2,26},{10... | collective-permute-start | bytes 12296 | tf_op jit(solution)/shard_map/ppermute | solution.py:352
  20.1 4.5 %collective-permute-start.9 = (f32[8,128]{1,0:T(8,128)S(1)}, f32[8,128]{1,0:T(8,128)S(1)}, u32[]{:S(2)}, u32[]{:S(2)}) collective-permute-start(f32[8,128]{1,0:T(8,128)S(1)} %get-tuple-element.17), channel_id=1, source_target_pairs={{0,16},{8,24},{16,0},{24,8},{1,17},{9,25},{17,1},{25,9},{2,18},{10... | collective-permute-start | bytes 12296 | tf_op jit(solution)/shard_map/ppermute | solution.py:352
  20.1 4.5 %collective-permute-start.10 = (f32[8,128]{1,0:T(8,128)S(1)}, f32[8,128]{1,0:T(8,128)S(1)}, u32[]{:S(2)}, u32[]{:S(2)}) collective-permute-start(f32[8,128]{1,0:T(8,128)S(1)} %get-tuple-element.18), channel_id=1, source_target_pairs={{0,8},{8,0},{16,24},{24,16},{1,9},{9,1},{17,25},{25,17},{2,10},{10... | collective-permute-start | bytes 12296 | tf_op jit(solution)/shard_map/ppermute | solution.py:352
  23.4 1.3 %collective-permute-start.7 = (f32[8,128]{1,0:T(8,128)S(1)}, f32[8,128]{1,0:T(8,128)S(1)}, u32[]{:S(2)}, u32[]{:S(2)}) collective-permute-start(f32[8,128]{1,0:T(8,128)S(1)} %score_batch.2), channel_id=1, source_target_pairs={{0,1},{1,0},{2,3},{3,2},{4,5},{5,4},{6,7},{7,6},{8,9},{9,8},{10,11... | collective-permute-start | bytes 12296 | tf_op jit(solution)/shard_map/ppermute | solution.py:355
